TPU v7x, 512 devices: a whole 4x8x8 slice. The times are simulated.
512 devices in a mesh: leaf: 128 (over y, z, core), cols: 4 (over x).
Axes of the slice: x: 4, y: 8, z: 8, core: 2. Of those that a mesh axis runs over, the one named last changes fastest.
Arguments:
- samples: bfloat16 [262144, 256], P(('leaf', 'cols')), may hold values from -6 to 6
- near_tiles: bfloat16 [2048, 16, 128, 128], P('leaf', 'cols'), may hold values from -0.1875 to 0.1875
- columns: int32 [2048, 16], P('leaf', 'cols'), may hold values from 0 to 2047, as said below
- tile_count: int32 [2048], P('leaf'), may hold values from 4 to 16, as said below
- skeleton_one: int32 [16, 64, 128], P('cols'), may hold values from 0 to 255, as said below
- skeleton_two: int32 [16, 32, 128], P('cols'), may hold values from 0 to 255, as said below
- skeleton_three: int32 [16, 16, 128], P('cols'), may hold values from 0 to 255, as said below
Outputs:
- transfer_one: float32 [128, 8, 256, 128], P('leaf', 'cols')
- transfer_two: float32 [128, 4, 256, 128], P('leaf', 'cols')
- transfer_three: float32 [128, 4, 256, 128], P('leaf', 'cols')
- top_samples: float32 [128, 4, 128, 256], P('leaf', 'cols')
Inputs may be any that keep to these rules, and one draw needn't show every extreme that they name: `columns`: the column cluster of a slot of row cluster r, of any layer, lies in region r // 16 or a region beside it. `tile_count`: slots at or past a cluster's count are unused; some cluster uses all 16. `skeleton_one`: each row holds 128 distinct indices. `skeleton_two`: each row holds 128 distinct indices. `skeleton_three`: each row holds 128 distinct indices.
All inputs are finite; a program needn't handle non-finite values.
Results may differ from a plain program's by a relative error of at most 0.0003.
Values may be sent and summed in bfloat16 or wider, within the bound.
No kernel may reach another device: no remote copies, remote signals or barrier semaphores. Data moves between devices by JAX's collectives and lax.ppermute only.
A program may use at most 64 MiB of HBM per device.

v0:
```python
import jax
import jax.numpy as jnp
from jax import lax
from jax.sharding import PartitionSpec as P

HIGHEST = lax.Precision.HIGHEST
RIDGE = 0.25


def padded(value, sides, width):
    for axis, dim in sides:
        count, length = (lax.axis_size(axis), value.shape[dim])
        up = [(i, (i + 1) % count) for i in range(count - 1)]
        down = [(j, i) for i, j in up]
        last = lax.slice_in_dim(value, length - width, length, axis=dim)
        initial = lax.slice_in_dim(value, 0, width, axis=dim)
        before = lax.ppermute(last, axis, up)
        after = lax.ppermute(initial, axis, down)
        value = jnp.concatenate([before, value, after], axis=dim)
    return value


def swapped(block, axis, apart):
    count = lax.axis_size(axis)
    route = []
    for low in range(count):
        high = low | 1 << apart
        if high != low and high < count:
            route += [(low, high), (high, low)]
    return lax.ppermute(block, axis, route)


def merge_pair(first, second, chosen):
    stacked = jnp.concatenate([first, second], axis=1)
    picked = jax.vmap(lambda block, index: block[index])(stacked, chosen)
    count = stacked.shape[2]
    rank = picked.shape[1]
    gram = jnp.einsum("mis,mjs->mij", picked, picked, precision=HIGHEST) / count
    gram = gram + RIDGE * jnp.eye(rank, dtype=jnp.float32)
    lower = jnp.linalg.cholesky(gram)
    basis = jax.vmap(
        lambda factor, rhs: jax.scipy.linalg.solve_triangular(factor, rhs, lower=True)
    )(lower, picked)
    transfer = jnp.einsum("mis,mjs->mij", stacked, basis, precision=HIGHEST) / count
    return (basis, transfer)


def local(samples, near_tiles, columns, tile_count, skeleton_one, skeleton_two, skeleton_three):
    leaf_index = lax.axis_index("leaf")
    cols_index = lax.axis_index("cols")
    clusters, slots, panels, _ = near_tiles.shape
    width = samples.shape[1]
    own_rows = lax.all_gather(samples, "cols", axis=0, tiled=True)
    near_rows = padded(own_rows, (("leaf", 0),), own_rows.shape[0])
    window = near_rows.reshape(3 * clusters, panels, width)
    local_cols = columns - (leaf_index - 1) * clusters
    picked = jnp.take(window, local_cols, axis=0)
    slot_ids = cols_index * slots + lax.iota(jnp.int32, slots)
    active = (slot_ids[None, :] < tile_count[:, None]).astype(picked.dtype)
    picked = picked * active[:, :, None, None]
    partial_value = jnp.einsum(
        "ksij,ksjn->kin", near_tiles, picked, preferred_element_type=jnp.float32
    )
    nodes = lax.psum_scatter(partial_value, "cols", scatter_dimension=0, tiled=True)
    subtrees = nodes.shape[0]
    outputs = []
    level = 0
    spread = 1
    for skeleton in (skeleton_one, skeleton_two, skeleton_three):
        level = level + 1
        side = leaf_index >> level - 1 & 1
        group = leaf_index >> level
        spread = min(2**level, subtrees)
        offset = leaf_index % spread
        chosen_all = lax.dynamic_index_in_dim(skeleton, group, axis=1, keepdims=False)
        other = swapped(nodes, "leaf", level - 1)
        first = jnp.where(side == 0, nodes, other)
        second = jnp.where(side == 0, other, nodes)
        basis, transfer = merge_pair(first, second, chosen_all)
        kept = lax.dynamic_index_in_dim(
            transfer.reshape(subtrees // spread, spread, 2 * panels, panels),
            offset,
            axis=1,
            keepdims=False,
        )
        outputs.append(kept[None])
        nodes = basis
    offset = leaf_index % spread
    top = lax.dynamic_index_in_dim(
        nodes.reshape(subtrees // spread, spread, panels, width), offset, axis=1, keepdims=False
    )
    return (outputs[0], outputs[1], outputs[2], top[None])


def solution(mesh):
    placed = (
        P(("leaf", "cols"), None),
        P("leaf", "cols", None, None),
        P("leaf", "cols"),
        P("leaf"),
        P("cols", None, None),
        P("cols", None, None),
        P("cols", None, None),
    )
    return jax.shard_map(
        local,
        mesh=mesh,
        in_specs=placed,
        out_specs=(
            P("leaf", "cols", None, None),
            P("leaf", "cols", None, None),
            P("leaf", "cols", None, None),
            P("leaf", "cols", None, None),
        ),
        check_vma=False,
    )
```

profile of v0, /device:TPU:1, one launch (start us, length us, event | category | flops | bytes accessed | tf_op | source)
XLA Modules:
  0.0 481.0 jit_solution(7024307054163040325)
XLA Ops:
  8.0 36.1 %all-gather.2.cloned.1.call-done = bf16[2048,256]{1,0:T(8,128)(2,1)} async-done(((bf16[512,256]{1,0:T(8,128)(2,1)}), bf16[2048,256]{1,0:T(8,128)(2,1)}) %all-gather.2.cloned.1.call-update) | async-done | bytes 1048592 | tf_op jit(solution)/shard_map/all_gather | solution.py:53
  44.0 4.7 collective-permute-start
  52.4 8.4 %collective-permute-done = bf16[2048,256]{1,0:T(8,128)(2,1)S(1)} collective-permute-done((bf16[2048,256]{1,0:T(8,128)(2,1)}, bf16[2048,256]{1,0:T(8,128)(2,1)S(1)}, u32[]{:S(2)}, u32[]{:S(2)}) %collective-permute-start) | collective-permute-done | bytes 1048608 | tf_op jit(solution)/shard_map/ppermute | solution.py:17
  60.8 4.4 collective-permute-done.1
  65.2 3.0 pad_maximum_fusion
  68.2 4.6 gather_fusion
  72.8 6.4 %copy.41 = bf16[64,128,256]{1,2,0:T(8,128)(2,1)} copy(bf16[64,128,256]{2,1,0:T(8,128)(2,1)} %gather_fusion) | data formatting | bytes 8388608 | tf_op jit(solution)/shard_map/jit(_take)/gather | solution.py:57
  79.2 4.8 %fusion.6 = f32[16,128,256]{1,2,0:T(8,128)} fusion(bf16[16,4,128,128]{3,2,1,0:T(8,128)(2,1)S(1)} %copy-done, bf16[16,4,128,256]{2,3,1,0:T(8,128)(2,1)} %bitcast.75, pred[16,4]{1,0:T(8,128)(4,1)S(1)} %copy.39, bf16[16,4]{1,0:T(8,128)(2,1)S(1)} %compare_convert_fusion), kind=kOutput, calls=%fused_computation.11 | convolution fusion | flops 541065216 | bytes 8388800 | tf_op jit(solution)/shard_map/ksij,ksjn->kin/dot_general | solution.py:61
  84.8 34.4 %reduce-scatter.2.cloned.1.call-done = f32[4,128,256]{1,2,0:T(8,128)} async-done(((f32[16,128,256]{1,2,0:T(8,128)}), f32[4,128,256]{1,2,0:T(8,128)}) %reduce-scatter.2.cloned.1.call-update) | async-done | bytes 524304 | tf_op jit(solution)/shard_map/reduce_scatter | solution.py:64
  119.3 2.5 collective-permute-start.2
  128.3 6.3 %gather_fusion.1 = f32[512,256]{1,0:T(8,128)} fusion(f32[4,256,256]{2,1,0:T(8,128)S(1)} %copy.42, s32[512]{0:T(512)S(1)} %get-tuple-element.14), kind=kCustom, calls=%fused_computation.1 | custom fusion | bytes 1052672 | tf_op jit(solution)/shard_map/vmap()/gather | solution.py:35
  136.6 46.9 %custom-call.16 = f32[4,128,128]{2,1,0:T(8,128)S(1)} custom-call(f32[4,128,128]{2,1,0:T(8,128)S(1)} %fusion.20), custom_call_target="Cholesky" | custom-call | tf_op jit(solution)/shard_map/jit(cholesky)/cholesky | solution.py:40
  183.8 39.3 %custom-call.17 = f32[4,1,128,128]{2,3,1,0:T(8,128)S(1)} custom-call(f32[4,1,128,128]{3,2,1,0:T(8,128)S(1)} %select_bitcast_fusion.2), custom_call_target="InvertDiagBlocksLowerTriangular" | custom-call | tf_op jit(solution)/shard_map/vmap(jit(_solve_triangular))/triangular_solve | solution.py:42
  224.8 3.5 collective-permute-start.3
  229.1 10.8 %collective-permute-done.3 = f32[4,128,256]{2,1,0:T(8,128)S(1)} collective-permute-done((f32[4,128,256]{2,1,0:T(8,128)S(1)}, f32[4,128,256]{2,1,0:T(8,128)S(1)}, u32[]{:S(2)}, u32[]{:S(2)}) %collective-permute-start.3) | collective-permute-done | bytes 524320 | tf_op jit(solution)/shard_map/ppermute | solution.py:30
  240.9 6.4 %gather_fusion.2 = f32[512,256]{1,0:T(8,128)} fusion(f32[4,256,256]{2,1,0:T(8,128)S(1)} %pad_maximum_fusion.2, s32[512]{0:T(512)S(1)} %get-tuple-element.15), kind=kCustom, calls=%fused_computation.2 | custom fusion | bytes 1052672 | tf_op jit(solution)/shard_map/vmap()/gather | solution.py:35
  251.7 47.7 %custom-call.18 = f32[4,128,128]{2,1,0:T(8,128)S(1)} custom-call(f32[4,128,128]{2,1,0:T(8,128)} %fusion.17), custom_call_target="Cholesky" | custom-call | tf_op jit(solution)/shard_map/jit(cholesky)/cholesky | solution.py:40
  300.4 40.1 %custom-call.19 = f32[4,1,128,128]{2,3,1,0:T(8,128)S(1)} custom-call(f32[4,1,128,128]{3,2,1,0:T(8,128)} %select_bitcast_fusion.1), custom_call_target="InvertDiagBlocksLowerTriangular" | custom-call | tf_op jit(solution)/shard_map/vmap(jit(_solve_triangular))/triangular_solve | solution.py:42
  342.3 4.4 collective-permute-start.4
  346.7 2.9 convolution_multiply_fusion
  352.1 17.0 %collective-permute-done.4 = f32[4,128,256]{2,1,0:T(8,128)S(1)} collective-permute-done((f32[4,128,256]{2,1,0:T(8,128)S(1)}, f32[4,128,256]{2,1,0:T(8,128)S(1)}, u32[]{:S(2)}, u32[]{:S(2)}) %collective-permute-start.4) | collective-permute-done | bytes 524320 | tf_op jit(solution)/shard_map/ppermute | solution.py:30
  370.3 6.6 %gather_fusion.3 = f32[512,256]{1,0:T(8,128)} fusion(f32[4,256,256]{2,1,0:T(8,128)S(1)} %pad_maximum_fusion.3, s32[512]{0:T(512)S(1)} %fusion.35), kind=kCustom, calls=%fused_computation.3 | custom fusion | bytes 1052672 | tf_op jit(solution)/shard_map/vmap()/gather | solution.py:35
  381.3 47.7 %custom-call.20 = f32[4,128,128]{2,1,0:T(8,128)S(1)} custom-call(f32[4,128,128]{2,1,0:T(8,128)} %fusion.14), custom_call_target="Cholesky" | custom-call | tf_op jit(solution)/shard_map/jit(cholesky)/cholesky | solution.py:40
  430.0 40.1 %custom-call.21 = f32[4,1,128,128]{2,3,1,0:T(8,128)S(1)} custom-call(f32[4,1,128,128]{3,2,1,0:T(8,128)} %select_bitcast_fusion), custom_call_target="InvertDiagBlocksLowerTriangular" | custom-call | tf_op jit(solution)/shard_map/vmap(jit(_solve_triangular))/triangular_solve | solution.py:42
  (83 shorter events, 37.5 us)
Async XLA Ops:
  7.2 72.1 %copy-start = (bf16[16,4,128,128]{3,2,1,0:T(8,128)(2,1)S(1)}, bf16[16,4,128,128]{3,2,1,0:T(8,128)(2,1)}, u32[]{:S(2)}) copy-start(bf16[16,4,128,128]{3,2,1,0:T(8,128)(2,1)} %param.11) | copy-start | bytes 6291460
  7.2 36.8 %all-gather.2.cloned.1.call-start = ((), (), s32[]{:S(2)}) async-start(), calls=%async_computation.1 | async-start | bytes 1310720 | tf_op jit(solution)/shard_map/all_gather | solution.py:53
  7.9 111.4 %reduce-scatter.2.cloned.1.call-start = ((), (), s32[]{:S(2)}) async-start(), calls=%async_computation.2 | async-start | bytes 2621440 | tf_op jit(solution)/shard_map/reduce_scatter | solution.py:64
  44.0 16.8 %collective-permute-start = (bf16[2048,256]{1,0:T(8,128)(2,1)}, bf16[2048,256]{1,0:T(8,128)(2,1)S(1)}, u32[]{:S(2)}, u32[]{:S(2)}) collective-permute-start(bf16[2048,256]{1,0:T(8,128)(2,1)} %all-gather.2.cloned.1.call-done), channel_id=1, source_target_pairs={{0,4},{4,8},{8,12},{12,16},{16,20},{20,24},{24,28},{28,32},{32,36}... | collective-permute-start | bytes 3145736 | tf_op jit(solution)/shard_map/ppermute | solution.py:17
  48.8 16.4 %collective-permute-start.1 = (bf16[2048,256]{1,0:T(8,128)(2,1)}, bf16[2048,256]{1,0:T(8,128)(2,1)}, u32[]{:S(2)}, u32[]{:S(2)}) collective-permute-start(bf16[2048,256]{1,0:T(8,128)(2,1)} %all-gather.2.cloned.1.call-done), channel_id=1, source_target_pairs={{4,0},{8,4},{12,8},{16,12},{20,16},{24,20},{28,24},{32,28},{36,32}... | collective-permute-start | bytes 3145736 | tf_op jit(solution)/shard_map/ppermute | solution.py:18
  119.3 4.3 collective-permute-start.2
  124.7 0.8 copy-start.3
  124.7 1.0 copy-start.5
  224.8 15.2 %copy-start.1 = (f32[4,128,256]{2,1,0:T(8,128)}, f32[4,128,256]{2,1,0:T(8,128)S(1)}, u32[]{:S(2)}) copy-start(f32[4,128,256]{2,1,0:T(8,128)S(1)} %fusion.18) | copy-start | bytes 1572868
  224.8 15.0 %collective-permute-start.3 = (f32[4,128,256]{2,1,0:T(8,128)S(1)}, f32[4,128,256]{2,1,0:T(8,128)S(1)}, u32[]{:S(2)}, u32[]{:S(2)}) collective-permute-start(f32[4,128,256]{2,1,0:T(8,128)S(1)} %fusion.18), channel_id=1, source_target_pairs={{0,8},{8,0},{4,12},{12,4},{16,24},{24,16},{20,28},{28,20},{32,40},... | collective-permute-start | bytes 1572872 | tf_op jit(solution)/shard_map/ppermute | solution.py:30
  240.0 0.8 copy-start.6
  240.0 1.0 copy-start.8
  247.3 99.4 %copy-start.2 = (f32[4,128,256]{2,1,0:T(8,128)S(1)}, f32[4,128,256]{2,1,0:T(8,128)}, u32[]{:S(2)}) copy-start(f32[4,128,256]{2,1,0:T(8,128)} %copy-done.1) | copy-start | bytes 1572868
  247.3 99.4 %copy-start.4 = (f32[4,128,256]{1,2,0:T(8,128)S(1)}, f32[4,128,256]{1,2,0:T(8,128)}, u32[]{:S(2)}) copy-start(f32[4,128,256]{1,2,0:T(8,128)} %copy-done.3) | copy-start | bytes 1572868
  340.5 9.8 %copy-start.7 = (f32[4,128,256]{2,1,0:T(8,128)S(1)}, f32[4,128,256]{2,1,0:T(8,128)}, u32[]{:S(2)}) copy-start(f32[4,128,256]{2,1,0:T(8,128)} %copy-done.6) | copy-start | bytes 1572868
  340.6 9.8 %copy-start.9 = (f32[4,128,256]{2,1,0:T(8,128)S(1)}, f32[4,128,256]{2,1,0:T(8,128)}, u32[]{:S(2)}) copy-start(f32[4,128,256]{2,1,0:T(8,128)} %copy-done.8) | copy-start | bytes 1572868
  342.3 26.8 %collective-permute-start.4 = (f32[4,128,256]{2,1,0:T(8,128)S(1)}, f32[4,128,256]{2,1,0:T(8,128)S(1)}, u32[]{:S(2)}, u32[]{:S(2)}) collective-permute-start(f32[4,128,256]{2,1,0:T(8,128)S(1)} %fusion.15), channel_id=1, source_target_pairs={{0,16},{16,0},{4,20},{20,4},{8,24},{24,8},{12,28},{28,12},{32,48},... | collective-permute-start | bytes 1572872 | tf_op jit(solution)/shard_map/ppermute | solution.py:30
  369.3 0.8 copy-start.10
  369.3 1.0 copy-start.12
  376.9 94.9 %copy-start.11 = (f32[4,128,256]{2,1,0:T(8,128)S(1)}, f32[4,128,256]{2,1,0:T(8,128)}, u32[]{:S(2)}) copy-start(f32[4,128,256]{2,1,0:T(8,128)} %copy-done.10) | copy-start | bytes 1572868
  376.9 94.9 %copy-start.13 = (f32[4,128,256]{2,1,0:T(8,128)S(1)}, f32[4,128,256]{2,1,0:T(8,128)}, u32[]{:S(2)}) copy-start(f32[4,128,256]{2,1,0:T(8,128)} %copy-done.12) | copy-start | bytes 1572868
Sparse Core Ops, SparseCore 0:
  10.1 33.8 all-gather.1
  84.2 35.0 reduce-scatter.1
where the time goes:
time: 482 us; the launch traced here: 481 us
  other arithmetic  276 us (57%)
  waiting for transfers between devices  113 us (23%)
  local copies, waits for them, and re-layouts  40.4 us (8%)
  matrix products  20.6 us (4%)
  starting transfers between devices  17.1 us (4%)
  between operations  14.5 us (3%)
    another operation x10, other arithmetic, merge_pair(): lower = jnp.linalg.cholesky(gram)  143 us
    another operation x7, other arithmetic, merge_pair(): jax.scipy.linalg.solve_triangular(factor, rhs, lower=True)  121 us
    all_gather x1, waiting for transfers between devices, local(): own_rows = lax.all_gather(samples, 'cols', axis=0, tiled=True)  36.1 us
    reduce_scatter x1, waiting for transfers between devices, local(): lax.psum_scatter(partial_value, 'cols', scatter_dimension=0, tiled=True)  34.4 us
    ppermute x3, waiting for transfers between devices, swapped(): return lax.ppermute(block, axis, route)  28.8 us
    gather x3, local copies, waits for them, and re-layouts, merge_pair(): picked = jax.vmap(lambda block, index: block[index])(stacked, chosen)  19.3 us
    gather x2, local copies, waits for them, and re-layouts, local(): picked = jnp.take(window, local_cols, axis=0)  11.1 us
    ppermute x3, starting transfers between devices, swapped(): return lax.ppermute(block, axis, route)  10.3 us
  transfers between devices with their start and end apart: 7, of which 7 were waited for; matrix products, arithmetic and copies ran while one was open for 2% of the time, Pallas kernels for 0%

commit v1 on v0

v1 whole, which is shorter than its diff:
```python
import functools

import jax
import jax.numpy as jnp
from jax import lax
from jax.experimental import pallas as pl
from jax.experimental.pallas import tpu as pltpu
from jax.sharding import PartitionSpec as P

RIDGE = 0.25
BF = jnp.bfloat16
F32 = jnp.float32
PANEL = 16


def dot(a, b, ca, cb):
    return lax.dot_general(a, b, (((ca,), (cb,)), ((), ())), preferred_element_type=F32)


def split2(x):
    hi = x.astype(BF)
    lo = (x - hi.astype(F32)).astype(BF)
    return hi, lo


def split3(x):
    hi = x.astype(BF)
    rest = x - hi.astype(F32)
    mid = rest.astype(BF)
    lo = (rest - mid.astype(F32)).astype(BF)
    return hi, mid, lo


def near_kernel(
    info, cols, counts, own_tiles, tiles_a, tiles_b, tiles_c, before, own, after,
    send_ref, keep_ref, win, tiles, sem,
):
    x = info[0]
    even = info[1]
    late = info[2]
    copies = [
        pltpu.make_async_copy(own, win.at[pl.ds(2048, 2048)], sem.at[0]),
        pltpu.make_async_copy(before, win.at[pl.ds(0, 2048)], sem.at[1]),
        pltpu.make_async_copy(after, win.at[pl.ds(4096, 2048)], sem.at[2]),
        pltpu.make_async_copy(own_tiles.at[pl.ds(x * 4, 4)], tiles.at[0], sem.at[3]),
        pltpu.make_async_copy(tiles_a, tiles.at[1], sem.at[4]),
        pltpu.make_async_copy(tiles_b, tiles.at[2], sem.at[5]),
        pltpu.make_async_copy(tiles_c, tiles.at[3], sem.at[6]),
    ]
    for copy in copies:
        copy.start()
    for copy in copies:
        copy.wait()
    for q in range(4):
        keep, slot = divmod(q, 2)
        parity = even if keep == 1 else 1 - even
        member = late if slot == 1 else 1 - late
        k = parity + 2 * member
        count = counts[k]
        total = jnp.zeros((128, 256), F32)
        for delta in range(4):
            source = (x + 4 - delta) % 4
            for s in range(0, 4, 2):
                pieces = []
                rows = []
                for t in (s, s + 1):
                    place = source * 4 + t
                    live = jnp.where(place < count, 1.0, 0.0).astype(F32)
                    piece = tiles[delta, k, t]
                    pieces.append(piece * jnp.full((128, 128), live, F32).astype(BF))
                    col = jnp.clip(cols[k, place], 0, 47)
                    rows.append(win[pl.ds(pl.multiple_of(col * 128, 128), 128), :])
                total = total + dot(
                    jnp.concatenate(pieces, axis=1), jnp.concatenate(rows, axis=0), 1, 0
                )
        if keep == 1:
            keep_ref[slot] = total
        else:
            send_ref[slot] = total


def near(info, cols, counts, own_tiles, received, before, own, after):
    smem = pl.BlockSpec(memory_space=pltpu.SMEM)
    hbm = pl.BlockSpec(memory_space=pl.ANY)
    vmem = pl.BlockSpec(memory_space=pltpu.VMEM)
    block = jax.ShapeDtypeStruct((2, 128, 256), F32)
    return pl.pallas_call(
        near_kernel,
        out_shape=(block, block),
        in_specs=[smem] * 3 + [hbm] * 7,
        out_specs=(vmem, vmem),
        scratch_shapes=[
            pltpu.VMEM((6144, 256), BF),
            pltpu.VMEM((4, 4, 4, 128, 128), BF),
            pltpu.SemaphoreType.DMA((7,)),
        ],
        compiler_params=pltpu.CompilerParams(vmem_limit_bytes=24 << 20),
        cost_estimate=pl.CostEstimate(
            flops=540_000_000, bytes_accessed=6_000_000, transcendentals=0
        ),
    )(info, cols, counts, own_tiles, *received, before, own, after)


def eliminate(j, gram, rhs):
    base = j * PANEL
    half = PANEL // 2
    rows = lax.broadcasted_iota(jnp.int32, (half, 128), 0)
    a = [gram[base + half * h : base + half * (h + 1), :] for h in range(2)]
    body = [
        [a[h]] + [rhs[base + half * h : base + half * (h + 1), 128 * c : 128 * (c + 1)] for c in range(2)]
        for h in range(2)
    ]
    column = [
        [jnp.broadcast_to(a[h][:, base + k : base + k + 1], (half, 128)) for k in range(PANEL)]
        for h in range(2)
    ]
    scale = [jnp.zeros((half, 128), F32) for _ in range(2)]
    for i in range(PANEL):
        h0, r = divmod(i, half)
        pivot = column[h0][i][r : r + 1, :]
        inverse = lax.rsqrt(pivot)
        reciprocal = inverse * inverse
        scale[h0] = jnp.where(rows == r, jnp.broadcast_to(inverse, (half, 128)), scale[h0])
        factor = {}
        for h in range(h0, 2):
            value = column[h][i] * reciprocal
            factor[h] = jnp.where(rows > r, value, 0.0) if h == h0 else value
        for k in range(i + 1, PANEL):
            row = column[h0][k][r : r + 1, :]
            for h in range(h0, 2):
                column[h][k] = column[h][k] - factor[h] * row
        for c in range(3):
            row = body[h0][c][r : r + 1, :]
            for h in range(h0, 2):
                body[h][c] = body[h][c] - factor[h] * row
    return jnp.concatenate(
        [jnp.concatenate([body[h][c] * scale[h] for c in range(3)], axis=1) for h in range(2)],
        axis=0,
    )


def merge_kernel(nodes, own, other, choice, *refs):
    outs, gram = refs[:nodes], refs[nodes]
    for m in range(nodes):
        wide = [jnp.concatenate(pair, axis=0) for pair in zip(split3(own[m]), split3(other[m]))]
        hi, mid, lo = (dot(choice[m], part, 1, 0) for part in wide)
        outs[m][0] = hi + (mid + lo)
        hi = hi.astype(BF)
        mid = mid.astype(BF)
        product = dot(
            jnp.concatenate([hi, hi, mid], axis=1), jnp.concatenate([hi, mid, hi], axis=1), 1, 1
        )
        on = lax.broadcasted_iota(jnp.int32, (128, 128), 0) == lax.broadcasted_iota(
            jnp.int32, (128, 128), 1
        )
        gram[m] = product * (1.0 / 256) + jnp.where(on, RIDGE, 0.0)
    for j in range(128 // PANEL):
        done = (j + 1) * PANEL
        for m in range(nodes):
            rows = eliminate(j, gram.at[m], outs[m].at[0])
            outs[m][0, j * PANEL : done, :] = rows[:, 128:]
            if done < 128:
                hi, mid, lo = split3(rows)
                left = jnp.concatenate([hi, hi, mid, mid, hi, lo], axis=0)[:, :128]
                right = jnp.concatenate([hi, mid, hi, mid, lo, hi], axis=0)
                update = dot(left, right, 0, 0)
                gram[m, done:, :] = gram[m, done:, :] - update[done:, :128]
                outs[m][0, done:, :] = outs[m][0, done:, :] - update[done:, 128:]


def merge(own, other, choice):
    nodes = own.shape[0]
    vmem = pl.BlockSpec(memory_space=pltpu.VMEM)
    return pl.pallas_call(
        functools.partial(merge_kernel, nodes),
        out_shape=tuple(jax.ShapeDtypeStruct((1, 128, 256), F32) for _ in range(nodes)),
        in_specs=[vmem] * 3,
        out_specs=tuple(vmem for _ in range(nodes)),
        scratch_shapes=[pltpu.VMEM((nodes, 128, 128), F32)],
        compiler_params=pltpu.CompilerParams(vmem_limit_bytes=24 << 20),
        cost_estimate=pl.CostEstimate(
            flops=nodes * 40_000_000, bytes_accessed=nodes * 600_000, transcendentals=0
        ),
    )(own, other, choice)


def transfer_kernel(nodes, info, own, other, *refs):
    basis, out = refs[:nodes], refs[nodes]
    side = info[3]
    for m in range(nodes):
        place = 0 if nodes == 1 else (info[2] if m == 1 else 1 - info[2])
        zh, zl = split2(basis[m][0])
        right = jnp.concatenate([zh, zl, zh], axis=1)
        for part, at in ((own, side), (other, 1 - side)):
            ch, cl = split2(part[m])
            value = dot(jnp.concatenate([ch, ch, cl], axis=1), right, 1, 1) * (1.0 / 256)
            out[0, place, pl.ds(pl.multiple_of(at * 128, 128), 128), :] = value


def transfer(info, own, other, basis):
    nodes = len(basis)
    smem = pl.BlockSpec(memory_space=pltpu.SMEM)
    vmem = pl.BlockSpec(memory_space=pltpu.VMEM)
    return pl.pallas_call(
        functools.partial(transfer_kernel, nodes),
        out_shape=jax.ShapeDtypeStruct((1, nodes, 256, 128), F32),
        in_specs=[smem] + [vmem] * (2 + nodes),
        out_specs=vmem,
        compiler_params=pltpu.CompilerParams(vmem_limit_bytes=24 << 20),
        cost_estimate=pl.CostEstimate(
            flops=nodes * 50_000_000, bytes_accessed=nodes * 600_000, transcendentals=0
        ),
    )(info, own, other, *basis)


def shifted(value, axis, by):
    count = lax.axis_size(axis)
    return lax.ppermute(value, axis, [(i, (i + by) % count) for i in range(count)])


def swapped(value, apart):
    count = lax.axis_size("leaf")
    return lax.ppermute(value, "leaf", [(i, i ^ apart) for i in range(count)])


def one_hot(skeleton, group, members, side):
    chosen = lax.dynamic_slice_in_dim(skeleton, group, 1, axis=1)[:, 0]
    chosen = jnp.concatenate(
        [lax.dynamic_slice_in_dim(chosen, k, 1, axis=0) for k in members], axis=0
    )
    target = chosen + 128 * side - 256 * side * (chosen >= 128)
    return (target[:, :, None] == lax.broadcasted_iota(jnp.int32, (1, 1, 256), 2)).astype(BF)


def local(samples, near_tiles, columns, tile_count, skeleton_one, skeleton_two, skeleton_three):
    d = lax.axis_index("leaf")
    x = lax.axis_index("cols")
    b0, b1, b2 = d & 1, (d >> 1) & 1, (d >> 2) & 1
    infos = [jnp.stack([x, b0, b1, side]).astype(jnp.int32) for side in (b0, b1, b2)]

    own = lax.all_gather(samples, "cols", axis=0, tiled=True)
    received = [
        shifted(
            lax.dynamic_slice_in_dim(near_tiles, ((x + by) % 4) * 4, 4, axis=0), "cols", by
        )
        for by in (1, 2, 3)
    ]
    all_columns = lax.all_gather(columns - (d - 1) * 16, "cols", axis=0)
    cols = lax.dynamic_slice_in_dim(all_columns, x * 4, 4, axis=1)
    cols = jnp.swapaxes(cols, 0, 1).reshape(4, 16)
    counts = lax.dynamic_slice_in_dim(tile_count, x * 4, 4, axis=0)
    leaves = lax.axis_size("leaf")
    up = [(i, i + 1) for i in range(leaves - 1)]
    before = lax.ppermute(own, "leaf", up)
    after = lax.ppermute(own, "leaf", [(j, i) for i, j in up])

    choice_one = one_hot(skeleton_one, d >> 1, (b0 + 2 - 2 * b1, b0 + 2 * b1), b0)
    choice_two = one_hot(skeleton_two, d >> 2, (d & 3,), b1)
    choice_three = one_hot(skeleton_three, d >> 3, (d & 3,), b2)

    send, keep = near(infos[0], cols, counts, near_tiles, received, before, own, after)
    other = swapped(send, 1)
    away, basis = merge(keep, other, choice_one)
    arrived = swapped(away, 2)
    out_one = transfer(infos[0], keep, other, (away, basis))
    (basis_two,) = merge(basis, arrived, choice_two)
    arrived_two = swapped(basis_two, 4)
    out_two = transfer(infos[1], basis, arrived, (basis_two,))
    (top,) = merge(basis_two, arrived_two, choice_three)
    out_three = transfer(infos[2], basis_two, arrived_two, (top,))
    return out_one, out_two, out_three, top[None]


def solution(mesh):
    placed = (
        P(("leaf", "cols"), None),
        P("leaf", "cols", None, None),
        P("leaf", "cols"),
        P("leaf"),
        P("cols", None, None),
        P("cols", None, None),
        P("cols", None, None),
    )
    return jax.shard_map(
        local,
        mesh=mesh,
        in_specs=placed,
        out_specs=(P("leaf", "cols", None, None),) * 4,
        check_vma=False,
    )
```

time: 482 us -> 140 us (0.29)
  other arithmetic: 276 us -> 1.84 us
  waiting for transfers between devices: 113 us -> 42.5 us
  local copies, waits for them, and re-layouts: 40.4 us -> 4.44 us
  blocking collectives: 0 us -> 24.8 us
  Pallas kernels: 0 us -> 21.5 us
  matrix products: 20.6 us -> 0 us
  starting transfers between devices: 17.1 us -> 30.1 us
    another operation x17 -> x2, other arithmetic: 264 us -> 0.15 us  [local(): jnp.stack([x, b0, b1, side]).astype(jnp.int32)]
    ppermute x5 -> x8, waiting for transfers between devices: 41.6 us -> 5.8 us  [the longest x3 5.79 us: swapped(): return lax.ppermute(value, 'leaf', [(i, i ^ apart) for i in range(count)])]
    reduce_scatter x1 -> x0, waiting for transfers between devices: 34.4 us -> none  [local(): lax.psum_scatter(partial_value, 'cols', scatter_dimension=0, tiled=True)]
    gather x5 -> x0, local copies, waits for them, and re-layouts: 30.3 us -> none  [the longest x3 19.3 us: merge_pair(): picked = jax.vmap(lambda block, index: block[index])(stacked, chosen)]
    all_gather x0 -> x1, blocking collectives: none -> 24.8 us  [local(): all_columns = lax.all_gather(columns - (d - 1) * 16, 'cols', axis=0)]
    pallas_call x0 -> x7, Pallas kernels: none -> 21.5 us  [the longest x3 13.6 us: merge(): pl.pallas_call(functools.partial(merge_kernel, nodes), out_shape=tuple((j...]
    dot_general x7 -> x0, matrix products: 15.5 us -> none  [the longest x3 5.65 us: merge_pair(): gram = jnp.einsum('mis,mjs->mij', picked, picked, precision=HIGHEST) / count]
    ppermute x5 -> x8, starting transfers between devices: 17 us -> 30 us  [the longest x3 13.7 us: swapped(): return lax.ppermute(value, 'leaf', [(i, i ^ apart) for i in range(count)])]
  transfers between devices with their start and end apart: 7 -> 9, of which waited for: 7 -> 4; matrix products, arithmetic and copies ran while one was open for 2% -> 4% of each run, Pallas kernels for 0% -> 2%
where the time goes in v1:
time: 140 us; the launch traced here: 139 us
  waiting for transfers between devices  42.5 us (30%)
  starting transfers between devices  30.1 us (22%)
  blocking collectives  24.8 us (18%)
  Pallas kernels  21.5 us (15%)
  between operations  14.3 us (10%)
  local copies, waits for them, and re-layouts  4.44 us (3%)
  other arithmetic  1.84 us (1%)
    all_gather x1, waiting for transfers between devices, local(): own = lax.all_gather(samples, 'cols', axis=0, tiled=True)  36.1 us
    all_gather x1, blocking collectives, local(): all_columns = lax.all_gather(columns - (d - 1) * 16, 'cols', axis=0)  24.8 us
    ppermute x3, starting transfers between devices, swapped(): return lax.ppermute(value, 'leaf', [(i, i ^ apart) for i in range(count)])  13.7 us
    pallas_call x3, Pallas kernels, merge(): pl.pallas_call(functools.partial(merge_kernel, nodes), out_shape=tuple((j...  13.6 us
    ppermute x3, starting transfers between devices, shifted(): lax.ppermute(value, axis, [(i, (i + by) % count) for i in range(count)])  9.56 us
    ppermute x3, waiting for transfers between devices, swapped(): return lax.ppermute(value, 'leaf', [(i, i ^ apart) for i in range(count)])  5.79 us
    ppermute x1, starting transfers between devices, local(): before = lax.ppermute(own, 'leaf', up)  4.86 us
    pallas_call x3, Pallas kernels, transfer(): pl.pallas_call(functools.partial(transfer_kernel, nodes), out_shape=jax.S...  4.55 us
  transfers between devices with their start and end apart: 9, of which 4 were waited for; matrix products, arithmetic and copies ran while one was open for 4% of the time, Pallas kernels for 2%

profile of v1, /device:TPU:1, one launch (start us, length us, event | category | flops | bytes accessed | tf_op | source)
XLA Modules:
  0.0 139.5 jit_solution(7050656327999603390)
XLA Ops:
  8.0 36.1 %all-gather.4.cloned.1.call-done.own = bf16[2048,256]{1,0:T(8,128)(2,1)} async-done(((bf16[512,256]{1,0:T(8,128)(2,1)}), bf16[2048,256]{1,0:T(8,128)(2,1)}) %all-gather.4.cloned.1.call-update) | async-done | bytes 1048592 | tf_op jit(solution)/shard_map/all_gather | solution.py:241
  44.0 4.9 %collective-permute-start.3 = (bf16[2048,256]{1,0:T(8,128)(2,1)}, bf16[2048,256]{1,0:T(8,128)(2,1)}, u32[]{:S(2)}, u32[]{:S(2)}) collective-permute-start(bf16[2048,256]{1,0:T(8,128)(2,1)} %all-gather.4.cloned.1.call-done.own), channel_id=1, source_target_pairs={{0,4},{4,8},{8,12},{12,16},{16,20},{20,24},{24,28},{28,32},{32,36}... | collective-permute-start | bytes 3145736 | tf_op jit(solution)/shard_map/ppermute | solution.py:254
  48.9 1.9 %collective-permute-start.4 = (bf16[2048,256]{1,0:T(8,128)(2,1)}, bf16[2048,256]{1,0:T(8,128)(2,1)}, u32[]{:S(2)}, u32[]{:S(2)}) collective-permute-start(bf16[2048,256]{1,0:T(8,128)(2,1)} %all-gather.4.cloned.1.call-done.own), channel_id=1, source_target_pairs={{4,0},{8,4},{12,8},{16,12},{20,16},{24,20},{28,24},{32,28},{36,32}... | collective-permute-start | bytes 3145736 | tf_op jit(solution)/shard_map/ppermute | solution.py:255
  50.8 2.6 %constant_dynamic-slice_fusion.4 = (bf16[4,4,128,128]{3,2,1,0:T(8,128)(2,1)}, bf16[4,4,128,128]{3,2,1,0:T(8,128)(2,1)}, bf16[4,4,128,128]{3,2,1,0:T(8,128)(2,1)}) fusion(bf16[16,4,128,128]{3,2,1,0:T(8,128)(2,1)} %own_tiles.1, s32[]{:T(128)S(6)} %select_n.65, s32[]{:T(128)S(6)} %select_n.63, s32[]{:T(128)S(6)} %select_n.61), kind=kLoop, calls=%fused_computation.10 | loop fusion | bytes 3145740 | tf_op jit(solution)/shard_map/dynamic_slice | solution.py:244
  53.4 2.2 %collective-permute-start = (bf16[4,4,128,128]{3,2,1,0:T(8,128)(2,1)}, bf16[4,4,128,128]{3,2,1,0:T(8,128)(2,1)}, u32[]{:S(2)}, u32[]{:S(2)}) collective-permute-start(bf16[4,4,128,128]{3,2,1,0:T(8,128)(2,1)} %get-tuple-element.16), channel_id=1, source_target_pairs={{0,1},{1,2},{2,3},{3,0},{4,5},{5,6},{6,7},{7,4},{8,9},{9,10},{10,1... | collective-permute-start | bytes 1572872 | tf_op jit(solution)/shard_map/ppermute | solution.py:218
  55.6 4.3 %collective-permute-start.1 = (bf16[4,4,128,128]{3,2,1,0:T(8,128)(2,1)}, bf16[4,4,128,128]{3,2,1,0:T(8,128)(2,1)}, u32[]{:S(2)}, u32[]{:S(2)}) collective-permute-start(bf16[4,4,128,128]{3,2,1,0:T(8,128)(2,1)} %get-tuple-element.15), channel_id=1, source_target_pairs={{0,2},{1,3},{2,0},{3,1},{4,6},{5,7},{6,4},{7,5},{8,10},{9,11},{10,... | collective-permute-start | bytes 1572872 | tf_op jit(solution)/shard_map/ppermute | solution.py:218
  59.9 3.1 %collective-permute-start.2 = (bf16[4,4,128,128]{3,2,1,0:T(8,128)(2,1)}, bf16[4,4,128,128]{3,2,1,0:T(8,128)(2,1)}, u32[]{:S(2)}, u32[]{:S(2)}) collective-permute-start(bf16[4,4,128,128]{3,2,1,0:T(8,128)(2,1)} %get-tuple-element.14), channel_id=1, source_target_pairs={{0,3},{1,0},{2,1},{3,2},{4,7},{5,4},{6,5},{7,6},{8,11},{9,8},{10,9... | collective-permute-start | bytes 1572872 | tf_op jit(solution)/shard_map/ppermute | solution.py:218
  63.0 24.8 %all-gather.1 = s32[4,16,4]{1,2,0:T(4,128)S(1)} all-gather(s32[1,16,4]{1,2,0:T(4,128)S(1)} %subtract_bitcast_fusion), channel_id=2, replica_groups=mesh['leaf'=128,'cols'=4] {'cols'}, dimensions={0}, use_global_device_ids=true | all-gather | bytes 1280 | tf_op jit(solution)/shard_map/all_gather | solution.py:248
  88.1 0.7 fusion.6
  89.0 3.4 %shard_map.102 = (f32[2,128,256]{2,1,0:T(8,128)S(1)}, f32[2,128,256]{2,1,0:T(8,128)S(1)}) custom-call(s32[4]{0:T(128)S(1)} %get-tuple-element.20.info, s32[4,16]{1,0:T(4,128)S(1)} %copy.13.cols, s32[4]{0:T(128)S(1)} %dynamic_slice.31.counts, bf16[16,4,128,128]{3,2,1,0:T(8,128)(2,1)S(1)} %copy-done, bf16[4,4,128,128]{3,2,1,0:T(8,128)(2,1)} %collective-permute-done.tiles_a, ...), custom_call_target="tpu_custom_call" | custom-call | flops 540000000 | bytes 6000000 | tf_op jit(solution)/shard_map/pallas_call | solution.py:87
  92.4 3.7 %collective-permute-start.5 = (f32[2,128,256]{2,1,0:T(8,128)S(1)}, f32[2,128,256]{2,1,0:T(8,128)S(1)}, u32[]{:S(2)}, u32[]{:S(2)}) collective-permute-start(f32[2,128,256]{2,1,0:T(8,128)S(1)} %get-tuple-element.9), channel_id=1, source_target_pairs={{0,4},{4,0},{8,12},{12,8},{16,20},{20,16},{24,28},{28,24},{32,36},... | collective-permute-start | bytes 786440 | tf_op jit(solution)/shard_map/ppermute | solution.py:223
  96.2 0.7 fusion.9
  97.3 4.9 %shard_map.103 = (f32[1,128,256]{2,1,0:T(8,128)S(1)}, f32[1,128,256]{2,1,0:T(8,128)S(1)}) custom-call(f32[2,128,256]{2,1,0:T(8,128)S(1)} %get-tuple-element.8.own, f32[2,128,256]{2,1,0:T(8,128)S(1)} %collective-permute-done.5.other, bf16[2,128,256]{2,1,0:T(8,128)(2,1)S(1)} %fusion.choice), custom_call_target="tpu_custom_call" | custom-call | flops 80000000 | bytes 1200000 | tf_op jit(solution)/shard_map/pallas_call | solution.py:174
  102.2 4.4 %collective-permute-start.6 = (f32[1,128,256]{2,1,0:T(8,128)S(1)}, f32[1,128,256]{2,1,0:T(8,128)S(1)}, u32[]{:S(2)}, u32[]{:S(2)}) collective-permute-start(f32[1,128,256]{2,1,0:T(8,128)S(1)} %get-tuple-element.10.refs_0_), channel_id=1, source_target_pairs={{0,8},{4,12},{8,0},{12,4},{16,24},{20,28},{24,16},{28,20},{32,40},... | collective-permute-start | bytes 393224 | tf_op jit(solution)/shard_map/ppermute | solution.py:223
  106.7 0.7 fusion.8
  107.4 2.7 %collective-permute-done.6.other = f32[1,128,256]{2,1,0:T(8,128)S(1)} collective-permute-done((f32[1,128,256]{2,1,0:T(8,128)S(1)}, f32[1,128,256]{2,1,0:T(8,128)S(1)}, u32[]{:S(2)}, u32[]{:S(2)}) %collective-permute-start.6) | collective-permute-done | bytes 131104 | tf_op jit(solution)/shard_map/ppermute | solution.py:223
  110.1 4.0 %shard_map.105.refs_0_.own = f32[1,128,256]{2,1,0:T(8,128)S(1)} custom-call(f32[1,128,256]{2,1,0:T(8,128)S(1)} %get-tuple-element.11.refs_1_.own, f32[1,128,256]{2,1,0:T(8,128)S(1)} %collective-permute-done.6.other, bf16[1,128,256]{2,1,0:T(8,128)(2,1)S(1)} %fusion.1.choice), custom_call_target="tpu_custom_call" | custom-call | flops 40000000 | bytes 600000 | tf_op jit(solution)/shard_map/pallas_call | solution.py:174
  114.1 5.6 %collective-permute-start.7 = (f32[1,128,256]{2,1,0:T(8,128)S(1)}, f32[1,128,256]{2,1,0:T(8,128)S(1)}, u32[]{:S(2)}, u32[]{:S(2)}) collective-permute-start(f32[1,128,256]{2,1,0:T(8,128)S(1)} %shard_map.105.refs_0_.own), channel_id=1, source_target_pairs={{0,16},{4,20},{8,24},{12,28},{16,0},{20,4},{24,8},{28,12},{32,48},... | collective-permute-start | bytes 393224 | tf_op jit(solution)/shard_map/ppermute | solution.py:223
  119.8 1.6 %shard_map.104 = f32[1,2,256,128]{3,2,1,0:T(8,128)} custom-call(s32[4]{0:T(128)S(1)} %get-tuple-element.20.info, f32[2,128,256]{2,1,0:T(8,128)S(1)} %get-tuple-element.8.own, f32[2,128,256]{2,1,0:T(8,128)S(1)} %collective-permute-done.5.other, f32[1,128,256]{2,1,0:T(8,128)S(1)} %get-tuple-element.10.refs_0_, f32[1,128,256]{2,1,0:T(8,128)S(1)} %get-tuple-element.11.refs_1_.own), custom_call_target="tpu_custom_call" | custom-call | flops 100000000 | bytes 1200000 | tf_op jit(solution)/shard_map/pallas_call | solution.py:204
  121.4 1.5 %shard_map.106 = f32[1,1,256,128]{3,2,1,0:T(8,128)} custom-call(s32[4]{0:T(128)S(1)} %get-tuple-element.19.info, f32[1,128,256]{2,1,0:T(8,128)S(1)} %get-tuple-element.11.refs_1_.own, f32[1,128,256]{2,1,0:T(8,128)S(1)} %collective-permute-done.6.other, f32[1,128,256]{2,1,0:T(8,128)S(1)} %shard_map.105.refs_0_.own), custom_call_target="tpu_custom_call" | custom-call | flops 50000000 | bytes 600000 | tf_op jit(solution)/shard_map/pallas_call | solution.py:204
  122.9 2.7 %collective-permute-done.7.other = f32[1,128,256]{2,1,0:T(8,128)S(1)} collective-permute-done((f32[1,128,256]{2,1,0:T(8,128)S(1)}, f32[1,128,256]{2,1,0:T(8,128)S(1)}, u32[]{:S(2)}, u32[]{:S(2)}) %collective-permute-start.7) | collective-permute-done | bytes 131104 | tf_op jit(solution)/shard_map/ppermute | solution.py:223
  125.6 4.7 %shard_map.107.refs_0_ = f32[1,128,256]{2,1,0:T(8,128)} custom-call(f32[1,128,256]{2,1,0:T(8,128)S(1)} %shard_map.105.refs_0_.own, f32[1,128,256]{2,1,0:T(8,128)S(1)} %collective-permute-done.7.other, bf16[1,128,256]{2,1,0:T(8,128)(2,1)S(1)} %fusion.2.choice), custom_call_target="tpu_custom_call" | custom-call | flops 40000000 | bytes 600000 | tf_op jit(solution)/shard_map/pallas_call | solution.py:174
  130.3 0.9 copy-done.2
  131.2 1.5 %shard_map.108 = f32[1,1,256,128]{3,2,1,0:T(8,128)} custom-call(s32[4]{0:T(128)S(1)} %get-tuple-element.12.info, f32[1,128,256]{2,1,0:T(8,128)S(1)} %shard_map.105.refs_0_.own, f32[1,128,256]{2,1,0:T(8,128)S(1)} %collective-permute-done.7.other, f32[1,128,256]{2,1,0:T(8,128)S(1)} %copy-done.2), custom_call_target="tpu_custom_call" | custom-call | flops 50000000 | bytes 600000 | tf_op jit(solution)/shard_map/pallas_call | solution.py:204
  (27 shorter events, 1.7 us)
Async XLA Ops:
  7.2 81.8 %copy-start = (bf16[16,4,128,128]{3,2,1,0:T(8,128)(2,1)S(1)}, bf16[16,4,128,128]{3,2,1,0:T(8,128)(2,1)}, u32[]{:S(2)}) copy-start(bf16[16,4,128,128]{3,2,1,0:T(8,128)(2,1)} %own_tiles.1) | copy-start | bytes 6291460
  7.2 55.8 %copy-start.3 = (s32[16,4]{0,1:T(4,128)S(1)}, s32[16,4]{0,1:T(4,128)}, u32[]{:S(2)}) copy-start(s32[16,4]{0,1:T(4,128)} %param.9) | copy-start | bytes 772
  7.2 80.8 %copy-start.4 = (s32[16]{0:T(128)S(1)}, s32[16]{0:T(128)}, u32[]{:S(2)}) copy-start(s32[16]{0:T(128)} %param.10) | copy-start | bytes 196
  7.2 36.8 %all-gather.4.cloned.1.call-start = ((), (), s32[]{:S(2)}) async-start(), calls=%async_computation | async-start | bytes 1310720 | tf_op jit(solution)/shard_map/all_gather | solution.py:241
  44.0 44.9 %copy-start.1 = (bf16[2048,256]{1,0:T(8,128)(2,1)S(1)}, bf16[2048,256]{1,0:T(8,128)(2,1)}, u32[]{:S(2)}) copy-start(bf16[2048,256]{1,0:T(8,128)(2,1)} %all-gather.4.cloned.1.call-done.own) | copy-start | bytes 3145732
  44.0 44.9 %collective-permute-start.3 = (bf16[2048,256]{1,0:T(8,128)(2,1)}, bf16[2048,256]{1,0:T(8,128)(2,1)}, u32[]{:S(2)}, u32[]{:S(2)}) collective-permute-start(bf16[2048,256]{1,0:T(8,128)(2,1)} %all-gather.4.cloned.1.call-done.own), channel_id=1, source_target_pairs={{0,4},{4,8},{8,12},{12,16},{16,20},{20,24},{24,28},{28,32},{32,36}... | collective-permute-start | bytes 3145736 | tf_op jit(solution)/shard_map/ppermute | solution.py:254
  48.9 40.1 %collective-permute-start.4 = (bf16[2048,256]{1,0:T(8,128)(2,1)}, bf16[2048,256]{1,0:T(8,128)(2,1)}, u32[]{:S(2)}, u32[]{:S(2)}) collective-permute-start(bf16[2048,256]{1,0:T(8,128)(2,1)} %all-gather.4.cloned.1.call-done.own), channel_id=1, source_target_pairs={{4,0},{8,4},{12,8},{16,12},{20,16},{24,20},{28,24},{32,28},{36,32}... | collective-permute-start | bytes 3145736 | tf_op jit(solution)/shard_map/ppermute | solution.py:255
  53.4 35.5 %collective-permute-start = (bf16[4,4,128,128]{3,2,1,0:T(8,128)(2,1)}, bf16[4,4,128,128]{3,2,1,0:T(8,128)(2,1)}, u32[]{:S(2)}, u32[]{:S(2)}) collective-permute-start(bf16[4,4,128,128]{3,2,1,0:T(8,128)(2,1)} %get-tuple-element.16), channel_id=1, source_target_pairs={{0,1},{1,2},{2,3},{3,0},{4,5},{5,6},{6,7},{7,4},{8,9},{9,10},{10,1... | collective-permute-start | bytes 1572872 | tf_op jit(solution)/shard_map/ppermute | solution.py:218
  55.6 33.3 %collective-permute-start.1 = (bf16[4,4,128,128]{3,2,1,0:T(8,128)(2,1)}, bf16[4,4,128,128]{3,2,1,0:T(8,128)(2,1)}, u32[]{:S(2)}, u32[]{:S(2)}) collective-permute-start(bf16[4,4,128,128]{3,2,1,0:T(8,128)(2,1)} %get-tuple-element.15), channel_id=1, source_target_pairs={{0,2},{1,3},{2,0},{3,1},{4,6},{5,7},{6,4},{7,5},{8,10},{9,11},{10,... | collective-permute-start | bytes 1572872 | tf_op jit(solution)/shard_map/ppermute | solution.py:218
  59.9 29.0 %collective-permute-start.2 = (bf16[4,4,128,128]{3,2,1,0:T(8,128)(2,1)}, bf16[4,4,128,128]{3,2,1,0:T(8,128)(2,1)}, u32[]{:S(2)}, u32[]{:S(2)}) collective-permute-start(bf16[4,4,128,128]{3,2,1,0:T(8,128)(2,1)} %get-tuple-element.14), channel_id=1, source_target_pairs={{0,3},{1,0},{2,1},{3,2},{4,7},{5,4},{6,5},{7,6},{8,11},{9,8},{10,9... | collective-permute-start | bytes 1572872 | tf_op jit(solution)/shard_map/ppermute | solution.py:218
  92.4 4.9 %collective-permute-start.5 = (f32[2,128,256]{2,1,0:T(8,128)S(1)}, f32[2,128,256]{2,1,0:T(8,128)S(1)}, u32[]{:S(2)}, u32[]{:S(2)}) collective-permute-start(f32[2,128,256]{2,1,0:T(8,128)S(1)} %get-tuple-element.9), channel_id=1, source_target_pairs={{0,4},{4,0},{8,12},{12,8},{16,20},{20,16},{24,28},{28,24},{32,36},... | collective-permute-start | bytes 786440 | tf_op jit(solution)/shard_map/ppermute | solution.py:223
  102.2 7.9 %collective-permute-start.6 = (f32[1,128,256]{2,1,0:T(8,128)S(1)}, f32[1,128,256]{2,1,0:T(8,128)S(1)}, u32[]{:S(2)}, u32[]{:S(2)}) collective-permute-start(f32[1,128,256]{2,1,0:T(8,128)S(1)} %get-tuple-element.10.refs_0_), channel_id=1, source_target_pairs={{0,8},{4,12},{8,0},{12,4},{16,24},{20,28},{24,16},{28,20},{32,40},... | collective-permute-start | bytes 393224 | tf_op jit(solution)/shard_map/ppermute | solution.py:223
  114.1 11.5 %collective-permute-start.7 = (f32[1,128,256]{2,1,0:T(8,128)S(1)}, f32[1,128,256]{2,1,0:T(8,128)S(1)}, u32[]{:S(2)}, u32[]{:S(2)}) collective-permute-start(f32[1,128,256]{2,1,0:T(8,128)S(1)} %shard_map.105.refs_0_.own), channel_id=1, source_target_pairs={{0,16},{4,20},{8,24},{12,28},{16,0},{20,4},{24,8},{28,12},{32,48},... | collective-permute-start | bytes 393224 | tf_op jit(solution)/shard_map/ppermute | solution.py:223
  130.3 0.9 copy-start.2
Sparse Core Ops, SparseCore 0:
  10.1 33.8 all-gather.3

commit v2 on v1

--- a/solution.py
+++ b/solution.py
@@ -32,7 +32,7 @@
 
 
 def near_kernel(
-    info, cols, counts, own_tiles, tiles_a, tiles_b, tiles_c, before, own, after,
+    info, cols, counts, own_tiles, tiles_a, tiles_b, tiles_c, tiles_d, before, own, after,
     send_ref, keep_ref, win, tiles, sem,
 ):
     x = info[0]
@@ -43,9 +43,10 @@
         pltpu.make_async_copy(before, win.at[pl.ds(0, 2048)], sem.at[1]),
         pltpu.make_async_copy(after, win.at[pl.ds(4096, 2048)], sem.at[2]),
         pltpu.make_async_copy(own_tiles.at[pl.ds(x * 4, 4)], tiles.at[0], sem.at[3]),
-        pltpu.make_async_copy(tiles_a, tiles.at[1], sem.at[4]),
-        pltpu.make_async_copy(tiles_b, tiles.at[2], sem.at[5]),
-        pltpu.make_async_copy(tiles_c, tiles.at[3], sem.at[6]),
+        pltpu.make_async_copy(tiles_a.at[pl.ds(0, 4)], tiles.at[1], sem.at[4]),
+        pltpu.make_async_copy(tiles_b, tiles.at[2, pl.ds(0, 2)], sem.at[5]),
+        pltpu.make_async_copy(tiles_c, tiles.at[2, pl.ds(2, 2)], sem.at[6]),
+        pltpu.make_async_copy(tiles_d.at[pl.ds(0, 4)], tiles.at[3], sem.at[7]),
     ]
     for copy in copies:
         copy.start()
@@ -54,8 +55,7 @@
     for q in range(4):
         keep, slot = divmod(q, 2)
         parity = even if keep == 1 else 1 - even
-        member = late if slot == 1 else 1 - late
-        k = parity + 2 * member
+        k = parity + 2 * (late if slot == 1 else 1 - late)
         count = counts[k]
         total = jnp.zeros((128, 256), F32)
         for delta in range(4):
@@ -68,7 +68,9 @@
                     live = jnp.where(place < count, 1.0, 0.0).astype(F32)
                     piece = tiles[delta, k, t]
                     pieces.append(piece * jnp.full((128, 128), live, F32).astype(BF))
-                    col = jnp.clip(cols[k, place], 0, 47)
+                    col = jnp.clip(cols[delta * 4 + k, t], 0, 47)
+                    member = col & 15
+                    col = (col - member) + ((x - (member >> 2)) & 3) * 4 + (member & 3)
                     rows.append(win[pl.ds(pl.multiple_of(col * 128, 128), 128), :])
                 total = total + dot(
                     jnp.concatenate(pieces, axis=1), jnp.concatenate(rows, axis=0), 1, 0
@@ -87,12 +89,12 @@
     return pl.pallas_call(
         near_kernel,
         out_shape=(block, block),
-        in_specs=[smem] * 3 + [hbm] * 7,
+        in_specs=[smem] * 3 + [hbm] * 8,
         out_specs=(vmem, vmem),
         scratch_shapes=[
             pltpu.VMEM((6144, 256), BF),
             pltpu.VMEM((4, 4, 4, 128, 128), BF),
-            pltpu.SemaphoreType.DMA((7,)),
+            pltpu.SemaphoreType.DMA((8,)),
         ],
         compiler_params=pltpu.CompilerParams(vmem_limit_bytes=24 << 20),
         cost_estimate=pl.CostEstimate(
@@ -238,16 +240,21 @@
     b0, b1, b2 = d & 1, (d >> 1) & 1, (d >> 2) & 1
     infos = [jnp.stack([x, b0, b1, side]).astype(jnp.int32) for side in (b0, b1, b2)]
 
-    own = lax.all_gather(samples, "cols", axis=0, tiled=True)
+    near_columns = jnp.clip(columns - (d - 1) * 16, 0, 47).astype(BF)
+    block = jnp.concatenate([samples, jnp.pad(near_columns, ((0, 0), (0, 252)))], axis=0)
+    blocks = [block] + [shifted(block, "cols", by) for by in (1, 3, 2)]
+    blocks = [blocks[0], blocks[1], blocks[3], blocks[2]]
+    def tiles_of(by, start, size):
+        return lax.dynamic_slice_in_dim(near_tiles, ((x + by) % 4) * 4 + start, size, axis=0)
+
+    far_up = shifted(jnp.concatenate([tiles_of(1, 0, 4), tiles_of(2, 0, 2)]), "cols", 1)
+    far_down = shifted(jnp.concatenate([tiles_of(3, 0, 4), tiles_of(2, 2, 2)]), "cols", 3)
     received = [
-        shifted(
-            lax.dynamic_slice_in_dim(near_tiles, ((x + by) % 4) * 4, 4, axis=0), "cols", by
-        )
-        for by in (1, 2, 3)
-    ]
-    all_columns = lax.all_gather(columns - (d - 1) * 16, "cols", axis=0)
-    cols = lax.dynamic_slice_in_dim(all_columns, x * 4, 4, axis=1)
-    cols = jnp.swapaxes(cols, 0, 1).reshape(4, 16)
+        far_up, shifted(far_up[4:], "cols", 1), shifted(far_down[4:], "cols", 3), far_down,
+    ]
+    own = jnp.concatenate([samples] + [part[:512] for part in blocks[1:]], axis=0)
+    cols = jnp.stack([part[512:, :4] for part in blocks])
+    cols = lax.dynamic_slice_in_dim(cols, x * 4, 4, axis=1).astype(jnp.int32).reshape(16, 4)
     counts = lax.dynamic_slice_in_dim(tile_count, x * 4, 4, axis=0)
     leaves = lax.axis_size("leaf")
     up = [(i, i + 1) for i in range(leaves - 1)]

time: 140 us -> 98.6 us (0.70)
  waiting for transfers between devices: 42.5 us -> 9.02 us
  blocking collectives: 24.8 us -> 0 us
  starting transfers between devices: 30.1 us -> 47.6 us
  between operations: 14.3 us -> 1.02 us
  local copies, waits for them, and re-layouts: 4.44 us -> 13 us
  other arithmetic: 1.84 us -> 4.9 us
    all_gather x1 -> x0, waiting for transfers between devices: 36.1 us -> none  [local(): own = lax.all_gather(samples, 'cols', axis=0, tiled=True)]
    all_gather x1 -> x0, blocking collectives: 24.8 us -> none  [local(): all_columns = lax.all_gather(columns - (d - 1) * 16, 'cols', axis=0)]
    ppermute x3 -> x7, starting transfers between devices: 9.56 us -> 24.3 us  [shifted(): lax.ppermute(value, axis, [(i, (i + by) % count) for i in range(count)])]
    slice x0 -> x11, local copies, waits for them, and re-layouts: none -> 5.72 us  [the longest x6 2.32 us: local(): cols = jnp.stack([part[512:, :4] for part in blocks])]
    unnamed x10 -> x19, local copies, waits for them, and re-layouts: 0.92 us -> 4.91 us
    concatenate x0 -> x4, other arithmetic: none -> 2.97 us  [the longest x1 0.98 us: local(): jnp.concatenate([tiles_of(3, 0, 4), tiles_of(2, 2, 2)])]
    ppermute x3 -> x7, waiting for transfers between devices: 0.01 us -> 2.7 us  [shifted(): lax.ppermute(value, axis, [(i, (i + by) % count) for i in range(count)])]
  transfers between devices with their start and end apart: 9 -> 12, of which waited for: 4 -> 4; matrix products, arithmetic and copies ran while one was open for 4% -> 12% of each run, Pallas kernels for 2% -> 3%
where the time goes in v2:
time: 98.6 us; the launch traced here: 97.1 us
  starting transfers between devices  47.6 us (48%)
  Pallas kernels  21.6 us (22%)
  local copies, waits for them, and re-layouts  13 us (13%)
  waiting for transfers between devices  9.02 us (9%)
  other arithmetic  4.9 us (5%)
  between operations  1.02 us (1%)
    ppermute x7, starting transfers between devices, shifted(): lax.ppermute(value, axis, [(i, (i + by) % count) for i in range(count)])  24.3 us
    ppermute x3, starting transfers between devices, swapped(): return lax.ppermute(value, 'leaf', [(i, i ^ apart) for i in range(count)])  14.1 us
    pallas_call x3, Pallas kernels, merge(): pl.pallas_call(functools.partial(merge_kernel, nodes), out_shape=tuple((j...  13.5 us
    ppermute x3, waiting for transfers between devices, swapped(): return lax.ppermute(value, 'leaf', [(i, i ^ apart) for i in range(count)])  6.31 us
    ppermute x1, starting transfers between devices, local(): before = lax.ppermute(own, 'leaf', up)  5.96 us
    unnamed x19, local copies, waits for them, and re-layouts  4.91 us
    pallas_call x3, Pallas kernels, transfer(): pl.pallas_call(functools.partial(transfer_kernel, nodes), out_shape=jax.S...  4.55 us
    pallas_call x1, Pallas kernels, near(): pl.pallas_call(near_kernel, out_shape=(block, block), in_specs=[smem] * 3...  3.45 us
  transfers between devices with their start and end apart: 12, of which 4 were waited for; matrix products, arithmetic and copies ran while one was open for 12% of the time, Pallas kernels for 3%

profile of v2, /device:TPU:1, one launch (start us, length us, event | category | flops | bytes accessed | tf_op | source)
XLA Modules:
  0.0 97.1 jit_solution(2957008385596219819)
XLA Ops:
  2.5 3.9 %collective-permute-start = (bf16[528,256]{1,0:T(8,128)(2,1)S(1)}, bf16[528,256]{1,0:T(8,128)(2,1)S(1)}, u32[]{:S(2)}, u32[]{:S(2)}) collective-permute-start(bf16[528,256]{1,0:T(8,128)(2,1)S(1)} %fusion.1), channel_id=1, source_target_pairs={{0,1},{1,2},{2,3},{3,0},{4,5},{5,6},{6,7},{7,4},{8,9},{9,10},{10,1... | collective-permute-start | bytes 811016 | tf_op jit(solution)/shard_map/ppermute | solution.py:220
  6.5 4.4 %collective-permute-start.1 = (bf16[528,256]{1,0:T(8,128)(2,1)S(1)}, bf16[528,256]{1,0:T(8,128)(2,1)S(1)}, u32[]{:S(2)}, u32[]{:S(2)}) collective-permute-start(bf16[528,256]{1,0:T(8,128)(2,1)S(1)} %fusion.1), channel_id=1, source_target_pairs={{0,2},{1,3},{2,0},{3,1},{4,6},{5,7},{6,4},{7,5},{8,10},{9,11},{10,... | collective-permute-start | bytes 811016 | tf_op jit(solution)/shard_map/ppermute | solution.py:220
  10.9 3.1 %collective-permute-start.2 = (bf16[528,256]{1,0:T(8,128)(2,1)S(1)}, bf16[528,256]{1,0:T(8,128)(2,1)S(1)}, u32[]{:S(2)}, u32[]{:S(2)}) collective-permute-start(bf16[528,256]{1,0:T(8,128)(2,1)S(1)} %fusion.1), channel_id=1, source_target_pairs={{0,3},{1,0},{2,1},{3,2},{4,7},{5,4},{6,5},{7,6},{8,11},{9,8},{10,9... | collective-permute-start | bytes 811016 | tf_op jit(solution)/shard_map/ppermute | solution.py:220
  16.3 2.2 %collective-permute-start.3 = (bf16[6,4,128,128]{3,2,1,0:T(8,128)(2,1)}, bf16[6,4,128,128]{3,2,1,0:T(8,128)(2,1)}, u32[]{:S(2)}, u32[]{:S(2)}) collective-permute-start(bf16[6,4,128,128]{3,2,1,0:T(8,128)(2,1)} %pad_maximum_fusion.1), channel_id=1, source_target_pairs={{0,1},{1,2},{2,3},{3,0},{4,5},{5,6},{6,7},{7,4},{8,9},{9,10},{10,1... | collective-permute-start | bytes 2359304 | tf_op jit(solution)/shard_map/ppermute | solution.py:220
  19.5 4.3 %collective-permute-start.5 = (bf16[6,4,128,128]{3,2,1,0:T(8,128)(2,1)}, bf16[6,4,128,128]{3,2,1,0:T(8,128)(2,1)}, u32[]{:S(2)}, u32[]{:S(2)}) collective-permute-start(bf16[6,4,128,128]{3,2,1,0:T(8,128)(2,1)} %pad_maximum_fusion.2), channel_id=1, source_target_pairs={{0,3},{1,0},{2,1},{3,2},{4,7},{5,4},{6,5},{7,6},{8,11},{9,8},{10,9... | collective-permute-start | bytes 2359304 | tf_op jit(solution)/shard_map/ppermute | solution.py:220
  25.4 6.0 %collective-permute-start.7 = (bf16[2048,256]{1,0:T(8,128)(2,1)S(1)}, bf16[2048,256]{1,0:T(8,128)(2,1)}, u32[]{:S(2)}, u32[]{:S(2)}) collective-permute-start(bf16[2048,256]{1,0:T(8,128)(2,1)S(1)} %pad_maximum_fusion.own), channel_id=1, source_target_pairs={{0,4},{4,8},{8,12},{12,16},{16,20},{20,24},{24,28},{28,32},{32,36}... | collective-permute-start | bytes 3145736 | tf_op jit(solution)/shard_map/ppermute | solution.py:261
  31.4 3.3 %collective-permute-start.8 = (bf16[2048,256]{1,0:T(8,128)(2,1)S(1)}, bf16[2048,256]{1,0:T(8,128)(2,1)}, u32[]{:S(2)}, u32[]{:S(2)}) collective-permute-start(bf16[2048,256]{1,0:T(8,128)(2,1)S(1)} %pad_maximum_fusion.own), channel_id=1, source_target_pairs={{4,0},{8,4},{12,8},{16,12},{20,16},{24,20},{28,24},{32,28},{36,32}... | collective-permute-start | bytes 3145736 | tf_op jit(solution)/shard_map/ppermute | solution.py:262
  34.8 2.7 %collective-permute-done.3.tiles_a = bf16[6,4,128,128]{3,2,1,0:T(8,128)(2,1)} collective-permute-done((bf16[6,4,128,128]{3,2,1,0:T(8,128)(2,1)}, bf16[6,4,128,128]{3,2,1,0:T(8,128)(2,1)}, u32[]{:S(2)}, u32[]{:S(2)}) %collective-permute-start.3) | collective-permute-done | bytes 786464 | tf_op jit(solution)/shard_map/ppermute | solution.py:220
  37.5 1.7 %slice.36 = bf16[2,4,128,128]{3,2,1,0:T(8,128)(2,1)} slice(bf16[6,4,128,128]{3,2,1,0:T(8,128)(2,1)} %collective-permute-done.3.tiles_a), slice={[4:6], [0:4], [0:128], [0:128]} | slice | bytes 524288 | tf_op jit(solution)/shard_map/slice | solution.py:253
  39.2 1.9 %collective-permute-start.4 = (bf16[2,4,128,128]{3,2,1,0:T(8,128)(2,1)}, bf16[2,4,128,128]{3,2,1,0:T(8,128)(2,1)S(1)}, u32[]{:S(2)}, u32[]{:S(2)}) collective-permute-start(bf16[2,4,128,128]{3,2,1,0:T(8,128)(2,1)} %slice.36), channel_id=1, source_target_pairs={{0,1},{1,2},{2,3},{3,0},{4,5},{5,6},{6,7},{7,4},{8,9},{9,10},{10,1... | collective-permute-start | bytes 786440 | tf_op jit(solution)/shard_map/ppermute | solution.py:220
  41.1 1.7 %slice.37 = bf16[2,4,128,128]{3,2,1,0:T(8,128)(2,1)} slice(bf16[6,4,128,128]{3,2,1,0:T(8,128)(2,1)} %collective-permute-done.5.tiles_d), slice={[4:6], [0:4], [0:128], [0:128]} | slice | bytes 524288 | tf_op jit(solution)/shard_map/slice | solution.py:253
  42.8 4.6 %collective-permute-start.6 = (bf16[2,4,128,128]{3,2,1,0:T(8,128)(2,1)}, bf16[2,4,128,128]{3,2,1,0:T(8,128)(2,1)}, u32[]{:S(2)}, u32[]{:S(2)}) collective-permute-start(bf16[2,4,128,128]{3,2,1,0:T(8,128)(2,1)} %slice.37), channel_id=1, source_target_pairs={{0,3},{1,0},{2,1},{3,2},{4,7},{5,4},{6,5},{7,6},{8,11},{9,8},{10,9... | collective-permute-start | bytes 786440 | tf_op jit(solution)/shard_map/ppermute | solution.py:220
  52.5 3.5 %shard_map.102 = (f32[2,128,256]{2,1,0:T(8,128)S(1)}, f32[2,128,256]{2,1,0:T(8,128)S(1)}) custom-call(s32[4]{0:T(128)S(1)} %get-tuple-element.21.info, s32[16,4]{1,0:T(8,128)S(1)} %bitcast.19, s32[4]{0:T(128)S(1)} %dynamic_slice.34.counts, bf16[16,4,128,128]{3,2,1,0:T(8,128)(2,1)S(1)} %copy-done, bf16[6,4,128,128]{3,2,1,0:T(8,128)(2,1)} %collective-permute-done.3.tiles_a, ...), custom_call_target="tpu_custom_call" | custom-call | flops 540000000 | bytes 6000000 | tf_op jit(solution)/shard_map/pallas_call | solution.py:89
  55.9 6.3 %collective-permute-start.9 = (f32[2,128,256]{2,1,0:T(8,128)S(1)}, f32[2,128,256]{2,1,0:T(8,128)S(1)}, u32[]{:S(2)}, u32[]{:S(2)}) collective-permute-start(f32[2,128,256]{2,1,0:T(8,128)S(1)} %get-tuple-element.9), channel_id=1, source_target_pairs={{0,4},{4,0},{8,12},{12,8},{16,20},{20,16},{24,28},{28,24},{32,36},... | collective-permute-start | bytes 786440 | tf_op jit(solution)/shard_map/ppermute | solution.py:225
  63.4 4.9 %shard_map.103 = (f32[1,128,256]{2,1,0:T(8,128)S(1)}, f32[1,128,256]{2,1,0:T(8,128)S(1)}) custom-call(f32[2,128,256]{2,1,0:T(8,128)S(1)} %get-tuple-element.8.own, f32[2,128,256]{2,1,0:T(8,128)S(1)} %collective-permute-done.9.other, bf16[2,128,256]{2,1,0:T(8,128)(2,1)S(1)} %fusion.2.choice), custom_call_target="tpu_custom_call" | custom-call | flops 80000000 | bytes 1200000 | tf_op jit(solution)/shard_map/pallas_call | solution.py:176
  68.2 2.5 %collective-permute-start.10 = (f32[1,128,256]{2,1,0:T(8,128)S(1)}, f32[1,128,256]{2,1,0:T(8,128)S(1)}, u32[]{:S(2)}, u32[]{:S(2)}) collective-permute-start(f32[1,128,256]{2,1,0:T(8,128)S(1)} %get-tuple-element.10.refs_0_), channel_id=1, source_target_pairs={{0,8},{4,12},{8,0},{12,4},{16,24},{20,28},{24,16},{28,20},{32,40},... | collective-permute-start | bytes 393224 | tf_op jit(solution)/shard_map/ppermute | solution.py:225
  71.6 3.3 %collective-permute-done.10.other = f32[1,128,256]{2,1,0:T(8,128)S(1)} collective-permute-done((f32[1,128,256]{2,1,0:T(8,128)S(1)}, f32[1,128,256]{2,1,0:T(8,128)S(1)}, u32[]{:S(2)}, u32[]{:S(2)}) %collective-permute-start.10) | collective-permute-done | bytes 131104 | tf_op jit(solution)/shard_map/ppermute | solution.py:225
  74.8 4.0 %shard_map.105.refs_0_.own = f32[1,128,256]{2,1,0:T(8,128)S(1)} custom-call(f32[1,128,256]{2,1,0:T(8,128)S(1)} %get-tuple-element.11.refs_1_.own, f32[1,128,256]{2,1,0:T(8,128)S(1)} %collective-permute-done.10.other, bf16[1,128,256]{2,1,0:T(8,128)(2,1)S(1)} %fusion.3.choice), custom_call_target="tpu_custom_call" | custom-call | flops 40000000 | bytes 600000 | tf_op jit(solution)/shard_map/pallas_call | solution.py:176
  78.8 5.3 %collective-permute-start.11 = (f32[1,128,256]{2,1,0:T(8,128)S(1)}, f32[1,128,256]{2,1,0:T(8,128)S(1)}, u32[]{:S(2)}, u32[]{:S(2)}) collective-permute-start(f32[1,128,256]{2,1,0:T(8,128)S(1)} %shard_map.105.refs_0_.own), channel_id=1, source_target_pairs={{0,16},{4,20},{8,24},{12,28},{16,0},{20,4},{24,8},{28,12},{32,48},... | collective-permute-start | bytes 393224 | tf_op jit(solution)/shard_map/ppermute | solution.py:225
  84.2 1.6 %shard_map.104 = f32[1,2,256,128]{3,2,1,0:T(8,128)} custom-call(s32[4]{0:T(128)S(1)} %get-tuple-element.21.info, f32[2,128,256]{2,1,0:T(8,128)S(1)} %get-tuple-element.8.own, f32[2,128,256]{2,1,0:T(8,128)S(1)} %collective-permute-done.9.other, f32[1,128,256]{2,1,0:T(8,128)S(1)} %get-tuple-element.10.refs_0_, f32[1,128,256]{2,1,0:T(8,128)S(1)} %get-tuple-element.11.refs_1_.own), custom_call_target="tpu_custom_call" | custom-call | flops 100000000 | bytes 1200000 | tf_op jit(solution)/shard_map/pallas_call | solution.py:206
  85.8 1.5 %shard_map.106 = f32[1,1,256,128]{3,2,1,0:T(8,128)} custom-call(s32[4]{0:T(128)S(1)} %get-tuple-element.20.info, f32[1,128,256]{2,1,0:T(8,128)S(1)} %get-tuple-element.11.refs_1_.own, f32[1,128,256]{2,1,0:T(8,128)S(1)} %collective-permute-done.10.other, f32[1,128,256]{2,1,0:T(8,128)S(1)} %shard_map.105.refs_0_.own), custom_call_target="tpu_custom_call" | custom-call | flops 50000000 | bytes 600000 | tf_op jit(solution)/shard_map/pallas_call | solution.py:206
  87.3 2.7 %collective-permute-done.11.other = f32[1,128,256]{2,1,0:T(8,128)S(1)} collective-permute-done((f32[1,128,256]{2,1,0:T(8,128)S(1)}, f32[1,128,256]{2,1,0:T(8,128)S(1)}, u32[]{:S(2)}, u32[]{:S(2)}) %collective-permute-start.11) | collective-permute-done | bytes 131104 | tf_op jit(solution)/shard_map/ppermute | solution.py:225
  90.0 4.7 %shard_map.107.refs_0_ = f32[1,128,256]{2,1,0:T(8,128)} custom-call(f32[1,128,256]{2,1,0:T(8,128)S(1)} %shard_map.105.refs_0_.own, f32[1,128,256]{2,1,0:T(8,128)S(1)} %collective-permute-done.11.other, bf16[1,128,256]{2,1,0:T(8,128)(2,1)S(1)} %fusion.4.choice), custom_call_target="tpu_custom_call" | custom-call | flops 40000000 | bytes 600000 | tf_op jit(solution)/shard_map/pallas_call | solution.py:176
  95.6 1.5 %shard_map.108 = f32[1,1,256,128]{3,2,1,0:T(8,128)} custom-call(s32[4]{0:T(128)S(1)} %get-tuple-element.12.info, f32[1,128,256]{2,1,0:T(8,128)S(1)} %shard_map.105.refs_0_.own, f32[1,128,256]{2,1,0:T(8,128)S(1)} %collective-permute-done.11.other, f32[1,128,256]{2,1,0:T(8,128)S(1)} %copy-done.1), custom_call_target="tpu_custom_call" | custom-call | flops 50000000 | bytes 600000 | tf_op jit(solution)/shard_map/pallas_call | solution.py:206
  (57 shorter events, 14.9 us)
Async XLA Ops:
  0.6 14.6 %copy-start = (bf16[16,4,128,128]{3,2,1,0:T(8,128)(2,1)S(1)}, bf16[16,4,128,128]{3,2,1,0:T(8,128)(2,1)}, u32[]{:S(2)}) copy-start(bf16[16,4,128,128]{3,2,1,0:T(8,128)(2,1)} %own_tiles.1) | copy-start | bytes 6291460
  2.5 21.2 %collective-permute-start = (bf16[528,256]{1,0:T(8,128)(2,1)S(1)}, bf16[528,256]{1,0:T(8,128)(2,1)S(1)}, u32[]{:S(2)}, u32[]{:S(2)}) collective-permute-start(bf16[528,256]{1,0:T(8,128)(2,1)S(1)} %fusion.1), channel_id=1, source_target_pairs={{0,1},{1,2},{2,3},{3,0},{4,5},{5,6},{6,7},{7,4},{8,9},{9,10},{10,1... | collective-permute-start | bytes 811016 | tf_op jit(solution)/shard_map/ppermute | solution.py:220
  6.5 17.3 %collective-permute-start.1 = (bf16[528,256]{1,0:T(8,128)(2,1)S(1)}, bf16[528,256]{1,0:T(8,128)(2,1)S(1)}, u32[]{:S(2)}, u32[]{:S(2)}) collective-permute-start(bf16[528,256]{1,0:T(8,128)(2,1)S(1)} %fusion.1), channel_id=1, source_target_pairs={{0,2},{1,3},{2,0},{3,1},{4,6},{5,7},{6,4},{7,5},{8,10},{9,11},{10,... | collective-permute-start | bytes 811016 | tf_op jit(solution)/shard_map/ppermute | solution.py:220
  10.9 13.0 %collective-permute-start.2 = (bf16[528,256]{1,0:T(8,128)(2,1)S(1)}, bf16[528,256]{1,0:T(8,128)(2,1)S(1)}, u32[]{:S(2)}, u32[]{:S(2)}) collective-permute-start(bf16[528,256]{1,0:T(8,128)(2,1)S(1)} %fusion.1), channel_id=1, source_target_pairs={{0,3},{1,0},{2,1},{3,2},{4,7},{5,4},{6,5},{7,6},{8,11},{9,8},{10,9... | collective-permute-start | bytes 811016 | tf_op jit(solution)/shard_map/ppermute | solution.py:220
  15.3 10.0 %copy-start.4 = (bf16[512,256]{1,0:T(8,128)(2,1)S(1)}, bf16[512,256]{1,0:T(8,128)(2,1)}, u32[]{:S(2)}) copy-start(bf16[512,256]{1,0:T(8,128)(2,1)} %param.7) | copy-start | bytes 786436
  16.3 21.2 %collective-permute-start.3 = (bf16[6,4,128,128]{3,2,1,0:T(8,128)(2,1)}, bf16[6,4,128,128]{3,2,1,0:T(8,128)(2,1)}, u32[]{:S(2)}, u32[]{:S(2)}) collective-permute-start(bf16[6,4,128,128]{3,2,1,0:T(8,128)(2,1)} %pad_maximum_fusion.1), channel_id=1, source_target_pairs={{0,1},{1,2},{2,3},{3,0},{4,5},{5,6},{6,7},{7,4},{8,9},{9,10},{10,1... | collective-permute-start | bytes 2359304 | tf_op jit(solution)/shard_map/ppermute | solution.py:220
  19.5 21.6 %collective-permute-start.5 = (bf16[6,4,128,128]{3,2,1,0:T(8,128)(2,1)}, bf16[6,4,128,128]{3,2,1,0:T(8,128)(2,1)}, u32[]{:S(2)}, u32[]{:S(2)}) collective-permute-start(bf16[6,4,128,128]{3,2,1,0:T(8,128)(2,1)} %pad_maximum_fusion.2), channel_id=1, source_target_pairs={{0,3},{1,0},{2,1},{3,2},{4,7},{5,4},{6,5},{7,6},{8,11},{9,8},{10,9... | collective-permute-start | bytes 2359304 | tf_op jit(solution)/shard_map/ppermute | solution.py:220
  23.8 0.7 copy-start.5
  23.8 24.4 %copy-start.8 = (s32[16]{0:T(128)S(1)}, s32[16]{0:T(128)}, u32[]{:S(2)}) copy-start(s32[16]{0:T(128)} %param.10) | copy-start | bytes 196
  23.8 0.7 copy-start.6
  24.6 0.7 copy-start.7
  25.4 26.1 %collective-permute-start.7 = (bf16[2048,256]{1,0:T(8,128)(2,1)S(1)}, bf16[2048,256]{1,0:T(8,128)(2,1)}, u32[]{:S(2)}, u32[]{:S(2)}) collective-permute-start(bf16[2048,256]{1,0:T(8,128)(2,1)S(1)} %pad_maximum_fusion.own), channel_id=1, source_target_pairs={{0,4},{4,8},{8,12},{12,16},{16,20},{20,24},{24,28},{28,32},{32,36}... | collective-permute-start | bytes 3145736 | tf_op jit(solution)/shard_map/ppermute | solution.py:261
  31.4 20.1 %collective-permute-start.8 = (bf16[2048,256]{1,0:T(8,128)(2,1)S(1)}, bf16[2048,256]{1,0:T(8,128)(2,1)}, u32[]{:S(2)}, u32[]{:S(2)}) collective-permute-start(bf16[2048,256]{1,0:T(8,128)(2,1)S(1)} %pad_maximum_fusion.own), channel_id=1, source_target_pairs={{4,0},{8,4},{12,8},{16,12},{20,16},{24,20},{28,24},{32,28},{36,32}... | collective-permute-start | bytes 3145736 | tf_op jit(solution)/shard_map/ppermute | solution.py:262
  39.2 11.6 %collective-permute-start.4 = (bf16[2,4,128,128]{3,2,1,0:T(8,128)(2,1)}, bf16[2,4,128,128]{3,2,1,0:T(8,128)(2,1)S(1)}, u32[]{:S(2)}, u32[]{:S(2)}) collective-permute-start(bf16[2,4,128,128]{3,2,1,0:T(8,128)(2,1)} %slice.36), channel_id=1, source_target_pairs={{0,1},{1,2},{2,3},{3,0},{4,5},{5,6},{6,7},{7,4},{8,9},{9,10},{10,1... | collective-permute-start | bytes 786440 | tf_op jit(solution)/shard_map/ppermute | solution.py:220
  42.8 8.7 %collective-permute-start.6 = (bf16[2,4,128,128]{3,2,1,0:T(8,128)(2,1)}, bf16[2,4,128,128]{3,2,1,0:T(8,128)(2,1)}, u32[]{:S(2)}, u32[]{:S(2)}) collective-permute-start(bf16[2,4,128,128]{3,2,1,0:T(8,128)(2,1)} %slice.37), channel_id=1, source_target_pairs={{0,3},{1,0},{2,1},{3,2},{4,7},{5,4},{6,5},{7,6},{8,11},{9,8},{10,9... | collective-permute-start | bytes 786440 | tf_op jit(solution)/shard_map/ppermute | solution.py:220
  50.8 0.7 copy-start.2
  51.5 1.0 copy-start.3
  55.9 7.4 %collective-permute-start.9 = (f32[2,128,256]{2,1,0:T(8,128)S(1)}, f32[2,128,256]{2,1,0:T(8,128)S(1)}, u32[]{:S(2)}, u32[]{:S(2)}) collective-permute-start(f32[2,128,256]{2,1,0:T(8,128)S(1)} %get-tuple-element.9), channel_id=1, source_target_pairs={{0,4},{4,0},{8,12},{12,8},{16,20},{20,16},{24,28},{28,24},{32,36},... | collective-permute-start | bytes 786440 | tf_op jit(solution)/shard_map/ppermute | solution.py:225
  68.2 6.6 %collective-permute-start.10 = (f32[1,128,256]{2,1,0:T(8,128)S(1)}, f32[1,128,256]{2,1,0:T(8,128)S(1)}, u32[]{:S(2)}, u32[]{:S(2)}) collective-permute-start(f32[1,128,256]{2,1,0:T(8,128)S(1)} %get-tuple-element.10.refs_0_), channel_id=1, source_target_pairs={{0,8},{4,12},{8,0},{12,4},{16,24},{20,28},{24,16},{28,20},{32,40},... | collective-permute-start | bytes 393224 | tf_op jit(solution)/shard_map/ppermute | solution.py:225
  78.8 11.2 %collective-permute-start.11 = (f32[1,128,256]{2,1,0:T(8,128)S(1)}, f32[1,128,256]{2,1,0:T(8,128)S(1)}, u32[]{:S(2)}, u32[]{:S(2)}) collective-permute-start(f32[1,128,256]{2,1,0:T(8,128)S(1)} %shard_map.105.refs_0_.own), channel_id=1, source_target_pairs={{0,16},{4,20},{8,24},{12,28},{16,0},{20,4},{24,8},{28,12},{32,48},... | collective-permute-start | bytes 393224 | tf_op jit(solution)/shard_map/ppermute | solution.py:225
  94.7 0.9 copy-start.1

commit v3 on v2

v3 whole, which is shorter than its diff:
```python
import functools

import jax
import jax.numpy as jnp
from jax import lax
from jax.experimental import pallas as pl
from jax.experimental.pallas import tpu as pltpu
from jax.sharding import PartitionSpec as P

RIDGE = 0.25
BF = jnp.bfloat16
F32 = jnp.float32
PANEL = 16


def dot(a, b, ca, cb):
    return lax.dot_general(a, b, (((ca,), (cb,)), ((), ())), preferred_element_type=F32)


def split2(x):
    hi = x.astype(BF)
    lo = (x - hi.astype(F32)).astype(BF)
    return hi, lo


def split3(x):
    hi = x.astype(BF)
    rest = x - hi.astype(F32)
    mid = rest.astype(BF)
    lo = (rest - mid.astype(F32)).astype(BF)
    return hi, mid, lo


ANY = pl.BlockSpec(memory_space=pl.ANY)
VMEM = pl.BlockSpec(memory_space=pltpu.VMEM)
SMEM = pl.BlockSpec(memory_space=pltpu.SMEM)
ROOM = pltpu.CompilerParams(vmem_limit_bytes=16 << 20)


def run(copies):
    for copy in copies:
        copy.start()
    for copy in copies:
        copy.wait()


def block_kernel(info, samples, columns, out, wide, extra, sem):
    body = pltpu.make_async_copy(samples, out.at[pl.ds(0, 512)], sem.at[0])
    body.start()
    wide[...] = jnp.zeros((16, 256), F32)
    wide[0:4, 0:16] = jnp.clip(columns[...] - info[4], 0, 47).astype(F32)
    extra[...] = wide[...].astype(BF)
    tail = pltpu.make_async_copy(extra, out.at[pl.ds(512, 16)], sem.at[1])
    tail.start()
    body.wait()
    tail.wait()


def sample_block(info, samples, columns):
    return pl.pallas_call(
        block_kernel,
        out_shape=jax.ShapeDtypeStruct((528, 256), BF),
        in_specs=[SMEM, ANY, VMEM],
        out_specs=ANY,
        scratch_shapes=[
            pltpu.VMEM((16, 256), F32),
            pltpu.VMEM((16, 256), BF),
            pltpu.SemaphoreType.DMA((2,)),
        ],
        compiler_params=ROOM,
    )(info, samples, columns.T)


def pack_kernel(info, tiles, up, down, sem):
    one, two, three = ((info[0] + by) % 4 * 4 for by in (1, 2, 3))
    run(
        [
            pltpu.make_async_copy(tiles.at[pl.ds(one, 4)], up.at[pl.ds(0, 4)], sem.at[0]),
            pltpu.make_async_copy(tiles.at[pl.ds(two, 2)], up.at[pl.ds(4, 2)], sem.at[1]),
            pltpu.make_async_copy(tiles.at[pl.ds(three, 4)], down.at[pl.ds(0, 4)], sem.at[2]),
            pltpu.make_async_copy(tiles.at[pl.ds(two + 2, 2)], down.at[pl.ds(4, 2)], sem.at[3]),
        ]
    )


def packed_tiles(info, tiles):
    block = jax.ShapeDtypeStruct((6, 4, 128, 128), BF)
    return pl.pallas_call(
        pack_kernel,
        out_shape=(block, block),
        in_specs=[SMEM, ANY],
        out_specs=(ANY, ANY),
        scratch_shapes=[pltpu.SemaphoreType.DMA((4,))],
        compiler_params=ROOM,
    )(info, tiles)


def forward_kernel(up, down, up_out, down_out, sem):
    run(
        [
            pltpu.make_async_copy(up.at[pl.ds(4, 2)], up_out, sem.at[0]),
            pltpu.make_async_copy(down.at[pl.ds(4, 2)], down_out, sem.at[1]),
        ]
    )


def forwarded(up, down):
    block = jax.ShapeDtypeStruct((2, 4, 128, 128), BF)
    return pl.pallas_call(
        forward_kernel,
        out_shape=(block, block),
        in_specs=[ANY, ANY],
        out_specs=(ANY, ANY),
        scratch_shapes=[pltpu.SemaphoreType.DMA((2,))],
        compiler_params=ROOM,
    )(up, down)


def gather_kernel(*refs):
    parts, own, columns, ids, sem = refs[:4], *refs[4:]
    copies = [
        pltpu.make_async_copy(part.at[pl.ds(0, 512)], own.at[pl.ds(512 * i, 512)], sem.at[i])
        for i, part in enumerate(parts)
    ]
    small = [
        pltpu.make_async_copy(part.at[pl.ds(512, 16)], ids.at[i], sem.at[4 + i])
        for i, part in enumerate(parts)
    ]
    for copy in copies + small:
        copy.start()
    for copy in small:
        copy.wait()
    for i in range(4):
        columns[16 * i : 16 * (i + 1), :] = ids[i][:, 0:128].astype(F32).astype(jnp.int32)
    for copy in copies:
        copy.wait()


def gathered(blocks):
    return pl.pallas_call(
        gather_kernel,
        out_shape=(
            jax.ShapeDtypeStruct((2048, 256), BF),
            jax.ShapeDtypeStruct((64, 128), jnp.int32),
        ),
        in_specs=[ANY] * 4,
        out_specs=(ANY, VMEM),
        scratch_shapes=[pltpu.VMEM((4, 16, 256), BF), pltpu.SemaphoreType.DMA((8,))],
        compiler_params=ROOM,
    )(*blocks)


def near_kernel(
    info, cols, counts, own_tiles, tiles_a, tiles_b, tiles_c, tiles_d, before, own, after,
    send_ref, keep_ref, win, tiles, sem,
):
    x = info[0]
    even = info[1]
    late = info[2]
    windows = [
        pltpu.make_async_copy(own, win.at[pl.ds(2048, 2048)], sem.at[0]),
        pltpu.make_async_copy(before, win.at[pl.ds(0, 2048)], sem.at[1]),
        pltpu.make_async_copy(after, win.at[pl.ds(4096, 2048)], sem.at[2]),
    ]
    arrivals = [
        [pltpu.make_async_copy(own_tiles.at[pl.ds(x * 4, 4)], tiles.at[0], sem.at[3])],
        [pltpu.make_async_copy(tiles_a.at[pl.ds(0, 4)], tiles.at[1], sem.at[4])],
        [
            pltpu.make_async_copy(tiles_b, tiles.at[2, pl.ds(0, 2)], sem.at[5]),
            pltpu.make_async_copy(tiles_c, tiles.at[2, pl.ds(2, 2)], sem.at[6]),
        ],
        [pltpu.make_async_copy(tiles_d.at[pl.ds(0, 4)], tiles.at[3], sem.at[7])],
    ]
    for copy in windows + sum(arrivals, []):
        copy.start()
    for copy in windows:
        copy.wait()
    for q in range(4):
        keep, slot = divmod(q, 2)
        parity = even if keep == 1 else 1 - even
        k = parity + 2 * (late if slot == 1 else 1 - late)
        count = counts[x * 4 + k]
        total = jnp.zeros((128, 256), F32)
        for delta in range(4):
            if q == 0:
                for copy in arrivals[delta]:
                    copy.wait()
            source = (x + 4 - delta) % 4
            for s in range(0, 4, 2):
                pieces = []
                rows = []
                for t in (s, s + 1):
                    place = source * 4 + t
                    live = jnp.where(place < count, 1.0, 0.0).astype(F32)
                    piece = tiles[delta, k, t]
                    pieces.append(piece * jnp.full((128, 128), live, F32).astype(BF))
                    col = jnp.clip(cols[delta * 16 + t, x * 4 + k], 0, 47)
                    member = col & 15
                    col = (col - member) + ((x - (member >> 2)) & 3) * 4 + (member & 3)
                    rows.append(win[pl.ds(pl.multiple_of(col * 128, 128), 128), :])
                total = total + dot(
                    jnp.concatenate(pieces, axis=1), jnp.concatenate(rows, axis=0), 1, 0
                )
        if keep == 1:
            keep_ref[slot] = total
        else:
            send_ref[slot] = total


def near(info, cols, counts, own_tiles, received, before, own, after):
    block = jax.ShapeDtypeStruct((2, 128, 256), F32)
    return pl.pallas_call(
        near_kernel,
        out_shape=(block, block),
        in_specs=[SMEM] * 3 + [ANY] * 8,
        out_specs=(VMEM, VMEM),
        scratch_shapes=[
            pltpu.VMEM((6144, 256), BF),
            pltpu.VMEM((4, 4, 4, 128, 128), BF),
            pltpu.SemaphoreType.DMA((8,)),
        ],
        compiler_params=ROOM,
        cost_estimate=pl.CostEstimate(
            flops=540_000_000, bytes_accessed=6_000_000, transcendentals=0
        ),
    )(info, cols, counts, own_tiles, *received, before, own, after)


def eliminate(j, gram, rhs):
    base = j * PANEL
    half = PANEL // 2
    rows = lax.broadcasted_iota(jnp.int32, (half, 128), 0)
    a = [gram[base + half * h : base + half * (h + 1), :] for h in range(2)]
    body = [
        [a[h]] + [rhs[base + half * h : base + half * (h + 1), 128 * c : 128 * (c + 1)] for c in range(2)]
        for h in range(2)
    ]
    column = [
        [jnp.broadcast_to(a[h][:, base + k : base + k + 1], (half, 128)) for k in range(PANEL)]
        for h in range(2)
    ]
    scale = [jnp.zeros((half, 128), F32) for _ in range(2)]
    for i in range(PANEL):
        h0, r = divmod(i, half)
        pivot = column[h0][i][r : r + 1, :]
        inverse = lax.rsqrt(pivot)
        reciprocal = inverse * inverse
        scale[h0] = jnp.where(rows == r, jnp.broadcast_to(inverse, (half, 128)), scale[h0])
        factor = {}
        for h in range(h0, 2):
            value = column[h][i] * reciprocal
            factor[h] = jnp.where(rows > r, value, 0.0) if h == h0 else value
        for k in range(i + 1, PANEL):
            row = column[h0][k][r : r + 1, :]
            for h in range(h0, 2):
                column[h][k] = column[h][k] - factor[h] * row
        for c in range(3):
            row = body[h0][c][r : r + 1, :]
            for h in range(h0, 2):
                body[h][c] = body[h][c] - factor[h] * row
    return jnp.concatenate(
        [jnp.concatenate([body[h][c] * scale[h] for c in range(3)], axis=1) for h in range(2)],
        axis=0,
    )


def put_transfer(out, place, side, own, other, basis):
    zh, zl = split2(basis)
    right = jnp.concatenate([zh, zl, zh], axis=1)
    for part, at in ((own, side), (other, 1 - side)):
        ch, cl = split2(part)
        value = dot(jnp.concatenate([ch, ch, cl], axis=1), right, 1, 1) * (1.0 / 256)
        out[0, place, pl.ds(pl.multiple_of(at * 128, 128), 128), :] = value


def merge_kernel(m, last, info, own, other, choice, out, *refs):
    gram = refs[-1]
    wide = [jnp.concatenate(pair, axis=0) for pair in zip(split3(own[m]), split3(other[m]))]
    hi, mid, lo = (dot(choice[m], part, 1, 0) for part in wide)
    out[0] = hi + (mid + lo)
    hi = hi.astype(BF)
    mid = mid.astype(BF)
    product = dot(
        jnp.concatenate([hi, hi, mid], axis=1), jnp.concatenate([hi, mid, hi], axis=1), 1, 1
    )
    on = lax.broadcasted_iota(jnp.int32, (128, 128), 0) == lax.broadcasted_iota(
        jnp.int32, (128, 128), 1
    )
    gram[...] = product * (1.0 / 256) + jnp.where(on, RIDGE, 0.0)
    for j in range(128 // PANEL):
        done = (j + 1) * PANEL
        rows = eliminate(j, gram, out.at[0])
        out[0, j * PANEL : done, :] = rows[:, 128:]
        if done < 128:
            hi, mid, lo = split3(rows)
            left = jnp.concatenate([hi, hi, mid, mid, hi, lo], axis=0)[:, :128]
            right = jnp.concatenate([hi, mid, hi, mid, lo, hi], axis=0)
            update = dot(left, right, 0, 0)
            gram[done:, :] = gram[done:, :] - update[done:, :128]
            out[0, done:, :] = out[0, done:, :] - update[done:, 128:]
    if last:
        put_transfer(refs[0], 0, info[3], own[m], other[m], out[0])


def merge(info, own, other, choice, m=0, last=False):
    shapes = [jax.ShapeDtypeStruct((1, 128, 256), F32)]
    if last:
        shapes.append(jax.ShapeDtypeStruct((1, 1, 256, 128), F32))
    return pl.pallas_call(
        functools.partial(merge_kernel, m, last),
        out_shape=tuple(shapes),
        in_specs=[SMEM] + [VMEM] * 3,
        out_specs=(VMEM,) * len(shapes),
        scratch_shapes=[pltpu.VMEM((128, 128), F32)],
        compiler_params=pltpu.CompilerParams(vmem_limit_bytes=24 << 20),
        cost_estimate=pl.CostEstimate(
            flops=4_000_000_000, bytes_accessed=600_000, transcendentals=0
        ),
    )(info, own, other, choice)


def transfer_kernel(nodes, info, own, other, *refs):
    basis, out = refs[:nodes], refs[nodes]
    for m in range(nodes):
        place = 0 if nodes == 1 else (info[2] if m == 1 else 1 - info[2])
        put_transfer(out, place, info[3], own[m], other[m], basis[m][0])


def transfer(info, own, other, basis):
    nodes = len(basis)
    return pl.pallas_call(
        functools.partial(transfer_kernel, nodes),
        out_shape=jax.ShapeDtypeStruct((1, nodes, 256, 128), F32),
        in_specs=[SMEM] + [VMEM] * (2 + nodes),
        out_specs=VMEM,
        compiler_params=pltpu.CompilerParams(vmem_limit_bytes=24 << 20),
        cost_estimate=pl.CostEstimate(
            flops=nodes * 50_000_000, bytes_accessed=nodes * 600_000, transcendentals=0
        ),
    )(info, own, other, *basis)


def shifted(value, axis, by):
    count = lax.axis_size(axis)
    return lax.ppermute(value, axis, [(i, (i + by) % count) for i in range(count)])


def swapped(value, apart):
    count = lax.axis_size("leaf")
    return lax.ppermute(value, "leaf", [(i, i ^ apart) for i in range(count)])


def one_hot(skeleton, group, members, side):
    chosen = lax.dynamic_slice_in_dim(skeleton, group, 1, axis=1)[:, 0]
    chosen = jnp.concatenate(
        [lax.dynamic_slice_in_dim(chosen, k, 1, axis=0) for k in members], axis=0
    )
    target = chosen + 128 * side - 256 * side * (chosen >= 128)
    return (target[:, :, None] == lax.broadcasted_iota(jnp.int32, (1, 1, 256), 2)).astype(BF)


def local(samples, near_tiles, columns, tile_count, skeleton_one, skeleton_two, skeleton_three):
    d = lax.axis_index("leaf")
    x = lax.axis_index("cols")
    b0, b1, b2 = d & 1, (d >> 1) & 1, (d >> 2) & 1
    infos = [
        jnp.stack([x, b0, b1, side, (d - 1) * 16]).astype(jnp.int32) for side in (b0, b1, b2)
    ]

    block = sample_block(infos[0], samples, columns)
    by_one, by_three, by_two = (shifted(block, "cols", by) for by in (1, 3, 2))
    up, down = packed_tiles(infos[0], near_tiles)
    far_up = shifted(up, "cols", 1)
    far_down = shifted(down, "cols", 3)
    next_up, next_down = forwarded(far_up, far_down)
    received = [far_up, shifted(next_up, "cols", 1), shifted(next_down, "cols", 3), far_down]
    own, cols = gathered([block, by_one, by_two, by_three])
    leaves = lax.axis_size("leaf")
    rising = [(i, i + 1) for i in range(leaves - 1)]
    before = lax.ppermute(own, "leaf", rising)
    after = lax.ppermute(own, "leaf", [(j, i) for i, j in rising])

    choice_one = one_hot(skeleton_one, d >> 1, (b0 + 2 - 2 * b1, b0 + 2 * b1), b0)
    choice_two = one_hot(skeleton_two, d >> 2, (d & 3,), b1)
    choice_three = one_hot(skeleton_three, d >> 3, (d & 3,), b2)

    send, keep = near(
        infos[0], cols, tile_count, near_tiles, received, before, own, after
    )
    other = swapped(send, 1)
    (away,) = merge(infos[0], keep, other, choice_one, 0)
    arrived = swapped(away, 2)
    (basis,) = merge(infos[0], keep, other, choice_one, 1)
    out_one = transfer(infos[0], keep, other, (away, basis))
    (basis_two,) = merge(infos[1], basis, arrived, choice_two)
    arrived_two = swapped(basis_two, 4)
    out_two = transfer(infos[1], basis, arrived, (basis_two,))
    top, out_three = merge(infos[2], basis_two, arrived_two, choice_three, last=True)
    return out_one, out_two, out_three, top[None]


def solution(mesh):
    placed = (
        P(("leaf", "cols"), None),
        P("leaf", "cols", None, None),
        P("leaf", "cols"),
        P("leaf"),
        P("cols", None, None),
        P("cols", None, None),
        P("cols", None, None),
    )
    return jax.shard_map(
        local,
        mesh=mesh,
        in_specs=placed,
        out_specs=(P("leaf", "cols", None, None),) * 4,
        check_vma=False,
    )
```

time: 98.6 us -> 109 us (1.11); the launches traced: 97.1 us -> 109 us
  Pallas kernels: 21.6 us -> 39.3 us
  local copies, waits for them, and re-layouts: 13 us -> 5.84 us
  starting transfers between devices: 47.6 us -> 52.8 us
  other arithmetic: 4.9 us -> 1.69 us
    pallas_call x4 -> x9, Pallas kernels: 17 us -> 36.2 us  [the longest x4 19.1 us: merge(): pl.pallas_call(functools.partial(merge_kernel, m, last), out_shape=tuple(...]
    slice x11 -> x0, local copies, waits for them, and re-layouts: 5.72 us -> none  [the longest x6 2.32 us: local(): cols = jnp.stack([part[512:, :4] for part in blocks])]
    ppermute x3, starting transfers between devices: 14.1 us -> 18.8 us  [swapped(): return lax.ppermute(value, 'leaf', [(i, i ^ apart) for i in range(count)])]
    concatenate x4 -> x0, other arithmetic: 2.97 us -> none  [the longest x1 0.98 us: local(): jnp.concatenate([tiles_of(3, 0, 4), tiles_of(2, 2, 2)])]
    ppermute x3, waiting for transfers between devices: 6.31 us -> 3.79 us  [swapped(): return lax.ppermute(value, 'leaf', [(i, i ^ apart) for i in range(count)])]
    ppermute x7, waiting for transfers between devices: 2.7 us -> 4.33 us  [shifted(): lax.ppermute(value, axis, [(i, (i + by) % count) for i in range(count)])]
    pallas_call x3 -> x2, Pallas kernels: 4.55 us -> 3.08 us  [transfer(): pl.pallas_call(functools.partial(transfer_kernel, nodes), out_shape=jax.S...]
    dynamic_slice x3 -> x0, local copies, waits for them, and re-layouts: 1.39 us -> none  [the longest x2 1.32 us: tiles_of(): lax.dynamic_slice_in_dim(near_tiles, (x + by) % 4 * 4 + start, size, axis=0)]
  transfers between devices with their start and end apart: 12 -> 12, of which waited for: 4 -> 5; matrix products, arithmetic and copies ran while one was open for 12% -> 2% of each run, Pallas kernels for 3% -> 18%
where the time goes in v3:
time: 109 us
  starting transfers between devices  52.8 us (48%)
  Pallas kernels  39.3 us (36%)
  waiting for transfers between devices  8.12 us (7%)
  local copies, waits for them, and re-layouts  5.84 us (5%)
  other arithmetic  1.69 us (2%)
    ppermute x7, starting transfers between devices, shifted(): lax.ppermute(value, axis, [(i, (i + by) % count) for i in range(count)])  24.9 us
    pallas_call x4, Pallas kernels, merge(): pl.pallas_call(functools.partial(merge_kernel, m, last), out_shape=tuple(...  19.1 us
    ppermute x3, starting transfers between devices, swapped(): return lax.ppermute(value, 'leaf', [(i, i ^ apart) for i in range(count)])  18.8 us
    pallas_call x1, Pallas kernels, forwarded(): pl.pallas_call(forward_kernel, out_shape=(block, block), in_specs=[ANY, A...  9.06 us
    ppermute x1, starting transfers between devices, local(): before = lax.ppermute(own, 'leaf', rising)  5.96 us
    unnamed x16, local copies, waits for them, and re-layouts  4.87 us
    pallas_call x1, Pallas kernels, near(): pl.pallas_call(near_kernel, out_shape=(block, block), in_specs=[SMEM] * 3...  4.58 us
    ppermute x7, waiting for transfers between devices, shifted(): lax.ppermute(value, axis, [(i, (i + by) % count) for i in range(count)])  4.33 us
  transfers between devices with their start and end apart: 12, of which 5 were waited for; matrix products, arithmetic and copies ran while one was open for 2% of the time, Pallas kernels for 18%

profile of v3, /device:TPU:1, one launch (start us, length us, event | category | flops | bytes accessed | tf_op | source)
XLA Modules:
  0.0 108.7 jit_solution(4909372076941840188)
XLA Ops:
  3.0 3.9 %collective-permute-start = (bf16[528,256]{1,0:T(8,128)(2,1)S(1)}, bf16[528,256]{1,0:T(8,128)(2,1)S(1)}, u32[]{:S(2)}, u32[]{:S(2)}) collective-permute-start(bf16[528,256]{1,0:T(8,128)(2,1)S(1)} %shard_map.102.refs_0_), channel_id=1, source_target_pairs={{0,1},{1,2},{2,3},{3,0},{4,5},{5,6},{6,7},{7,4},{8,9},{9,10},{10,1... | collective-permute-start | bytes 811016 | tf_op jit(solution)/shard_map/ppermute | solution.py:345
  6.9 4.4 %collective-permute-start.1 = (bf16[528,256]{1,0:T(8,128)(2,1)S(1)}, bf16[528,256]{1,0:T(8,128)(2,1)S(1)}, u32[]{:S(2)}, u32[]{:S(2)}) collective-permute-start(bf16[528,256]{1,0:T(8,128)(2,1)S(1)} %shard_map.102.refs_0_), channel_id=1, source_target_pairs={{0,2},{1,3},{2,0},{3,1},{4,6},{5,7},{6,4},{7,5},{8,10},{9,11},{10,... | collective-permute-start | bytes 811016 | tf_op jit(solution)/shard_map/ppermute | solution.py:345
  11.3 3.1 %collective-permute-start.2 = (bf16[528,256]{1,0:T(8,128)(2,1)S(1)}, bf16[528,256]{1,0:T(8,128)(2,1)S(1)}, u32[]{:S(2)}, u32[]{:S(2)}) collective-permute-start(bf16[528,256]{1,0:T(8,128)(2,1)S(1)} %shard_map.102.refs_0_), channel_id=1, source_target_pairs={{0,3},{1,0},{2,1},{3,2},{4,7},{5,4},{6,5},{7,6},{8,11},{9,8},{10,9... | collective-permute-start | bytes 811016 | tf_op jit(solution)/shard_map/ppermute | solution.py:345
  14.4 1.6 %copy-done = bf16[16,4,128,128]{3,2,1,0:T(8,128)(2,1)S(1)} copy-done((bf16[16,4,128,128]{3,2,1,0:T(8,128)(2,1)S(1)}, bf16[16,4,128,128]{3,2,1,0:T(8,128)(2,1)}, u32[]{:S(2)}) %copy-start) | copy-done | bytes 2097176
  16.0 1.8 %shard_map.104 = (bf16[6,4,128,128]{3,2,1,0:T(8,128)(2,1)}, bf16[6,4,128,128]{3,2,1,0:T(8,128)(2,1)}) custom-call(s32[5]{0:T(128)S(1)} %stack.38.info, bf16[16,4,128,128]{3,2,1,0:T(8,128)(2,1)S(1)} %copy-done), custom_call_target="tpu_custom_call" | custom-call | tf_op jit(solution)/shard_map/pallas_call | solution.py:88
  17.7 2.2 %collective-permute-start.3 = (bf16[6,4,128,128]{3,2,1,0:T(8,128)(2,1)}, bf16[6,4,128,128]{3,2,1,0:T(8,128)(2,1)S(1)}, u32[]{:S(2)}, u32[]{:S(2)}) collective-permute-start(bf16[6,4,128,128]{3,2,1,0:T(8,128)(2,1)} %get-tuple-element.15), channel_id=1, source_target_pairs={{0,1},{1,2},{2,3},{3,0},{4,5},{5,6},{6,7},{7,4},{8,9},{9,10},{10,1... | collective-permute-start | bytes 2359304 | tf_op jit(solution)/shard_map/ppermute | solution.py:345
  20.0 4.3 %collective-permute-start.4 = (bf16[6,4,128,128]{3,2,1,0:T(8,128)(2,1)}, bf16[6,4,128,128]{3,2,1,0:T(8,128)(2,1)}, u32[]{:S(2)}, u32[]{:S(2)}) collective-permute-start(bf16[6,4,128,128]{3,2,1,0:T(8,128)(2,1)} %get-tuple-element.16), channel_id=1, source_target_pairs={{0,3},{1,0},{2,1},{3,2},{4,7},{5,4},{6,5},{7,6},{8,11},{9,8},{10,9... | collective-permute-start | bytes 2359304 | tf_op jit(solution)/shard_map/ppermute | solution.py:345
  25.4 6.0 %collective-permute-start.7 = (bf16[2048,256]{1,0:T(8,128)(2,1)}, bf16[2048,256]{1,0:T(8,128)(2,1)}, u32[]{:S(2)}, u32[]{:S(2)}) collective-permute-start(bf16[2048,256]{1,0:T(8,128)(2,1)} %get-tuple-element.19.own), channel_id=1, source_target_pairs={{0,4},{4,8},{8,12},{12,16},{16,20},{20,24},{24,28},{28,32},{32,36}... | collective-permute-start | bytes 3145736 | tf_op jit(solution)/shard_map/ppermute | solution.py:380
  31.3 3.2 %collective-permute-start.8 = (bf16[2048,256]{1,0:T(8,128)(2,1)}, bf16[2048,256]{1,0:T(8,128)(2,1)}, u32[]{:S(2)}, u32[]{:S(2)}) collective-permute-start(bf16[2048,256]{1,0:T(8,128)(2,1)} %get-tuple-element.19.own), channel_id=1, source_target_pairs={{4,0},{8,4},{12,8},{16,12},{20,16},{24,20},{28,24},{32,28},{36,32}... | collective-permute-start | bytes 3145736 | tf_op jit(solution)/shard_map/ppermute | solution.py:381
  35.3 1.5 %collective-permute-done.3.up.tiles_a = bf16[6,4,128,128]{3,2,1,0:T(8,128)(2,1)S(1)} collective-permute-done((bf16[6,4,128,128]{3,2,1,0:T(8,128)(2,1)}, bf16[6,4,128,128]{3,2,1,0:T(8,128)(2,1)S(1)}, u32[]{:S(2)}, u32[]{:S(2)}) %collective-permute-start.3) | collective-permute-done | bytes 786464 | tf_op jit(solution)/shard_map/ppermute | solution.py:345
  36.8 9.1 %shard_map.105 = (bf16[2,4,128,128]{3,2,1,0:T(8,128)(2,1)}, bf16[2,4,128,128]{3,2,1,0:T(8,128)(2,1)}) custom-call(bf16[6,4,128,128]{3,2,1,0:T(8,128)(2,1)S(1)} %collective-permute-done.3.up.tiles_a, bf16[6,4,128,128]{3,2,1,0:T(8,128)(2,1)} %collective-permute-done.4.down.tiles_d), custom_call_target="tpu_custom_call" | custom-call | tf_op jit(solution)/shard_map/pallas_call | solution.py:109
  45.9 1.9 %collective-permute-start.5 = (bf16[2,4,128,128]{3,2,1,0:T(8,128)(2,1)}, bf16[2,4,128,128]{3,2,1,0:T(8,128)(2,1)S(1)}, u32[]{:S(2)}, u32[]{:S(2)}) collective-permute-start(bf16[2,4,128,128]{3,2,1,0:T(8,128)(2,1)} %get-tuple-element.17), channel_id=1, source_target_pairs={{0,1},{1,2},{2,3},{3,0},{4,5},{5,6},{6,7},{7,4},{8,9},{9,10},{10,1... | collective-permute-start | bytes 786440 | tf_op jit(solution)/shard_map/ppermute | solution.py:345
  47.8 5.1 %collective-permute-start.6 = (bf16[2,4,128,128]{3,2,1,0:T(8,128)(2,1)}, bf16[2,4,128,128]{3,2,1,0:T(8,128)(2,1)S(1)}, u32[]{:S(2)}, u32[]{:S(2)}) collective-permute-start(bf16[2,4,128,128]{3,2,1,0:T(8,128)(2,1)} %get-tuple-element.18), channel_id=1, source_target_pairs={{0,3},{1,0},{2,1},{3,2},{4,7},{5,4},{6,5},{7,6},{8,11},{9,8},{10,9... | collective-permute-start | bytes 786440 | tf_op jit(solution)/shard_map/ppermute | solution.py:345
  55.0 1.6 %collective-permute-done.6.tiles_c = bf16[2,4,128,128]{3,2,1,0:T(8,128)(2,1)S(1)} collective-permute-done((bf16[2,4,128,128]{3,2,1,0:T(8,128)(2,1)}, bf16[2,4,128,128]{3,2,1,0:T(8,128)(2,1)S(1)}, u32[]{:S(2)}, u32[]{:S(2)}) %collective-permute-start.6) | collective-permute-done | bytes 262176 | tf_op jit(solution)/shard_map/ppermute | solution.py:345
  56.6 4.6 %shard_map.106 = (f32[2,128,256]{2,1,0:T(8,128)}, f32[2,128,256]{2,1,0:T(8,128)S(1)}) custom-call(s32[5]{0:T(128)S(1)} %stack.38.info, s32[64,128]{1,0:T(8,128)S(1)} %get-tuple-element.14.cols, s32[16]{0:T(128)S(1)} %copy-done.7, bf16[16,4,128,128]{3,2,1,0:T(8,128)(2,1)S(1)} %copy-done.1, bf16[6,4,128,128]{3,2,1,0:T(8,128)(2,1)S(1)} %collective-permute-done.3.up.tiles_a, ...), custom_call_target="tpu_custom_call" | custom-call | flops 540000000 | bytes 6000000 | tf_op jit(solution)/shard_map/pallas_call | solution.py:212
  61.9 8.4 %collective-permute-start.9 = (f32[2,128,256]{2,1,0:T(8,128)}, f32[2,128,256]{2,1,0:T(8,128)S(1)}, u32[]{:S(2)}, u32[]{:S(2)}) collective-permute-start(f32[2,128,256]{2,1,0:T(8,128)} %get-tuple-element.21), channel_id=1, source_target_pairs={{0,4},{4,0},{8,12},{12,8},{16,20},{20,16},{24,28},{28,24},{32,36},... | collective-permute-start | bytes 786440 | tf_op jit(solution)/shard_map/ppermute | solution.py:350
  72.6 4.5 %shard_map.107.refs_0_ = f32[1,128,256]{2,1,0:T(8,128)S(1)} custom-call(s32[5]{0:T(128)S(1)} %stack.38.info, f32[2,128,256]{2,1,0:T(8,128)S(1)} %copy-done.4, f32[2,128,256]{2,1,0:T(8,128)S(1)} %collective-permute-done.9.other, bf16[2,128,256]{2,1,0:T(8,128)(2,1)S(1)} %fusion.choice), custom_call_target="tpu_custom_call" | custom-call | flops 4000000000 | bytes 600000 | tf_op jit(solution)/shard_map/pallas_call | solution.py:309
  77.1 4.5 %collective-permute-start.10 = (f32[1,128,256]{2,1,0:T(8,128)S(1)}, f32[1,128,256]{2,1,0:T(8,128)S(1)}, u32[]{:S(2)}, u32[]{:S(2)}) collective-permute-start(f32[1,128,256]{2,1,0:T(8,128)S(1)} %shard_map.107.refs_0_), channel_id=1, source_target_pairs={{0,8},{4,12},{8,0},{12,4},{16,24},{20,28},{24,16},{28,20},{32,40},... | collective-permute-start | bytes 393224 | tf_op jit(solution)/shard_map/ppermute | solution.py:350
  81.7 4.5 %shard_map.108.refs_1_.own = f32[1,128,256]{2,1,0:T(8,128)S(1)} custom-call(s32[5]{0:T(128)S(1)} %stack.38.info, f32[2,128,256]{2,1,0:T(8,128)S(1)} %copy-done.4, f32[2,128,256]{2,1,0:T(8,128)S(1)} %collective-permute-done.9.other, bf16[2,128,256]{2,1,0:T(8,128)(2,1)S(1)} %fusion.choice), custom_call_target="tpu_custom_call" | custom-call | flops 4000000000 | bytes 600000 | tf_op jit(solution)/shard_map/pallas_call | solution.py:309
  86.2 4.5 %shard_map.110.refs_0_.own = f32[1,128,256]{2,1,0:T(8,128)S(1)} custom-call(s32[5]{0:T(128)S(1)} %stack.39.info, f32[1,128,256]{2,1,0:T(8,128)S(1)} %shard_map.108.refs_1_.own, f32[1,128,256]{2,1,0:T(8,128)S(1)} %collective-permute-done.10.other, bf16[1,128,256]{2,1,0:T(8,128)(2,1)S(1)} %fusion.1.choice), custom_call_target="tpu_custom_call" | custom-call | flops 4000000000 | bytes 600000 | tf_op jit(solution)/shard_map/pallas_call | solution.py:309
  90.8 5.8 %collective-permute-start.11 = (f32[1,128,256]{2,1,0:T(8,128)S(1)}, f32[1,128,256]{2,1,0:T(8,128)S(1)}, u32[]{:S(2)}, u32[]{:S(2)}) collective-permute-start(f32[1,128,256]{2,1,0:T(8,128)S(1)} %shard_map.110.refs_0_.own), channel_id=1, source_target_pairs={{0,16},{4,20},{8,24},{12,28},{16,0},{20,4},{24,8},{28,12},{32,48},... | collective-permute-start | bytes 393224 | tf_op jit(solution)/shard_map/ppermute | solution.py:350
  96.7 1.6 %shard_map.109 = f32[1,2,256,128]{3,2,1,0:T(8,128)} custom-call(s32[5]{0:T(128)S(1)} %stack.38.info, f32[2,128,256]{2,1,0:T(8,128)S(1)} %copy-done.5, f32[2,128,256]{2,1,0:T(8,128)S(1)} %collective-permute-done.9.other, f32[1,128,256]{2,1,0:T(8,128)S(1)} %shard_map.107.refs_0_, f32[1,128,256]{2,1,0:T(8,128)S(1)} %shard_map.108.refs_1_.own), custom_call_target="tpu_custom_call" | custom-call | flops 100000000 | bytes 1200000 | tf_op jit(solution)/shard_map/pallas_call | solution.py:331
  99.8 3.4 %collective-permute-done.11.other = f32[1,128,256]{2,1,0:T(8,128)S(1)} collective-permute-done((f32[1,128,256]{2,1,0:T(8,128)S(1)}, f32[1,128,256]{2,1,0:T(8,128)S(1)}, u32[]{:S(2)}, u32[]{:S(2)}) %collective-permute-start.11) | collective-permute-done | bytes 131104 | tf_op jit(solution)/shard_map/ppermute | solution.py:350
  103.2 5.5 %shard_map.112 = (f32[1,128,256]{2,1,0:T(8,128)}, f32[1,1,256,128]{3,2,1,0:T(8,128)}) custom-call(s32[5]{0:T(128)S(1)} %stack.41.info, f32[1,128,256]{2,1,0:T(8,128)S(1)} %shard_map.110.refs_0_.own, f32[1,128,256]{2,1,0:T(8,128)S(1)} %collective-permute-done.11.other, bf16[1,128,256]{2,1,0:T(8,128)(2,1)S(1)} %fusion.2.choice), custom_call_target="tpu_custom_call" | custom-call | flops 4000000000 | bytes 600000 | tf_op jit(solution)/shard_map/pallas_call | solution.py:309
  (37 shorter events, 10.7 us)
Async XLA Ops:
  0.7 1.0 copy-start.2
  1.7 0.7 copy-start.6
  2.4 54.2 %copy-start.7 = (s32[16]{0:T(128)S(1)}, s32[16]{0:T(128)}, u32[]{:S(2)}) copy-start(s32[16]{0:T(128)} %counts.1) | copy-start | bytes 196
  3.0 21.3 %collective-permute-start = (bf16[528,256]{1,0:T(8,128)(2,1)S(1)}, bf16[528,256]{1,0:T(8,128)(2,1)S(1)}, u32[]{:S(2)}, u32[]{:S(2)}) collective-permute-start(bf16[528,256]{1,0:T(8,128)(2,1)S(1)} %shard_map.102.refs_0_), channel_id=1, source_target_pairs={{0,1},{1,2},{2,3},{3,0},{4,5},{5,6},{6,7},{7,4},{8,9},{9,10},{10,1... | collective-permute-start | bytes 811016 | tf_op jit(solution)/shard_map/ppermute | solution.py:345
  6.9 17.3 %collective-permute-start.1 = (bf16[528,256]{1,0:T(8,128)(2,1)S(1)}, bf16[528,256]{1,0:T(8,128)(2,1)S(1)}, u32[]{:S(2)}, u32[]{:S(2)}) collective-permute-start(bf16[528,256]{1,0:T(8,128)(2,1)S(1)} %shard_map.102.refs_0_), channel_id=1, source_target_pairs={{0,2},{1,3},{2,0},{3,1},{4,6},{5,7},{6,4},{7,5},{8,10},{9,11},{10,... | collective-permute-start | bytes 811016 | tf_op jit(solution)/shard_map/ppermute | solution.py:345
  11.3 13.0 %collective-permute-start.2 = (bf16[528,256]{1,0:T(8,128)(2,1)S(1)}, bf16[528,256]{1,0:T(8,128)(2,1)S(1)}, u32[]{:S(2)}, u32[]{:S(2)}) collective-permute-start(bf16[528,256]{1,0:T(8,128)(2,1)S(1)} %shard_map.102.refs_0_), channel_id=1, source_target_pairs={{0,3},{1,0},{2,1},{3,2},{4,7},{5,4},{6,5},{7,6},{8,11},{9,8},{10,9... | collective-permute-start | bytes 811016 | tf_op jit(solution)/shard_map/ppermute | solution.py:345
  14.4 1.6 %copy-start = (bf16[16,4,128,128]{3,2,1,0:T(8,128)(2,1)S(1)}, bf16[16,4,128,128]{3,2,1,0:T(8,128)(2,1)}, u32[]{:S(2)}) copy-start(bf16[16,4,128,128]{3,2,1,0:T(8,128)(2,1)} %own_tiles.1) | copy-start | bytes 6291460
  16.0 40.6 %copy-start.1 = (bf16[16,4,128,128]{3,2,1,0:T(8,128)(2,1)S(1)}, bf16[16,4,128,128]{3,2,1,0:T(8,128)(2,1)}, u32[]{:S(2)}) copy-start(bf16[16,4,128,128]{3,2,1,0:T(8,128)(2,1)} %own_tiles.1) | copy-start | bytes 6291460
  17.7 19.1 %collective-permute-start.3 = (bf16[6,4,128,128]{3,2,1,0:T(8,128)(2,1)}, bf16[6,4,128,128]{3,2,1,0:T(8,128)(2,1)S(1)}, u32[]{:S(2)}, u32[]{:S(2)}) collective-permute-start(bf16[6,4,128,128]{3,2,1,0:T(8,128)(2,1)} %get-tuple-element.15), channel_id=1, source_target_pairs={{0,1},{1,2},{2,3},{3,0},{4,5},{5,6},{6,7},{7,4},{8,9},{9,10},{10,1... | collective-permute-start | bytes 2359304 | tf_op jit(solution)/shard_map/ppermute | solution.py:345
  20.0 16.9 %collective-permute-start.4 = (bf16[6,4,128,128]{3,2,1,0:T(8,128)(2,1)}, bf16[6,4,128,128]{3,2,1,0:T(8,128)(2,1)}, u32[]{:S(2)}, u32[]{:S(2)}) collective-permute-start(bf16[6,4,128,128]{3,2,1,0:T(8,128)(2,1)} %get-tuple-element.16), channel_id=1, source_target_pairs={{0,3},{1,0},{2,1},{3,2},{4,7},{5,4},{6,5},{7,6},{8,11},{9,8},{10,9... | collective-permute-start | bytes 2359304 | tf_op jit(solution)/shard_map/ppermute | solution.py:345
  25.4 31.2 %collective-permute-start.7 = (bf16[2048,256]{1,0:T(8,128)(2,1)}, bf16[2048,256]{1,0:T(8,128)(2,1)}, u32[]{:S(2)}, u32[]{:S(2)}) collective-permute-start(bf16[2048,256]{1,0:T(8,128)(2,1)} %get-tuple-element.19.own), channel_id=1, source_target_pairs={{0,4},{4,8},{8,12},{12,16},{16,20},{20,24},{24,28},{28,32},{32,36}... | collective-permute-start | bytes 3145736 | tf_op jit(solution)/shard_map/ppermute | solution.py:380
  31.3 25.2 %collective-permute-start.8 = (bf16[2048,256]{1,0:T(8,128)(2,1)}, bf16[2048,256]{1,0:T(8,128)(2,1)}, u32[]{:S(2)}, u32[]{:S(2)}) collective-permute-start(bf16[2048,256]{1,0:T(8,128)(2,1)} %get-tuple-element.19.own), channel_id=1, source_target_pairs={{4,0},{8,4},{12,8},{16,12},{20,16},{24,20},{28,24},{32,28},{36,32}... | collective-permute-start | bytes 3145736 | tf_op jit(solution)/shard_map/ppermute | solution.py:381
  45.9 9.1 %collective-permute-start.5 = (bf16[2,4,128,128]{3,2,1,0:T(8,128)(2,1)}, bf16[2,4,128,128]{3,2,1,0:T(8,128)(2,1)S(1)}, u32[]{:S(2)}, u32[]{:S(2)}) collective-permute-start(bf16[2,4,128,128]{3,2,1,0:T(8,128)(2,1)} %get-tuple-element.17), channel_id=1, source_target_pairs={{0,1},{1,2},{2,3},{3,0},{4,5},{5,6},{6,7},{7,4},{8,9},{9,10},{10,1... | collective-permute-start | bytes 786440 | tf_op jit(solution)/shard_map/ppermute | solution.py:345
  47.8 8.7 %collective-permute-start.6 = (bf16[2,4,128,128]{3,2,1,0:T(8,128)(2,1)}, bf16[2,4,128,128]{3,2,1,0:T(8,128)(2,1)S(1)}, u32[]{:S(2)}, u32[]{:S(2)}) collective-permute-start(bf16[2,4,128,128]{3,2,1,0:T(8,128)(2,1)} %get-tuple-element.18), channel_id=1, source_target_pairs={{0,3},{1,0},{2,1},{3,2},{4,7},{5,4},{6,5},{7,6},{8,11},{9,8},{10,9... | collective-permute-start | bytes 786440 | tf_op jit(solution)/shard_map/ppermute | solution.py:345
  61.1 0.7 copy-start.3
  61.9 9.8 %collective-permute-start.9 = (f32[2,128,256]{2,1,0:T(8,128)}, f32[2,128,256]{2,1,0:T(8,128)S(1)}, u32[]{:S(2)}, u32[]{:S(2)}) collective-permute-start(f32[2,128,256]{2,1,0:T(8,128)} %get-tuple-element.21), channel_id=1, source_target_pairs={{0,4},{4,0},{8,12},{12,8},{16,20},{20,16},{24,28},{28,24},{32,36},... | collective-permute-start | bytes 786440 | tf_op jit(solution)/shard_map/ppermute | solution.py:350
  71.6 0.9 copy-start.4
  77.1 9.1 %collective-permute-start.10 = (f32[1,128,256]{2,1,0:T(8,128)S(1)}, f32[1,128,256]{2,1,0:T(8,128)S(1)}, u32[]{:S(2)}, u32[]{:S(2)}) collective-permute-start(f32[1,128,256]{2,1,0:T(8,128)S(1)} %shard_map.107.refs_0_), channel_id=1, source_target_pairs={{0,8},{4,12},{8,0},{12,4},{16,24},{20,28},{24,16},{28,20},{32,40},... | collective-permute-start | bytes 393224 | tf_op jit(solution)/shard_map/ppermute | solution.py:350
  86.2 10.5 %copy-start.5 = (f32[2,128,256]{2,1,0:T(8,128)S(1)}, f32[2,128,256]{2,1,0:T(8,128)}, u32[]{:S(2)}) copy-start(f32[2,128,256]{2,1,0:T(8,128)} %copy-done.3) | copy-start | bytes 786436
  90.8 12.4 %collective-permute-start.11 = (f32[1,128,256]{2,1,0:T(8,128)S(1)}, f32[1,128,256]{2,1,0:T(8,128)S(1)}, u32[]{:S(2)}, u32[]{:S(2)}) collective-permute-start(f32[1,128,256]{2,1,0:T(8,128)S(1)} %shard_map.110.refs_0_.own), channel_id=1, source_target_pairs={{0,16},{4,20},{8,24},{12,28},{16,0},{20,4},{24,8},{28,12},{32,48},... | collective-permute-start | bytes 393224 | tf_op jit(solution)/shard_map/ppermute | solution.py:350

commit v4 on v1

--- a/solution.py
+++ b/solution.py
@@ -29,6 +29,46 @@
     mid = rest.astype(BF)
     lo = (rest - mid.astype(F32)).astype(BF)
     return hi, mid, lo
+
+
+ANY = pl.BlockSpec(memory_space=pl.ANY)
+VMEM = pl.BlockSpec(memory_space=pltpu.VMEM)
+SMEM = pl.BlockSpec(memory_space=pltpu.SMEM)
+ROOM = pltpu.CompilerParams(vmem_limit_bytes=16 << 20)
+
+
+def gather_kernel(*refs):
+    parts, own, columns, ids, sem = refs[:4], *refs[4:]
+    copies = [
+        pltpu.make_async_copy(part.at[pl.ds(0, 512)], own.at[pl.ds(512 * i, 512)], sem.at[i])
+        for i, part in enumerate(parts)
+    ]
+    small = [
+        pltpu.make_async_copy(part.at[pl.ds(512, 16)], ids.at[i], sem.at[4 + i])
+        for i, part in enumerate(parts)
+    ]
+    for copy in copies + small:
+        copy.start()
+    for copy in small:
+        copy.wait()
+    for i in range(4):
+        columns[4 * i : 4 * (i + 1), :] = ids[i].astype(F32)[0:4, 0:128].astype(jnp.int32)
+    for copy in copies:
+        copy.wait()
+
+
+def gathered(blocks):
+    return pl.pallas_call(
+        gather_kernel,
+        out_shape=(
+            jax.ShapeDtypeStruct((2048, 256), BF),
+            jax.ShapeDtypeStruct((16, 128), jnp.int32),
+        ),
+        in_specs=[ANY] * 4,
+        out_specs=(ANY, VMEM),
+        scratch_shapes=[pltpu.VMEM((4, 16, 256), BF), pltpu.SemaphoreType.DMA((8,))],
+        compiler_params=pltpu.CompilerParams(vmem_limit_bytes=4 << 20),
+    )(*blocks)
 
 
 def near_kernel(
@@ -38,27 +78,29 @@
     x = info[0]
     even = info[1]
     late = info[2]
-    copies = [
+    windows = [
         pltpu.make_async_copy(own, win.at[pl.ds(2048, 2048)], sem.at[0]),
         pltpu.make_async_copy(before, win.at[pl.ds(0, 2048)], sem.at[1]),
         pltpu.make_async_copy(after, win.at[pl.ds(4096, 2048)], sem.at[2]),
-        pltpu.make_async_copy(own_tiles.at[pl.ds(x * 4, 4)], tiles.at[0], sem.at[3]),
-        pltpu.make_async_copy(tiles_a, tiles.at[1], sem.at[4]),
-        pltpu.make_async_copy(tiles_b, tiles.at[2], sem.at[5]),
-        pltpu.make_async_copy(tiles_c, tiles.at[3], sem.at[6]),
-    ]
-    for copy in copies:
+    ]
+    arrivals = [pltpu.make_async_copy(own_tiles.at[pl.ds(x * 4, 4)], tiles.at[0], sem.at[3])]
+    arrivals += [
+        pltpu.make_async_copy(part, tiles.at[i + 1], sem.at[i + 4])
+        for i, part in enumerate((tiles_a, tiles_b, tiles_c))
+    ]
+    for copy in windows + arrivals:
         copy.start()
-    for copy in copies:
+    for copy in windows:
         copy.wait()
     for q in range(4):
         keep, slot = divmod(q, 2)
         parity = even if keep == 1 else 1 - even
-        member = late if slot == 1 else 1 - late
-        k = parity + 2 * member
-        count = counts[k]
+        k = parity + 2 * (late if slot == 1 else 1 - late)
+        count = counts[x * 4 + k]
         total = jnp.zeros((128, 256), F32)
         for delta in range(4):
+            if q == 0:
+                arrivals[delta].wait()
             source = (x + 4 - delta) % 4
             for s in range(0, 4, 2):
                 pieces = []
@@ -68,7 +110,9 @@
                     live = jnp.where(place < count, 1.0, 0.0).astype(F32)
                     piece = tiles[delta, k, t]
                     pieces.append(piece * jnp.full((128, 128), live, F32).astype(BF))
-                    col = jnp.clip(cols[k, place], 0, 47)
+                    col = jnp.clip(cols[delta * 4 + t, x * 4 + k], 0, 47)
+                    member = col & 15
+                    col = (col - member) + ((x - (member >> 2)) & 3) * 4 + (member & 3)
                     rows.append(win[pl.ds(pl.multiple_of(col * 128, 128), 128), :])
                 total = total + dot(
                     jnp.concatenate(pieces, axis=1), jnp.concatenate(rows, axis=0), 1, 0
@@ -80,21 +124,18 @@
 
 
 def near(info, cols, counts, own_tiles, received, before, own, after):
-    smem = pl.BlockSpec(memory_space=pltpu.SMEM)
-    hbm = pl.BlockSpec(memory_space=pl.ANY)
-    vmem = pl.BlockSpec(memory_space=pltpu.VMEM)
     block = jax.ShapeDtypeStruct((2, 128, 256), F32)
     return pl.pallas_call(
         near_kernel,
         out_shape=(block, block),
-        in_specs=[smem] * 3 + [hbm] * 7,
-        out_specs=(vmem, vmem),
+        in_specs=[SMEM] * 3 + [ANY] * 7,
+        out_specs=(VMEM, VMEM),
         scratch_shapes=[
             pltpu.VMEM((6144, 256), BF),
             pltpu.VMEM((4, 4, 4, 128, 128), BF),
             pltpu.SemaphoreType.DMA((7,)),
         ],
-        compiler_params=pltpu.CompilerParams(vmem_limit_bytes=24 << 20),
+        compiler_params=ROOM,
         cost_estimate=pl.CostEstimate(
             flops=540_000_000, bytes_accessed=6_000_000, transcendentals=0
         ),
@@ -139,8 +180,21 @@
     )
 
 
-def merge_kernel(nodes, own, other, choice, *refs):
-    outs, gram = refs[:nodes], refs[nodes]
+def put_transfer(out, place, side, own, other, basis):
+    zh, zl = split2(basis)
+    right = jnp.concatenate([zh, zl, zh], axis=1)
+    for part, at in ((own, side), (other, 1 - side)):
+        ch, cl = split2(part)
+        value = dot(jnp.concatenate([ch, ch, cl], axis=1), right, 1, 1) * (1.0 / 256)
+        out[0, place, pl.ds(pl.multiple_of(at * 128, 128), 128), :] = value
+
+
+def merge_kernel(nodes, last, *refs):
+    info = None
+    if last:
+        info, refs = refs[0], refs[1:]
+    own, other, choice = refs[:3]
+    outs, gram = refs[3 : 3 + nodes], refs[-1]
     for m in range(nodes):
         wide = [jnp.concatenate(pair, axis=0) for pair in zip(split3(own[m]), split3(other[m]))]
         hi, mid, lo = (dot(choice[m], part, 1, 0) for part in wide)
@@ -166,46 +220,43 @@
                 update = dot(left, right, 0, 0)
                 gram[m, done:, :] = gram[m, done:, :] - update[done:, :128]
                 outs[m][0, done:, :] = outs[m][0, done:, :] - update[done:, 128:]
-
-
-def merge(own, other, choice):
+    if last:
+        put_transfer(refs[3 + nodes], 0, info[3], own[0], other[0], outs[0][0])
+
+
+def merge(own, other, choice, info=None):
     nodes = own.shape[0]
-    vmem = pl.BlockSpec(memory_space=pltpu.VMEM)
+    last = info is not None
+    shapes = [jax.ShapeDtypeStruct((1, 128, 256), F32)] * nodes
+    if last:
+        shapes.append(jax.ShapeDtypeStruct((1, 1, 256, 128), F32))
     return pl.pallas_call(
-        functools.partial(merge_kernel, nodes),
-        out_shape=tuple(jax.ShapeDtypeStruct((1, 128, 256), F32) for _ in range(nodes)),
-        in_specs=[vmem] * 3,
-        out_specs=tuple(vmem for _ in range(nodes)),
+        functools.partial(merge_kernel, nodes, last),
+        out_shape=tuple(shapes),
+        in_specs=[SMEM] * last + [VMEM] * 3,
+        out_specs=(VMEM,) * len(shapes),
         scratch_shapes=[pltpu.VMEM((nodes, 128, 128), F32)],
-        compiler_params=pltpu.CompilerParams(vmem_limit_bytes=24 << 20),
+        compiler_params=ROOM,
         cost_estimate=pl.CostEstimate(
             flops=nodes * 40_000_000, bytes_accessed=nodes * 600_000, transcendentals=0
         ),
-    )(own, other, choice)
+    )(*([info] * last), own, other, choice)
 
 
 def transfer_kernel(nodes, info, own, other, *refs):
     basis, out = refs[:nodes], refs[nodes]
-    side = info[3]
     for m in range(nodes):
         place = 0 if nodes == 1 else (info[2] if m == 1 else 1 - info[2])
-        zh, zl = split2(basis[m][0])
-        right = jnp.concatenate([zh, zl, zh], axis=1)
-        for part, at in ((own, side), (other, 1 - side)):
-            ch, cl = split2(part[m])
-            value = dot(jnp.concatenate([ch, ch, cl], axis=1), right, 1, 1) * (1.0 / 256)
-            out[0, place, pl.ds(pl.multiple_of(at * 128, 128), 128), :] = value
+        put_transfer(out, place, info[3], own[m], other[m], basis[m][0])
 
 
 def transfer(info, own, other, basis):
     nodes = len(basis)
-    smem = pl.BlockSpec(memory_space=pltpu.SMEM)
-    vmem = pl.BlockSpec(memory_space=pltpu.VMEM)
     return pl.pallas_call(
         functools.partial(transfer_kernel, nodes),
         out_shape=jax.ShapeDtypeStruct((1, nodes, 256, 128), F32),
-        in_specs=[smem] + [vmem] * (2 + nodes),
-        out_specs=vmem,
+        in_specs=[SMEM] + [VMEM] * (2 + nodes),
+        out_specs=VMEM,
         compiler_params=pltpu.CompilerParams(vmem_limit_bytes=24 << 20),
         cost_estimate=pl.CostEstimate(
             flops=nodes * 50_000_000, bytes_accessed=nodes * 600_000, transcendentals=0
@@ -236,29 +287,33 @@
     d = lax.axis_index("leaf")
     x = lax.axis_index("cols")
     b0, b1, b2 = d & 1, (d >> 1) & 1, (d >> 2) & 1
-    infos = [jnp.stack([x, b0, b1, side]).astype(jnp.int32) for side in (b0, b1, b2)]
-
-    own = lax.all_gather(samples, "cols", axis=0, tiled=True)
-    received = [
-        shifted(
-            lax.dynamic_slice_in_dim(near_tiles, ((x + by) % 4) * 4, 4, axis=0), "cols", by
-        )
-        for by in (1, 2, 3)
-    ]
-    all_columns = lax.all_gather(columns - (d - 1) * 16, "cols", axis=0)
-    cols = lax.dynamic_slice_in_dim(all_columns, x * 4, 4, axis=1)
-    cols = jnp.swapaxes(cols, 0, 1).reshape(4, 16)
-    counts = lax.dynamic_slice_in_dim(tile_count, x * 4, 4, axis=0)
+    infos = [
+        jnp.stack([x, b0, b1, side]).astype(jnp.int32) for side in (b0, b1, b2)
+    ]
+
+    near_columns = jnp.clip(columns - (d - 1) * 16, 0, 47).astype(BF).T
+    block = jnp.concatenate([samples, jnp.pad(near_columns, ((0, 12), (0, 240)))], axis=0)
+    by_one, by_three, by_two = (shifted(block, "cols", by) for by in (1, 3, 2))
+    one, two, three = (
+        lax.dynamic_slice_in_dim(near_tiles, (x + by) % 4 * 4, 4, axis=0) for by in (1, 2, 3)
+    )
+    tiles_one = shifted(one, "cols", 1)
+    tiles_three = shifted(three, "cols", 3)
+    two, tiles_one, tiles_three = lax.optimization_barrier((two, tiles_one, tiles_three))
+    received = [tiles_one, shifted(two, "cols", 2), tiles_three]
+    own, cols = gathered([block, by_one, by_two, by_three])
     leaves = lax.axis_size("leaf")
-    up = [(i, i + 1) for i in range(leaves - 1)]
-    before = lax.ppermute(own, "leaf", up)
-    after = lax.ppermute(own, "leaf", [(j, i) for i, j in up])
+    rising = [(i, i + 1) for i in range(leaves - 1)]
+    before = lax.ppermute(own, "leaf", rising)
+    after = lax.ppermute(own, "leaf", [(j, i) for i, j in rising])
 
     choice_one = one_hot(skeleton_one, d >> 1, (b0 + 2 - 2 * b1, b0 + 2 * b1), b0)
     choice_two = one_hot(skeleton_two, d >> 2, (d & 3,), b1)
     choice_three = one_hot(skeleton_three, d >> 3, (d & 3,), b2)
 
-    send, keep = near(infos[0], cols, counts, near_tiles, received, before, own, after)
+    send, keep = near(
+        infos[0], cols, tile_count, near_tiles, received, before, own, after
+    )
     other = swapped(send, 1)
     away, basis = merge(keep, other, choice_one)
     arrived = swapped(away, 2)
@@ -266,8 +321,7 @@
     (basis_two,) = merge(basis, arrived, choice_two)
     arrived_two = swapped(basis_two, 4)
     out_two = transfer(infos[1], basis, arrived, (basis_two,))
-    (top,) = merge(basis_two, arrived_two, choice_three)
-    out_three = transfer(infos[2], basis_two, arrived_two, (top,))
+    top, out_three = merge(basis_two, arrived_two, choice_three, infos[2])
     return out_one, out_two, out_three, top[None]
 
 

time: 140 us -> 95 us (0.68)
  blocking collectives: 24.8 us -> 0 us
  waiting for transfers between devices: 42.5 us -> 19 us
  between operations: 14.3 us -> 0.93 us
  starting transfers between devices: 30.1 us -> 41.5 us
  local copies, waits for them, and re-layouts: 4.44 us -> 8.38 us
  other arithmetic: 1.84 us -> 3.5 us
    all_gather x1 -> x0, waiting for transfers between devices: 36.1 us -> none  [local(): own = lax.all_gather(samples, 'cols', axis=0, tiled=True)]
    all_gather x1 -> x0, blocking collectives: 24.8 us -> none  [local(): all_columns = lax.all_gather(columns - (d - 1) * 16, 'cols', axis=0)]
    ppermute x3 -> x6, waiting for transfers between devices: 0.01 us -> 13 us  [shifted(): lax.ppermute(value, axis, [(i, (i + by) % count) for i in range(count)])]
    ppermute x3 -> x6, starting transfers between devices: 9.56 us -> 21.2 us  [shifted(): lax.ppermute(value, axis, [(i, (i + by) % count) for i in range(count)])]
    unnamed x10 -> x16, local copies, waits for them, and re-layouts: 0.92 us -> 4.98 us
    ppermute x3, starting transfers between devices: 13.7 us -> 11.1 us  [swapped(): return lax.ppermute(value, 'leaf', [(i, i ^ apart) for i in range(count)])]
    ppermute x2, starting transfers between devices: 6.78 us -> 9.25 us  [the longest x1 5.96 us: local(): before = lax.ppermute(own, 'leaf', rising)]
    pallas_call x3 -> x2, Pallas kernels: 4.55 us -> 3.09 us  [transfer(): pl.pallas_call(functools.partial(transfer_kernel, nodes), out_shape=jax.S...]
  transfers between devices with their start and end apart: 9 -> 11, of which waited for: 4 -> 4; matrix products, arithmetic and copies ran while one was open for 4% -> 6% of each run, Pallas kernels for 2% -> 3%
where the time goes in v4:
time: 95 us; the launch traced here: 94.3 us
  starting transfers between devices  41.5 us (44%)
  Pallas kernels  21.1 us (22%)
  waiting for transfers between devices  19 us (20%)
  local copies, waits for them, and re-layouts  8.38 us (9%)
  other arithmetic  3.5 us (4%)
    ppermute x6, starting transfers between devices, shifted(): lax.ppermute(value, axis, [(i, (i + by) % count) for i in range(count)])  21.2 us
    pallas_call x3, Pallas kernels, merge(): pl.pallas_call(functools.partial(merge_kernel, nodes, last), out_shape=tu...  14.4 us
    ppermute x6, waiting for transfers between devices, shifted(): lax.ppermute(value, axis, [(i, (i + by) % count) for i in range(count)])  13 us
    ppermute x3, starting transfers between devices, swapped(): return lax.ppermute(value, 'leaf', [(i, i ^ apart) for i in range(count)])  11.1 us
    ppermute x1, starting transfers between devices, local(): before = lax.ppermute(own, 'leaf', rising)  5.96 us
    ppermute x3, waiting for transfers between devices, swapped(): return lax.ppermute(value, 'leaf', [(i, i ^ apart) for i in range(count)])  5.95 us
    unnamed x16, local copies, waits for them, and re-layouts  4.98 us
    pallas_call x1, Pallas kernels, near(): pl.pallas_call(near_kernel, out_shape=(block, block), in_specs=[SMEM] * 3...  3.42 us
  transfers between devices with their start and end apart: 11, of which 4 were waited for; matrix products, arithmetic and copies ran while one was open for 6% of the time, Pallas kernels for 3%

profile of v4, /device:TPU:1, one launch (start us, length us, event | category | flops | bytes accessed | tf_op | source)
XLA Modules:
  0.0 94.3 jit_solution(1810772714529898662)
XLA Ops:
  1.3 1.0 %fusion.1.refs_0_ = bf16[528,256]{1,0:T(8,128)(2,1)S(1)} fusion(bf16[4,16]{1,0:T(4,128)(2,1)S(1)} %fusion.6, bf16[512,256]{1,0:T(8,128)(2,1)} %param.7), kind=kLoop, calls=%fused_computation.2 | loop fusion | flops 811008 | bytes 532608 | tf_op jit(solution)/shard_map/concatenate | solution.py:295
  2.3 3.9 %collective-permute-start = (bf16[528,256]{1,0:T(8,128)(2,1)S(1)}, bf16[528,256]{1,0:T(8,128)(2,1)S(1)}, u32[]{:S(2)}, u32[]{:S(2)}) collective-permute-start(bf16[528,256]{1,0:T(8,128)(2,1)S(1)} %fusion.1.refs_0_), channel_id=1, source_target_pairs={{0,1},{1,2},{2,3},{3,0},{4,5},{5,6},{6,7},{7,4},{8,9},{9,10},{10,1... | collective-permute-start | bytes 811016 | tf_op jit(solution)/shard_map/ppermute | solution.py:269
  6.3 4.4 %collective-permute-start.1 = (bf16[528,256]{1,0:T(8,128)(2,1)S(1)}, bf16[528,256]{1,0:T(8,128)(2,1)S(1)}, u32[]{:S(2)}, u32[]{:S(2)}) collective-permute-start(bf16[528,256]{1,0:T(8,128)(2,1)S(1)} %fusion.1.refs_0_), channel_id=1, source_target_pairs={{0,2},{1,3},{2,0},{3,1},{4,6},{5,7},{6,4},{7,5},{8,10},{9,11},{10,... | collective-permute-start | bytes 811016 | tf_op jit(solution)/shard_map/ppermute | solution.py:269
  10.6 3.1 %collective-permute-start.2 = (bf16[528,256]{1,0:T(8,128)(2,1)S(1)}, bf16[528,256]{1,0:T(8,128)(2,1)S(1)}, u32[]{:S(2)}, u32[]{:S(2)}) collective-permute-start(bf16[528,256]{1,0:T(8,128)(2,1)S(1)} %fusion.1.refs_0_), channel_id=1, source_target_pairs={{0,3},{1,0},{2,1},{3,2},{4,7},{5,4},{6,5},{7,6},{8,11},{9,8},{10,9... | collective-permute-start | bytes 811016 | tf_op jit(solution)/shard_map/ppermute | solution.py:269
  13.8 2.7 %constant_dynamic-slice_fusion.4 = (bf16[4,4,128,128]{3,2,1,0:T(8,128)(2,1)}, bf16[4,4,128,128]{3,2,1,0:T(8,128)(2,1)}, bf16[4,4,128,128]{3,2,1,0:T(8,128)(2,1)}) fusion(bf16[16,4,128,128]{3,2,1,0:T(8,128)(2,1)} %own_tiles.1, s32[]{:T(128)S(6)} %select_n.60, s32[]{:T(128)S(6)} %select_n.58, s32[]{:T(128)S(6)} %select_n.56), kind=kLoop, calls=%fused_computation.17 | loop fusion | bytes 3145740 | tf_op jit(solution)/shard_map/dynamic_slice | solution.py:298
  16.5 2.2 %collective-permute-start.3 = (bf16[4,4,128,128]{3,2,1,0:T(8,128)(2,1)}, bf16[4,4,128,128]{3,2,1,0:T(8,128)(2,1)}, u32[]{:S(2)}, u32[]{:S(2)}) collective-permute-start(bf16[4,4,128,128]{3,2,1,0:T(8,128)(2,1)} %get-tuple-element.29), channel_id=1, source_target_pairs={{0,1},{1,2},{2,3},{3,0},{4,5},{5,6},{6,7},{7,4},{8,9},{9,10},{10,1... | collective-permute-start | bytes 1572872 | tf_op jit(solution)/shard_map/ppermute | solution.py:269
  18.7 4.3 %collective-permute-start.4 = (bf16[4,4,128,128]{3,2,1,0:T(8,128)(2,1)}, bf16[4,4,128,128]{3,2,1,0:T(8,128)(2,1)}, u32[]{:S(2)}, u32[]{:S(2)}) collective-permute-start(bf16[4,4,128,128]{3,2,1,0:T(8,128)(2,1)} %get-tuple-element.28), channel_id=1, source_target_pairs={{0,3},{1,0},{2,1},{3,2},{4,7},{5,4},{6,5},{7,6},{8,11},{9,8},{10,9... | collective-permute-start | bytes 1572872 | tf_op jit(solution)/shard_map/ppermute | solution.py:269
  25.1 1.0 %copy-done.2 = bf16[528,256]{1,0:T(8,128)(2,1)S(1)} copy-done((bf16[528,256]{1,0:T(8,128)(2,1)S(1)}, bf16[528,256]{1,0:T(8,128)(2,1)}, u32[]{:S(2)}) %copy-start.2) | copy-done | bytes 270360
  26.0 1.0 %copy-done.4 = bf16[528,256]{1,0:T(8,128)(2,1)S(1)} copy-done((bf16[528,256]{1,0:T(8,128)(2,1)S(1)}, bf16[528,256]{1,0:T(8,128)(2,1)}, u32[]{:S(2)}) %copy-start.4) | copy-done | bytes 270360
  28.2 6.0 %collective-permute-start.6 = (bf16[2048,256]{1,0:T(8,128)(2,1)S(1)}, bf16[2048,256]{1,0:T(8,128)(2,1)}, u32[]{:S(2)}, u32[]{:S(2)}) collective-permute-start(bf16[2048,256]{1,0:T(8,128)(2,1)S(1)} %get-tuple-element.19.own), channel_id=1, source_target_pairs={{0,4},{4,8},{8,12},{12,16},{16,20},{20,24},{24,28},{28,32},{32,36}... | collective-permute-start | bytes 3145736 | tf_op jit(solution)/shard_map/ppermute | solution.py:307
  34.1 3.3 %collective-permute-start.7 = (bf16[2048,256]{1,0:T(8,128)(2,1)S(1)}, bf16[2048,256]{1,0:T(8,128)(2,1)}, u32[]{:S(2)}, u32[]{:S(2)}) collective-permute-start(bf16[2048,256]{1,0:T(8,128)(2,1)S(1)} %get-tuple-element.19.own), channel_id=1, source_target_pairs={{4,0},{8,4},{12,8},{16,12},{20,16},{24,20},{28,24},{32,28},{36,32}... | collective-permute-start | bytes 3145736 | tf_op jit(solution)/shard_map/ppermute | solution.py:308
  37.5 3.3 %collective-permute-start.5 = (bf16[4,4,128,128]{3,2,1,0:T(8,128)(2,1)}, bf16[4,4,128,128]{3,2,1,0:T(8,128)(2,1)S(1)}, u32[]{:S(2)}, u32[]{:S(2)}) collective-permute-start(bf16[4,4,128,128]{3,2,1,0:T(8,128)(2,1)} %get-tuple-element.17), channel_id=1, source_target_pairs={{0,2},{1,3},{2,0},{3,1},{4,6},{5,7},{6,4},{7,5},{8,10},{9,11},{10,... | collective-permute-start | bytes 1572872 | tf_op jit(solution)/shard_map/ppermute | solution.py:269
  41.7 13.0 %collective-permute-done.5.tiles_b = bf16[4,4,128,128]{3,2,1,0:T(8,128)(2,1)S(1)} collective-permute-done((bf16[4,4,128,128]{3,2,1,0:T(8,128)(2,1)}, bf16[4,4,128,128]{3,2,1,0:T(8,128)(2,1)S(1)}, u32[]{:S(2)}, u32[]{:S(2)}) %collective-permute-start.5) | collective-permute-done | bytes 524320 | tf_op jit(solution)/shard_map/ppermute | solution.py:269
  54.7 3.4 %shard_map.103 = (f32[2,128,256]{2,1,0:T(8,128)S(1)}, f32[2,128,256]{2,1,0:T(8,128)S(1)}) custom-call(s32[4]{0:T(128)S(1)} %get-tuple-element.34.info, s32[16,128]{1,0:T(8,128)S(1)} %get-tuple-element.15.cols, s32[16]{0:T(128)S(1)} %copy-done.7, bf16[16,4,128,128]{3,2,1,0:T(8,128)(2,1)S(1)} %copy-done, ...), custom_call_target="tpu_custom_call" | custom-call | flops 540000000 | bytes 6000000 | tf_op jit(solution)/shard_map/pallas_call | solution.py:128
  58.2 2.3 %collective-permute-start.8 = (f32[2,128,256]{2,1,0:T(8,128)S(1)}, f32[2,128,256]{2,1,0:T(8,128)S(1)}, u32[]{:S(2)}, u32[]{:S(2)}) collective-permute-start(f32[2,128,256]{2,1,0:T(8,128)S(1)} %get-tuple-element.21), channel_id=1, source_target_pairs={{0,4},{4,0},{8,12},{12,8},{16,20},{20,16},{24,28},{28,24},{32,36},... | collective-permute-start | bytes 786440 | tf_op jit(solution)/shard_map/ppermute | solution.py:274
  61.6 4.9 %shard_map.104 = (f32[1,128,256]{2,1,0:T(8,128)S(1)}, f32[1,128,256]{2,1,0:T(8,128)S(1)}) custom-call(f32[2,128,256]{2,1,0:T(8,128)S(1)} %get-tuple-element.20.refs_0_.own, f32[2,128,256]{2,1,0:T(8,128)S(1)} %collective-permute-done.8.refs_1_.other, bf16[2,128,256]{2,1,0:T(8,128)(2,1)S(1)} %fusion.2.refs_2_), custom_call_target="tpu_custom_call" | custom-call | flops 80000000 | bytes 1200000 | tf_op jit(solution)/shard_map/pallas_call | solution.py:233
  66.5 3.0 %collective-permute-start.9 = (f32[1,128,256]{2,1,0:T(8,128)S(1)}, f32[1,128,256]{2,1,0:T(8,128)S(1)}, u32[]{:S(2)}, u32[]{:S(2)}) collective-permute-start(f32[1,128,256]{2,1,0:T(8,128)S(1)} %get-tuple-element.22.refs_0_), channel_id=1, source_target_pairs={{0,8},{4,12},{8,0},{12,4},{16,24},{20,28},{24,16},{28,20},{32,40},... | collective-permute-start | bytes 393224 | tf_op jit(solution)/shard_map/ppermute | solution.py:274
  70.3 2.8 %collective-permute-done.9.refs_1_.other = f32[1,128,256]{2,1,0:T(8,128)S(1)} collective-permute-done((f32[1,128,256]{2,1,0:T(8,128)S(1)}, f32[1,128,256]{2,1,0:T(8,128)S(1)}, u32[]{:S(2)}, u32[]{:S(2)}) %collective-permute-start.9) | collective-permute-done | bytes 131104 | tf_op jit(solution)/shard_map/ppermute | solution.py:274
  73.1 4.0 %shard_map.106.refs_0_.refs_1_ = f32[1,128,256]{2,1,0:T(8,128)S(1)} custom-call(f32[1,128,256]{2,1,0:T(8,128)S(1)} %get-tuple-element.23.refs_1_.refs_0_.own, f32[1,128,256]{2,1,0:T(8,128)S(1)} %collective-permute-done.9.refs_1_.other, bf16[1,128,256]{2,1,0:T(8,128)(2,1)S(1)} %fusion.3.refs_2_), custom_call_target="tpu_custom_call" | custom-call | flops 40000000 | bytes 600000 | tf_op jit(solution)/shard_map/pallas_call | solution.py:233
  77.1 5.8 %collective-permute-start.10 = (f32[1,128,256]{2,1,0:T(8,128)S(1)}, f32[1,128,256]{2,1,0:T(8,128)S(1)}, u32[]{:S(2)}, u32[]{:S(2)}) collective-permute-start(f32[1,128,256]{2,1,0:T(8,128)S(1)} %shard_map.106.refs_0_.refs_1_), channel_id=1, source_target_pairs={{0,16},{4,20},{8,24},{12,28},{16,0},{20,4},{24,8},{28,12},{32,48},... | collective-permute-start | bytes 393224 | tf_op jit(solution)/shard_map/ppermute | solution.py:274
  83.0 1.6 %shard_map.105 = f32[1,2,256,128]{3,2,1,0:T(8,128)} custom-call(s32[4]{0:T(128)S(1)} %get-tuple-element.34.info, f32[2,128,256]{2,1,0:T(8,128)S(1)} %get-tuple-element.20.refs_0_.own, f32[2,128,256]{2,1,0:T(8,128)S(1)} %collective-permute-done.8.refs_1_.other, f32[1,128,256]{2,1,0:T(8,128)S(1)} %get-tuple-element.22.refs_0_, ...), custom_call_target="tpu_custom_call" | custom-call | flops 100000000 | bytes 1200000 | tf_op jit(solution)/shard_map/pallas_call | solution.py:255
  84.6 1.5 %shard_map.107 = f32[1,1,256,128]{3,2,1,0:T(8,128)} custom-call(s32[4]{0:T(128)S(1)} %get-tuple-element.33.info, f32[1,128,256]{2,1,0:T(8,128)S(1)} %get-tuple-element.23.refs_1_.refs_0_.own, f32[1,128,256]{2,1,0:T(8,128)S(1)} %collective-permute-done.9.refs_1_.other, f32[1,128,256]{2,1,0:T(8,128)S(1)} %shard_map.106.refs_0_.refs_1_), custom_call_target="tpu_custom_call" | custom-call | flops 50000000 | bytes 600000 | tf_op jit(solution)/shard_map/pallas_call | solution.py:255
  86.1 2.8 %collective-permute-done.10.refs_2_ = f32[1,128,256]{2,1,0:T(8,128)S(1)} collective-permute-done((f32[1,128,256]{2,1,0:T(8,128)S(1)}, f32[1,128,256]{2,1,0:T(8,128)S(1)}, u32[]{:S(2)}, u32[]{:S(2)}) %collective-permute-start.10) | collective-permute-done | bytes 131104 | tf_op jit(solution)/shard_map/ppermute | solution.py:274
  88.9 5.5 %shard_map.108 = (f32[1,128,256]{2,1,0:T(8,128)}, f32[1,1,256,128]{3,2,1,0:T(8,128)}) custom-call(s32[4]{0:T(128)S(1)} %get-tuple-element.26.refs_0_, f32[1,128,256]{2,1,0:T(8,128)S(1)} %shard_map.106.refs_0_.refs_1_, f32[1,128,256]{2,1,0:T(8,128)S(1)} %collective-permute-done.10.refs_2_, bf16[1,128,256]{2,1,0:T(8,128)(2,1)S(1)} %fusion.4.refs_3_), custom_call_target="tpu_custom_call" | custom-call | flops 40000000 | bytes 600000 | tf_op jit(solution)/shard_map/pallas_call | solution.py:233
  (33 shorter events, 6.9 us)
Async XLA Ops:
  2.3 20.7 %collective-permute-start = (bf16[528,256]{1,0:T(8,128)(2,1)S(1)}, bf16[528,256]{1,0:T(8,128)(2,1)S(1)}, u32[]{:S(2)}, u32[]{:S(2)}) collective-permute-start(bf16[528,256]{1,0:T(8,128)(2,1)S(1)} %fusion.1.refs_0_), channel_id=1, source_target_pairs={{0,1},{1,2},{2,3},{3,0},{4,5},{5,6},{6,7},{7,4},{8,9},{9,10},{10,1... | collective-permute-start | bytes 811016 | tf_op jit(solution)/shard_map/ppermute | solution.py:269
  6.3 17.4 %collective-permute-start.1 = (bf16[528,256]{1,0:T(8,128)(2,1)S(1)}, bf16[528,256]{1,0:T(8,128)(2,1)S(1)}, u32[]{:S(2)}, u32[]{:S(2)}) collective-permute-start(bf16[528,256]{1,0:T(8,128)(2,1)S(1)} %fusion.1.refs_0_), channel_id=1, source_target_pairs={{0,2},{1,3},{2,0},{3,1},{4,6},{5,7},{6,4},{7,5},{8,10},{9,11},{10,... | collective-permute-start | bytes 811016 | tf_op jit(solution)/shard_map/ppermute | solution.py:269
  10.6 13.8 %collective-permute-start.2 = (bf16[528,256]{1,0:T(8,128)(2,1)S(1)}, bf16[528,256]{1,0:T(8,128)(2,1)S(1)}, u32[]{:S(2)}, u32[]{:S(2)}) collective-permute-start(bf16[528,256]{1,0:T(8,128)(2,1)S(1)} %fusion.1.refs_0_), channel_id=1, source_target_pairs={{0,3},{1,0},{2,1},{3,2},{4,7},{5,4},{6,5},{7,6},{8,11},{9,8},{10,9... | collective-permute-start | bytes 811016 | tf_op jit(solution)/shard_map/ppermute | solution.py:269
  13.7 41.0 %copy-start = (bf16[16,4,128,128]{3,2,1,0:T(8,128)(2,1)S(1)}, bf16[16,4,128,128]{3,2,1,0:T(8,128)(2,1)}, u32[]{:S(2)}) copy-start(bf16[16,4,128,128]{3,2,1,0:T(8,128)(2,1)} %own_tiles.1) | copy-start | bytes 6291460
  13.7 41.0 %copy-start.7 = (s32[16]{0:T(128)S(1)}, s32[16]{0:T(128)}, u32[]{:S(2)}) copy-start(s32[16]{0:T(128)} %counts.1) | copy-start | bytes 196
  16.5 21.0 %collective-permute-start.3 = (bf16[4,4,128,128]{3,2,1,0:T(8,128)(2,1)}, bf16[4,4,128,128]{3,2,1,0:T(8,128)(2,1)}, u32[]{:S(2)}, u32[]{:S(2)}) collective-permute-start(bf16[4,4,128,128]{3,2,1,0:T(8,128)(2,1)} %get-tuple-element.29), channel_id=1, source_target_pairs={{0,1},{1,2},{2,3},{3,0},{4,5},{5,6},{6,7},{7,4},{8,9},{9,10},{10,1... | collective-permute-start | bytes 1572872 | tf_op jit(solution)/shard_map/ppermute | solution.py:269
  18.7 18.8 %collective-permute-start.4 = (bf16[4,4,128,128]{3,2,1,0:T(8,128)(2,1)}, bf16[4,4,128,128]{3,2,1,0:T(8,128)(2,1)}, u32[]{:S(2)}, u32[]{:S(2)}) collective-permute-start(bf16[4,4,128,128]{3,2,1,0:T(8,128)(2,1)} %get-tuple-element.28), channel_id=1, source_target_pairs={{0,3},{1,0},{2,1},{3,2},{4,7},{5,4},{6,5},{7,6},{8,11},{9,8},{10,9... | collective-permute-start | bytes 1572872 | tf_op jit(solution)/shard_map/ppermute | solution.py:269
  23.0 0.7 copy-start.1
  23.7 0.7 copy-start.3
  24.4 0.7 copy-start.5
  25.1 1.0 %copy-start.2 = (bf16[528,256]{1,0:T(8,128)(2,1)S(1)}, bf16[528,256]{1,0:T(8,128)(2,1)}, u32[]{:S(2)}) copy-start(bf16[528,256]{1,0:T(8,128)(2,1)} %copy-done.1) | copy-start | bytes 811012
  26.0 1.0 %copy-start.4 = (bf16[528,256]{1,0:T(8,128)(2,1)S(1)}, bf16[528,256]{1,0:T(8,128)(2,1)}, u32[]{:S(2)}) copy-start(bf16[528,256]{1,0:T(8,128)(2,1)} %copy-done.3) | copy-start | bytes 811012
  27.0 1.0 %copy-start.6 = (bf16[528,256]{1,0:T(8,128)(2,1)S(1)}, bf16[528,256]{1,0:T(8,128)(2,1)}, u32[]{:S(2)}) copy-start(bf16[528,256]{1,0:T(8,128)(2,1)} %copy-done.5) | copy-start | bytes 811012
  28.2 26.5 %collective-permute-start.6 = (bf16[2048,256]{1,0:T(8,128)(2,1)S(1)}, bf16[2048,256]{1,0:T(8,128)(2,1)}, u32[]{:S(2)}, u32[]{:S(2)}) collective-permute-start(bf16[2048,256]{1,0:T(8,128)(2,1)S(1)} %get-tuple-element.19.own), channel_id=1, source_target_pairs={{0,4},{4,8},{8,12},{12,16},{16,20},{20,24},{24,28},{28,32},{32,36}... | collective-permute-start | bytes 3145736 | tf_op jit(solution)/shard_map/ppermute | solution.py:307
  34.1 20.6 %collective-permute-start.7 = (bf16[2048,256]{1,0:T(8,128)(2,1)S(1)}, bf16[2048,256]{1,0:T(8,128)(2,1)}, u32[]{:S(2)}, u32[]{:S(2)}) collective-permute-start(bf16[2048,256]{1,0:T(8,128)(2,1)S(1)} %get-tuple-element.19.own), channel_id=1, source_target_pairs={{4,0},{8,4},{12,8},{16,12},{20,16},{24,20},{28,24},{32,28},{36,32}... | collective-permute-start | bytes 3145736 | tf_op jit(solution)/shard_map/ppermute | solution.py:308
  37.5 17.2 %collective-permute-start.5 = (bf16[4,4,128,128]{3,2,1,0:T(8,128)(2,1)}, bf16[4,4,128,128]{3,2,1,0:T(8,128)(2,1)S(1)}, u32[]{:S(2)}, u32[]{:S(2)}) collective-permute-start(bf16[4,4,128,128]{3,2,1,0:T(8,128)(2,1)} %get-tuple-element.17), channel_id=1, source_target_pairs={{0,2},{1,3},{2,0},{3,1},{4,6},{5,7},{6,4},{7,5},{8,10},{9,11},{10,... | collective-permute-start | bytes 1572872 | tf_op jit(solution)/shard_map/ppermute | solution.py:269
  58.2 3.5 %collective-permute-start.8 = (f32[2,128,256]{2,1,0:T(8,128)S(1)}, f32[2,128,256]{2,1,0:T(8,128)S(1)}, u32[]{:S(2)}, u32[]{:S(2)}) collective-permute-start(f32[2,128,256]{2,1,0:T(8,128)S(1)} %get-tuple-element.21), channel_id=1, source_target_pairs={{0,4},{4,0},{8,12},{12,8},{16,20},{20,16},{24,28},{28,24},{32,36},... | collective-permute-start | bytes 786440 | tf_op jit(solution)/shard_map/ppermute | solution.py:274
  66.5 6.6 %collective-permute-start.9 = (f32[1,128,256]{2,1,0:T(8,128)S(1)}, f32[1,128,256]{2,1,0:T(8,128)S(1)}, u32[]{:S(2)}, u32[]{:S(2)}) collective-permute-start(f32[1,128,256]{2,1,0:T(8,128)S(1)} %get-tuple-element.22.refs_0_), channel_id=1, source_target_pairs={{0,8},{4,12},{8,0},{12,4},{16,24},{20,28},{24,16},{28,20},{32,40},... | collective-permute-start | bytes 393224 | tf_op jit(solution)/shard_map/ppermute | solution.py:274
  77.1 11.8 %collective-permute-start.10 = (f32[1,128,256]{2,1,0:T(8,128)S(1)}, f32[1,128,256]{2,1,0:T(8,128)S(1)}, u32[]{:S(2)}, u32[]{:S(2)}) collective-permute-start(f32[1,128,256]{2,1,0:T(8,128)S(1)} %shard_map.106.refs_0_.refs_1_), channel_id=1, source_target_pairs={{0,16},{4,20},{8,24},{12,28},{16,0},{20,4},{24,8},{28,12},{32,48},... | collective-permute-start | bytes 393224 | tf_op jit(solution)/shard_map/ppermute | solution.py:274

commit v5 on v4

--- a/solution.py
+++ b/solution.py
@@ -37,42 +37,8 @@
 ROOM = pltpu.CompilerParams(vmem_limit_bytes=16 << 20)
 
 
-def gather_kernel(*refs):
-    parts, own, columns, ids, sem = refs[:4], *refs[4:]
-    copies = [
-        pltpu.make_async_copy(part.at[pl.ds(0, 512)], own.at[pl.ds(512 * i, 512)], sem.at[i])
-        for i, part in enumerate(parts)
-    ]
-    small = [
-        pltpu.make_async_copy(part.at[pl.ds(512, 16)], ids.at[i], sem.at[4 + i])
-        for i, part in enumerate(parts)
-    ]
-    for copy in copies + small:
-        copy.start()
-    for copy in small:
-        copy.wait()
-    for i in range(4):
-        columns[4 * i : 4 * (i + 1), :] = ids[i].astype(F32)[0:4, 0:128].astype(jnp.int32)
-    for copy in copies:
-        copy.wait()
-
-
-def gathered(blocks):
-    return pl.pallas_call(
-        gather_kernel,
-        out_shape=(
-            jax.ShapeDtypeStruct((2048, 256), BF),
-            jax.ShapeDtypeStruct((16, 128), jnp.int32),
-        ),
-        in_specs=[ANY] * 4,
-        out_specs=(ANY, VMEM),
-        scratch_shapes=[pltpu.VMEM((4, 16, 256), BF), pltpu.SemaphoreType.DMA((8,))],
-        compiler_params=pltpu.CompilerParams(vmem_limit_bytes=4 << 20),
-    )(*blocks)
-
-
 def near_kernel(
-    info, cols, counts, own_tiles, tiles_a, tiles_b, tiles_c, before, own, after,
+    info, cols, counts, own_tiles, tiles_a, tiles_b, tiles_c, _, before, own, after,
     send_ref, keep_ref, win, tiles, sem,
 ):
     x = info[0]
@@ -128,7 +94,7 @@
     return pl.pallas_call(
         near_kernel,
         out_shape=(block, block),
-        in_specs=[SMEM] * 3 + [ANY] * 7,
+        in_specs=[SMEM] * 3 + [ANY] * 8,
         out_specs=(VMEM, VMEM),
         scratch_shapes=[
             pltpu.VMEM((6144, 256), BF),
@@ -299,9 +265,12 @@
     )
     tiles_one = shifted(one, "cols", 1)
     tiles_three = shifted(three, "cols", 3)
-    two, tiles_one, tiles_three = lax.optimization_barrier((two, tiles_one, tiles_three))
-    received = [tiles_one, shifted(two, "cols", 2), tiles_three]
-    own, cols = gathered([block, by_one, by_two, by_three])
+    tiles_one, tiles_three = lax.optimization_barrier((tiles_one, tiles_three))
+    tie = swapped(tiles_one, 1)
+    own = jnp.concatenate([samples] + [part[:512] for part in (by_one, by_two, by_three)], axis=0)
+    cols = jnp.concatenate([part[512:516, :16] for part in (block, by_one, by_two, by_three)])
+    own, two, cols = lax.optimization_barrier((own, two, cols.astype(jnp.int32)))
+    received = [tiles_one, shifted(two, "cols", 2), tiles_three, tie]
     leaves = lax.axis_size("leaf")
     rising = [(i, i + 1) for i in range(leaves - 1)]
     before = lax.ppermute(own, "leaf", rising)

time: 95 us -> 92.6 us (0.975)
  local copies, waits for them, and re-layouts: 8.38 us -> 5.75 us
  starting transfers between devices: 41.5 us -> 44.1 us
  waiting for transfers between devices: 19 us -> 16.7 us
    unnamed x16 -> x10, local copies, waits for them, and re-layouts: 4.98 us -> 1.09 us
    ppermute x3 -> x4, starting transfers between devices: 11.1 us -> 13.6 us  [swapped(): return lax.ppermute(value, 'leaf', [(i, i ^ apart) for i in range(count)])]
    ppermute x6, waiting for transfers between devices: 13 us -> 11 us  [shifted(): lax.ppermute(value, axis, [(i, (i + by) % count) for i in range(count)])]
    slice x0 -> x6, local copies, waits for them, and re-layouts: none -> 1.37 us  [the longest x3 1.31 us: local(): part[512:516, :16]]
    ppermute x1, starting transfers between devices: 5.96 us -> 7.09 us  [local(): before = lax.ppermute(own, 'leaf', rising)]
    ppermute x3 -> x4, waiting for transfers between devices: 5.95 us -> 5.65 us  [swapped(): return lax.ppermute(value, 'leaf', [(i, i ^ apart) for i in range(count)])]
  transfers between devices with their start and end apart: 11 -> 12, of which waited for: 4 -> 5; matrix products, arithmetic and copies ran while one was open for 6% -> 7% of each run, Pallas kernels for 3% -> 3%
where the time goes in v5:
time: 92.6 us; the launch traced here: 92 us
  starting transfers between devices  44.1 us (48%)
  Pallas kernels  20.9 us (23%)
  waiting for transfers between devices  16.7 us (18%)
  local copies, waits for them, and re-layouts  5.75 us (6%)
  other arithmetic  3.58 us (4%)
  between operations  0.98 us (1%)
    ppermute x6, starting transfers between devices, shifted(): lax.ppermute(value, axis, [(i, (i + by) % count) for i in range(count)])  20.5 us
    pallas_call x3, Pallas kernels, merge(): pl.pallas_call(functools.partial(merge_kernel, nodes, last), out_shape=tu...  14.3 us
    ppermute x4, starting transfers between devices, swapped(): return lax.ppermute(value, 'leaf', [(i, i ^ apart) for i in range(count)])  13.6 us
    ppermute x6, waiting for transfers between devices, shifted(): lax.ppermute(value, axis, [(i, (i + by) % count) for i in range(count)])  11 us
    ppermute x1, starting transfers between devices, local(): before = lax.ppermute(own, 'leaf', rising)  7.09 us
    ppermute x4, waiting for transfers between devices, swapped(): return lax.ppermute(value, 'leaf', [(i, i ^ apart) for i in range(count)])  5.65 us
    pallas_call x1, Pallas kernels, near(): pl.pallas_call(near_kernel, out_shape=(block, block), in_specs=[SMEM] * 3...  3.42 us
    pallas_call x2, Pallas kernels, transfer(): pl.pallas_call(functools.partial(transfer_kernel, nodes), out_shape=jax.S...  3.09 us
  transfers between devices with their start and end apart: 12, of which 5 were waited for; matrix products, arithmetic and copies ran while one was open for 7% of the time, Pallas kernels for 3%

profile of v5, /device:TPU:1, one launch (start us, length us, event | category | flops | bytes accessed | tf_op | source)
XLA Modules:
  0.0 92.0 jit_solution(4159129190420119971)
XLA Ops:
  1.3 1.0 %fusion.1 = bf16[528,256]{1,0:T(8,128)(2,1)S(1)} fusion(bf16[4,16]{1,0:T(4,128)(2,1)S(1)} %fusion.6, bf16[512,256]{1,0:T(8,128)(2,1)} %param.7), kind=kLoop, calls=%fused_computation.3 | loop fusion | flops 811008 | bytes 532608 | tf_op jit(solution)/shard_map/concatenate | solution.py:261
  2.3 5.2 %collective-permute-start.2 = (bf16[528,256]{1,0:T(8,128)(2,1)S(1)}, bf16[528,256]{1,0:T(8,128)(2,1)S(1)}, u32[]{:S(2)}, u32[]{:S(2)}) collective-permute-start(bf16[528,256]{1,0:T(8,128)(2,1)S(1)} %fusion.1), channel_id=1, source_target_pairs={{0,3},{1,0},{2,1},{3,2},{4,7},{5,4},{6,5},{7,6},{8,11},{9,8},{10,9... | collective-permute-start | bytes 811016 | tf_op jit(solution)/shard_map/ppermute | solution.py:235
  7.5 2.4 %collective-permute-start.1 = (bf16[528,256]{1,0:T(8,128)(2,1)S(1)}, bf16[528,256]{1,0:T(8,128)(2,1)S(1)}, u32[]{:S(2)}, u32[]{:S(2)}) collective-permute-start(bf16[528,256]{1,0:T(8,128)(2,1)S(1)} %fusion.1), channel_id=1, source_target_pairs={{0,2},{1,3},{2,0},{3,1},{4,6},{5,7},{6,4},{7,5},{8,10},{9,11},{10,... | collective-permute-start | bytes 811016 | tf_op jit(solution)/shard_map/ppermute | solution.py:235
  10.0 2.5 %collective-permute-start = (bf16[528,256]{1,0:T(8,128)(2,1)S(1)}, bf16[528,256]{1,0:T(8,128)(2,1)S(1)}, u32[]{:S(2)}, u32[]{:S(2)}) collective-permute-start(bf16[528,256]{1,0:T(8,128)(2,1)S(1)} %fusion.1), channel_id=1, source_target_pairs={{0,1},{1,2},{2,3},{3,0},{4,5},{5,6},{6,7},{7,4},{8,9},{9,10},{10,1... | collective-permute-start | bytes 811016 | tf_op jit(solution)/shard_map/ppermute | solution.py:235
  12.5 2.6 %constant_dynamic-slice_fusion.4 = (bf16[4,4,128,128]{3,2,1,0:T(8,128)(2,1)}, bf16[4,4,128,128]{3,2,1,0:T(8,128)(2,1)}, bf16[4,4,128,128]{3,2,1,0:T(8,128)(2,1)}) fusion(bf16[16,4,128,128]{3,2,1,0:T(8,128)(2,1)} %own_tiles.1, s32[]{:T(128)S(6)} %select_n.60, s32[]{:T(128)S(6)} %select_n.58, s32[]{:T(128)S(6)} %select_n.56), kind=kLoop, calls=%fused_computation.19 | loop fusion | bytes 3145740 | tf_op jit(solution)/shard_map/dynamic_slice | solution.py:264
  15.1 3.6 %collective-permute-start.3 = (bf16[4,4,128,128]{3,2,1,0:T(8,128)(2,1)}, bf16[4,4,128,128]{3,2,1,0:T(8,128)(2,1)}, u32[]{:S(2)}, u32[]{:S(2)}) collective-permute-start(bf16[4,4,128,128]{3,2,1,0:T(8,128)(2,1)} %get-tuple-element.29), channel_id=1, source_target_pairs={{0,1},{1,2},{2,3},{3,0},{4,5},{5,6},{6,7},{7,4},{8,9},{9,10},{10,1... | collective-permute-start | bytes 1572872 | tf_op jit(solution)/shard_map/ppermute | solution.py:235
  18.7 3.1 %collective-permute-start.4 = (bf16[4,4,128,128]{3,2,1,0:T(8,128)(2,1)}, bf16[4,4,128,128]{3,2,1,0:T(8,128)(2,1)}, u32[]{:S(2)}, u32[]{:S(2)}) collective-permute-start(bf16[4,4,128,128]{3,2,1,0:T(8,128)(2,1)} %get-tuple-element.28), channel_id=1, source_target_pairs={{0,3},{1,0},{2,1},{3,2},{4,7},{5,4},{6,5},{7,6},{8,11},{9,8},{10,9... | collective-permute-start | bytes 1572872 | tf_op jit(solution)/shard_map/ppermute | solution.py:235
  24.7 7.1 %collective-permute-start.7 = (bf16[2048,256]{1,0:T(8,128)(2,1)S(1)}, bf16[2048,256]{1,0:T(8,128)(2,1)}, u32[]{:S(2)}, u32[]{:S(2)}) collective-permute-start(bf16[2048,256]{1,0:T(8,128)(2,1)S(1)} %pad_maximum_fusion.own), channel_id=1, source_target_pairs={{0,4},{4,8},{8,12},{12,16},{16,20},{20,24},{24,28},{28,32},{32,36}... | collective-permute-start | bytes 3145736 | tf_op jit(solution)/shard_map/ppermute | solution.py:276
  31.8 3.0 %collective-permute-start.8 = (bf16[2048,256]{1,0:T(8,128)(2,1)S(1)}, bf16[2048,256]{1,0:T(8,128)(2,1)}, u32[]{:S(2)}, u32[]{:S(2)}) collective-permute-start(bf16[2048,256]{1,0:T(8,128)(2,1)S(1)} %pad_maximum_fusion.own), channel_id=1, source_target_pairs={{4,0},{8,4},{12,8},{16,12},{20,16},{24,20},{28,24},{32,28},{36,32}... | collective-permute-start | bytes 3145736 | tf_op jit(solution)/shard_map/ppermute | solution.py:277
  34.8 3.7 %collective-permute-start.5 = (bf16[4,4,128,128]{3,2,1,0:T(8,128)(2,1)}, bf16[4,4,128,128]{3,2,1,0:T(8,128)(2,1)S(1)}, u32[]{:S(2)}, u32[]{:S(2)}) collective-permute-start(bf16[4,4,128,128]{3,2,1,0:T(8,128)(2,1)} %get-tuple-element.17), channel_id=1, source_target_pairs={{0,2},{1,3},{2,0},{3,1},{4,6},{5,7},{6,4},{7,5},{8,10},{9,11},{10,... | collective-permute-start | bytes 1572872 | tf_op jit(solution)/shard_map/ppermute | solution.py:235
  38.5 1.9 %collective-permute-start.6 = (bf16[4,4,128,128]{3,2,1,0:T(8,128)(2,1)}, bf16[4,4,128,128]{3,2,1,0:T(8,128)(2,1)S(1)}, u32[]{:S(2)}, u32[]{:S(2)}) collective-permute-start(bf16[4,4,128,128]{3,2,1,0:T(8,128)(2,1)} %collective-permute-done.3.tiles_a), channel_id=1, source_target_pairs={{0,4},{4,0},{8,12},{12,8},{16,20},{20,16},{24,28},{28,24},{32,36},... | collective-permute-start | bytes 1572872 | tf_op jit(solution)/shard_map/ppermute | solution.py:240
  40.5 0.7 fusion.7
  41.3 10.7 %collective-permute-done.5.tiles_b = bf16[4,4,128,128]{3,2,1,0:T(8,128)(2,1)S(1)} collective-permute-done((bf16[4,4,128,128]{3,2,1,0:T(8,128)(2,1)}, bf16[4,4,128,128]{3,2,1,0:T(8,128)(2,1)S(1)}, u32[]{:S(2)}, u32[]{:S(2)}) %collective-permute-start.5) | collective-permute-done | bytes 524320 | tf_op jit(solution)/shard_map/ppermute | solution.py:235
  52.0 3.4 %shard_map.102 = (f32[2,128,256]{2,1,0:T(8,128)S(1)}, f32[2,128,256]{2,1,0:T(8,128)S(1)}) custom-call(s32[4]{0:T(128)S(1)} %get-tuple-element.34.info, s32[16,16]{1,0:T(8,128)S(1)} %maximum_convert_fusion.cols, s32[16]{0:T(128)S(1)} %copy-done.1, bf16[16,4,128,128]{3,2,1,0:T(8,128)(2,1)S(1)} %copy-done, ...), custom_call_target="tpu_custom_call" | custom-call | flops 540000000 | bytes 6000000 | tf_op jit(solution)/shard_map/pallas_call | solution.py:94
  55.5 2.3 %collective-permute-start.9 = (f32[2,128,256]{2,1,0:T(8,128)S(1)}, f32[2,128,256]{2,1,0:T(8,128)S(1)}, u32[]{:S(2)}, u32[]{:S(2)}) collective-permute-start(f32[2,128,256]{2,1,0:T(8,128)S(1)} %get-tuple-element.21), channel_id=1, source_target_pairs={{0,4},{4,0},{8,12},{12,8},{16,20},{20,16},{24,28},{28,24},{32,36},... | collective-permute-start | bytes 786440 | tf_op jit(solution)/shard_map/ppermute | solution.py:240
  58.9 4.9 %shard_map.103 = (f32[1,128,256]{2,1,0:T(8,128)S(1)}, f32[1,128,256]{2,1,0:T(8,128)S(1)}) custom-call(f32[2,128,256]{2,1,0:T(8,128)S(1)} %get-tuple-element.20.refs_0_.own, f32[2,128,256]{2,1,0:T(8,128)S(1)} %collective-permute-done.9.refs_1_.other, bf16[2,128,256]{2,1,0:T(8,128)(2,1)S(1)} %fusion.2.refs_2_), custom_call_target="tpu_custom_call" | custom-call | flops 80000000 | bytes 1200000 | tf_op jit(solution)/shard_map/pallas_call | solution.py:199
  63.8 3.3 %collective-permute-start.10 = (f32[1,128,256]{2,1,0:T(8,128)S(1)}, f32[1,128,256]{2,1,0:T(8,128)S(1)}, u32[]{:S(2)}, u32[]{:S(2)}) collective-permute-start(f32[1,128,256]{2,1,0:T(8,128)S(1)} %get-tuple-element.22.refs_0_), channel_id=1, source_target_pairs={{0,8},{4,12},{8,0},{12,4},{16,24},{20,28},{24,16},{28,20},{32,40},... | collective-permute-start | bytes 393224 | tf_op jit(solution)/shard_map/ppermute | solution.py:240
  67.9 2.5 %collective-permute-done.10.refs_1_.other = f32[1,128,256]{2,1,0:T(8,128)S(1)} collective-permute-done((f32[1,128,256]{2,1,0:T(8,128)S(1)}, f32[1,128,256]{2,1,0:T(8,128)S(1)}, u32[]{:S(2)}, u32[]{:S(2)}) %collective-permute-start.10) | collective-permute-done | bytes 131104 | tf_op jit(solution)/shard_map/ppermute | solution.py:240
  70.4 4.0 %shard_map.105.refs_0_.refs_1_ = f32[1,128,256]{2,1,0:T(8,128)S(1)} custom-call(f32[1,128,256]{2,1,0:T(8,128)S(1)} %get-tuple-element.23.refs_1_.refs_0_.own, f32[1,128,256]{2,1,0:T(8,128)S(1)} %collective-permute-done.10.refs_1_.other, bf16[1,128,256]{2,1,0:T(8,128)(2,1)S(1)} %fusion.3.refs_2_), custom_call_target="tpu_custom_call" | custom-call | flops 40000000 | bytes 600000 | tf_op jit(solution)/shard_map/pallas_call | solution.py:199
  74.4 6.1 %collective-permute-start.11 = (f32[1,128,256]{2,1,0:T(8,128)S(1)}, f32[1,128,256]{2,1,0:T(8,128)S(1)}, u32[]{:S(2)}, u32[]{:S(2)}) collective-permute-start(f32[1,128,256]{2,1,0:T(8,128)S(1)} %shard_map.105.refs_0_.refs_1_), channel_id=1, source_target_pairs={{0,16},{4,20},{8,24},{12,28},{16,0},{20,4},{24,8},{28,12},{32,48},... | collective-permute-start | bytes 393224 | tf_op jit(solution)/shard_map/ppermute | solution.py:240
  80.6 1.6 %shard_map.104 = f32[1,2,256,128]{3,2,1,0:T(8,128)} custom-call(s32[4]{0:T(128)S(1)} %get-tuple-element.34.info, f32[2,128,256]{2,1,0:T(8,128)S(1)} %get-tuple-element.20.refs_0_.own, f32[2,128,256]{2,1,0:T(8,128)S(1)} %collective-permute-done.9.refs_1_.other, f32[1,128,256]{2,1,0:T(8,128)S(1)} %get-tuple-element.22.refs_0_, ...), custom_call_target="tpu_custom_call" | custom-call | flops 100000000 | bytes 1200000 | tf_op jit(solution)/shard_map/pallas_call | solution.py:221
  82.2 1.5 %shard_map.106 = f32[1,1,256,128]{3,2,1,0:T(8,128)} custom-call(s32[4]{0:T(128)S(1)} %get-tuple-element.33.info, f32[1,128,256]{2,1,0:T(8,128)S(1)} %get-tuple-element.23.refs_1_.refs_0_.own, f32[1,128,256]{2,1,0:T(8,128)S(1)} %collective-permute-done.10.refs_1_.other, f32[1,128,256]{2,1,0:T(8,128)S(1)} %shard_map.105.refs_0_.refs_1_), custom_call_target="tpu_custom_call" | custom-call | flops 50000000 | bytes 600000 | tf_op jit(solution)/shard_map/pallas_call | solution.py:221
  83.7 2.8 %collective-permute-done.11.refs_2_ = f32[1,128,256]{2,1,0:T(8,128)S(1)} collective-permute-done((f32[1,128,256]{2,1,0:T(8,128)S(1)}, f32[1,128,256]{2,1,0:T(8,128)S(1)}, u32[]{:S(2)}, u32[]{:S(2)}) %collective-permute-start.11) | collective-permute-done | bytes 131104 | tf_op jit(solution)/shard_map/ppermute | solution.py:240
  86.5 5.5 %shard_map.107 = (f32[1,128,256]{2,1,0:T(8,128)}, f32[1,1,256,128]{3,2,1,0:T(8,128)}) custom-call(s32[4]{0:T(128)S(1)} %get-tuple-element.26.refs_0_, f32[1,128,256]{2,1,0:T(8,128)S(1)} %shard_map.105.refs_0_.refs_1_, f32[1,128,256]{2,1,0:T(8,128)S(1)} %collective-permute-done.11.refs_2_, bf16[1,128,256]{2,1,0:T(8,128)(2,1)S(1)} %fusion.4.refs_3_), custom_call_target="tpu_custom_call" | custom-call | flops 40000000 | bytes 600000 | tf_op jit(solution)/shard_map/pallas_call | solution.py:199
  (36 shorter events, 5.7 us)
Async XLA Ops:
  2.3 19.5 %collective-permute-start.2 = (bf16[528,256]{1,0:T(8,128)(2,1)S(1)}, bf16[528,256]{1,0:T(8,128)(2,1)S(1)}, u32[]{:S(2)}, u32[]{:S(2)}) collective-permute-start(bf16[528,256]{1,0:T(8,128)(2,1)S(1)} %fusion.1), channel_id=1, source_target_pairs={{0,3},{1,0},{2,1},{3,2},{4,7},{5,4},{6,5},{7,6},{8,11},{9,8},{10,9... | collective-permute-start | bytes 811016 | tf_op jit(solution)/shard_map/ppermute | solution.py:235
  7.5 14.3 %collective-permute-start.1 = (bf16[528,256]{1,0:T(8,128)(2,1)S(1)}, bf16[528,256]{1,0:T(8,128)(2,1)S(1)}, u32[]{:S(2)}, u32[]{:S(2)}) collective-permute-start(bf16[528,256]{1,0:T(8,128)(2,1)S(1)} %fusion.1), channel_id=1, source_target_pairs={{0,2},{1,3},{2,0},{3,1},{4,6},{5,7},{6,4},{7,5},{8,10},{9,11},{10,... | collective-permute-start | bytes 811016 | tf_op jit(solution)/shard_map/ppermute | solution.py:235
  10.0 12.2 %collective-permute-start = (bf16[528,256]{1,0:T(8,128)(2,1)S(1)}, bf16[528,256]{1,0:T(8,128)(2,1)S(1)}, u32[]{:S(2)}, u32[]{:S(2)}) collective-permute-start(bf16[528,256]{1,0:T(8,128)(2,1)S(1)} %fusion.1), channel_id=1, source_target_pairs={{0,1},{1,2},{2,3},{3,0},{4,5},{5,6},{6,7},{7,4},{8,9},{9,10},{10,1... | collective-permute-start | bytes 811016 | tf_op jit(solution)/shard_map/ppermute | solution.py:235
  12.5 10.7 %copy-start.2 = (bf16[512,256]{1,0:T(8,128)(2,1)S(1)}, bf16[512,256]{1,0:T(8,128)(2,1)}, u32[]{:S(2)}) copy-start(bf16[512,256]{1,0:T(8,128)(2,1)} %param.7) | copy-start | bytes 786436
  15.1 36.9 %copy-start = (bf16[16,4,128,128]{3,2,1,0:T(8,128)(2,1)S(1)}, bf16[16,4,128,128]{3,2,1,0:T(8,128)(2,1)}, u32[]{:S(2)}) copy-start(bf16[16,4,128,128]{3,2,1,0:T(8,128)(2,1)} %own_tiles.1) | copy-start | bytes 6291460
  15.1 36.9 %copy-start.1 = (s32[16]{0:T(128)S(1)}, s32[16]{0:T(128)}, u32[]{:S(2)}) copy-start(s32[16]{0:T(128)} %counts.1) | copy-start | bytes 196
  15.1 23.3 %collective-permute-start.3 = (bf16[4,4,128,128]{3,2,1,0:T(8,128)(2,1)}, bf16[4,4,128,128]{3,2,1,0:T(8,128)(2,1)}, u32[]{:S(2)}, u32[]{:S(2)}) collective-permute-start(bf16[4,4,128,128]{3,2,1,0:T(8,128)(2,1)} %get-tuple-element.29), channel_id=1, source_target_pairs={{0,1},{1,2},{2,3},{3,0},{4,5},{5,6},{6,7},{7,4},{8,9},{9,10},{10,1... | collective-permute-start | bytes 1572872 | tf_op jit(solution)/shard_map/ppermute | solution.py:235
  18.7 19.8 %collective-permute-start.4 = (bf16[4,4,128,128]{3,2,1,0:T(8,128)(2,1)}, bf16[4,4,128,128]{3,2,1,0:T(8,128)(2,1)}, u32[]{:S(2)}, u32[]{:S(2)}) collective-permute-start(bf16[4,4,128,128]{3,2,1,0:T(8,128)(2,1)} %get-tuple-element.28), channel_id=1, source_target_pairs={{0,3},{1,0},{2,1},{3,2},{4,7},{5,4},{6,5},{7,6},{8,11},{9,8},{10,9... | collective-permute-start | bytes 1572872 | tf_op jit(solution)/shard_map/ppermute | solution.py:235
  21.8 0.7 copy-start.3
  22.5 0.7 copy-start.4
  24.7 27.4 %collective-permute-start.7 = (bf16[2048,256]{1,0:T(8,128)(2,1)S(1)}, bf16[2048,256]{1,0:T(8,128)(2,1)}, u32[]{:S(2)}, u32[]{:S(2)}) collective-permute-start(bf16[2048,256]{1,0:T(8,128)(2,1)S(1)} %pad_maximum_fusion.own), channel_id=1, source_target_pairs={{0,4},{4,8},{8,12},{12,16},{16,20},{20,24},{24,28},{28,32},{32,36}... | collective-permute-start | bytes 3145736 | tf_op jit(solution)/shard_map/ppermute | solution.py:276
  31.8 20.3 %collective-permute-start.8 = (bf16[2048,256]{1,0:T(8,128)(2,1)S(1)}, bf16[2048,256]{1,0:T(8,128)(2,1)}, u32[]{:S(2)}, u32[]{:S(2)}) collective-permute-start(bf16[2048,256]{1,0:T(8,128)(2,1)S(1)} %pad_maximum_fusion.own), channel_id=1, source_target_pairs={{4,0},{8,4},{12,8},{16,12},{20,16},{24,20},{28,24},{32,28},{36,32}... | collective-permute-start | bytes 3145736 | tf_op jit(solution)/shard_map/ppermute | solution.py:277
  34.8 17.2 %collective-permute-start.5 = (bf16[4,4,128,128]{3,2,1,0:T(8,128)(2,1)}, bf16[4,4,128,128]{3,2,1,0:T(8,128)(2,1)S(1)}, u32[]{:S(2)}, u32[]{:S(2)}) collective-permute-start(bf16[4,4,128,128]{3,2,1,0:T(8,128)(2,1)} %get-tuple-element.17), channel_id=1, source_target_pairs={{0,2},{1,3},{2,0},{3,1},{4,6},{5,7},{6,4},{7,5},{8,10},{9,11},{10,... | collective-permute-start | bytes 1572872 | tf_op jit(solution)/shard_map/ppermute | solution.py:235
  38.5 13.5 %collective-permute-start.6 = (bf16[4,4,128,128]{3,2,1,0:T(8,128)(2,1)}, bf16[4,4,128,128]{3,2,1,0:T(8,128)(2,1)S(1)}, u32[]{:S(2)}, u32[]{:S(2)}) collective-permute-start(bf16[4,4,128,128]{3,2,1,0:T(8,128)(2,1)} %collective-permute-done.3.tiles_a), channel_id=1, source_target_pairs={{0,4},{4,0},{8,12},{12,8},{16,20},{20,16},{24,28},{28,24},{32,36},... | collective-permute-start | bytes 1572872 | tf_op jit(solution)/shard_map/ppermute | solution.py:240
  55.5 3.5 %collective-permute-start.9 = (f32[2,128,256]{2,1,0:T(8,128)S(1)}, f32[2,128,256]{2,1,0:T(8,128)S(1)}, u32[]{:S(2)}, u32[]{:S(2)}) collective-permute-start(f32[2,128,256]{2,1,0:T(8,128)S(1)} %get-tuple-element.21), channel_id=1, source_target_pairs={{0,4},{4,0},{8,12},{12,8},{16,20},{20,16},{24,28},{28,24},{32,36},... | collective-permute-start | bytes 786440 | tf_op jit(solution)/shard_map/ppermute | solution.py:240
  63.8 6.6 %collective-permute-start.10 = (f32[1,128,256]{2,1,0:T(8,128)S(1)}, f32[1,128,256]{2,1,0:T(8,128)S(1)}, u32[]{:S(2)}, u32[]{:S(2)}) collective-permute-start(f32[1,128,256]{2,1,0:T(8,128)S(1)} %get-tuple-element.22.refs_0_), channel_id=1, source_target_pairs={{0,8},{4,12},{8,0},{12,4},{16,24},{20,28},{24,16},{28,20},{32,40},... | collective-permute-start | bytes 393224 | tf_op jit(solution)/shard_map/ppermute | solution.py:240
  74.4 12.1 %collective-permute-start.11 = (f32[1,128,256]{2,1,0:T(8,128)S(1)}, f32[1,128,256]{2,1,0:T(8,128)S(1)}, u32[]{:S(2)}, u32[]{:S(2)}) collective-permute-start(f32[1,128,256]{2,1,0:T(8,128)S(1)} %shard_map.105.refs_0_.refs_1_), channel_id=1, source_target_pairs={{0,16},{4,20},{8,24},{12,28},{16,0},{20,4},{24,8},{28,12},{32,48},... | collective-permute-start | bytes 393224 | tf_op jit(solution)/shard_map/ppermute | solution.py:240

commit v6 on v5

--- a/solution.py
+++ b/solution.py
@@ -10,7 +10,7 @@
 RIDGE = 0.25
 BF = jnp.bfloat16
 F32 = jnp.float32
-PANEL = 16
+PANEL = 32
 
 
 def dot(a, b, ca, cb):
@@ -108,40 +108,47 @@
     )(info, cols, counts, own_tiles, *received, before, own, after)
 
 
-def eliminate(j, gram, rhs):
-    base = j * PANEL
-    half = PANEL // 2
-    rows = lax.broadcasted_iota(jnp.int32, (half, 128), 0)
-    a = [gram[base + half * h : base + half * (h + 1), :] for h in range(2)]
-    body = [
-        [a[h]] + [rhs[base + half * h : base + half * (h + 1), 128 * c : 128 * (c + 1)] for c in range(2)]
-        for h in range(2)
-    ]
-    column = [
-        [jnp.broadcast_to(a[h][:, base + k : base + k + 1], (half, 128)) for k in range(PANEL)]
-        for h in range(2)
-    ]
-    scale = [jnp.zeros((half, 128), F32) for _ in range(2)]
-    for i in range(PANEL):
-        h0, r = divmod(i, half)
-        pivot = column[h0][i][r : r + 1, :]
-        inverse = lax.rsqrt(pivot)
+def sweep(body, lane, first, rows):
+    column = {
+        h: [jnp.broadcast_to(body[h][0][:, lane + k : lane + k + 1], (8, 128)) for k in range(16)]
+        for h in range(first, len(body))
+    }
+    scale = [jnp.zeros((8, 128), F32) for _ in range(2)]
+    for i in range(16):
+        low, r = divmod(i, 8)
+        h0 = first + low
+        inverse = lax.rsqrt(column[h0][i][r : r + 1, :])
         reciprocal = inverse * inverse
-        scale[h0] = jnp.where(rows == r, jnp.broadcast_to(inverse, (half, 128)), scale[h0])
+        scale[low] = jnp.where(rows == r, jnp.broadcast_to(inverse, (8, 128)), scale[low])
         factor = {}
-        for h in range(h0, 2):
+        for h in range(h0, len(body)):
             value = column[h][i] * reciprocal
             factor[h] = jnp.where(rows > r, value, 0.0) if h == h0 else value
-        for k in range(i + 1, PANEL):
+        for k in range(i + 1, 16):
             row = column[h0][k][r : r + 1, :]
-            for h in range(h0, 2):
+            for h in range(h0, len(body)):
                 column[h][k] = column[h][k] - factor[h] * row
         for c in range(3):
             row = body[h0][c][r : r + 1, :]
-            for h in range(h0, 2):
+            for h in range(h0, len(body)):
                 body[h][c] = body[h][c] - factor[h] * row
+    return scale
+
+
+def eliminate(j, gram, rhs):
+    base = j * PANEL
+    halves = PANEL // 8
+    rows = lax.broadcasted_iota(jnp.int32, (8, 128), 0)
+    body = [
+        [gram[base + 8 * h : base + 8 * (h + 1), :]]
+        + [rhs[base + 8 * h : base + 8 * (h + 1), 128 * c : 128 * (c + 1)] for c in range(2)]
+        for h in range(halves)
+    ]
+    scale = []
+    for first in range(0, halves, 2):
+        scale += sweep(body, base + 8 * first, first, rows)
     return jnp.concatenate(
-        [jnp.concatenate([body[h][c] * scale[h] for c in range(3)], axis=1) for h in range(2)],
+        [jnp.concatenate([part * scale[h] for part in body[h]], axis=1) for h in range(halves)],
         axis=0,
     )
 
@@ -180,9 +187,9 @@
             rows = eliminate(j, gram.at[m], outs[m].at[0])
             outs[m][0, j * PANEL : done, :] = rows[:, 128:]
             if done < 128:
-                hi, mid, lo = split3(rows)
-                left = jnp.concatenate([hi, hi, mid, mid, hi, lo], axis=0)[:, :128]
-                right = jnp.concatenate([hi, mid, hi, mid, lo, hi], axis=0)
+                hi, mid = split2(rows)
+                left = jnp.concatenate([hi, hi, mid, mid], axis=0)[:, :128]
+                right = jnp.concatenate([hi, mid, hi, mid], axis=0)
                 update = dot(left, right, 0, 0)
                 gram[m, done:, :] = gram[m, done:, :] - update[done:, :128]
                 outs[m][0, done:, :] = outs[m][0, done:, :] - update[done:, 128:]
@@ -268,8 +275,8 @@
     tiles_one, tiles_three = lax.optimization_barrier((tiles_one, tiles_three))
     tie = swapped(tiles_one, 1)
     own = jnp.concatenate([samples] + [part[:512] for part in (by_one, by_two, by_three)], axis=0)
-    cols = jnp.concatenate([part[512:516, :16] for part in (block, by_one, by_two, by_three)])
-    own, two, cols = lax.optimization_barrier((own, two, cols.astype(jnp.int32)))
+    cols = jnp.concatenate([part[512:516, :16] for part in (block, by_one, by_two, by_three)]).astype(jnp.int32)
+    own, two = lax.optimization_barrier((own, two))
     received = [tiles_one, shifted(two, "cols", 2), tiles_three, tie]
     leaves = lax.axis_size("leaf")
     rising = [(i, i + 1) for i in range(leaves - 1)]

time: 92.6 us -> 90.3 us (0.975)
  waiting for transfers between devices: 16.7 us -> 15.1 us
  Pallas kernels: 20.9 us -> 19.8 us
    ppermute x6, waiting for transfers between devices: 11 us -> 9.64 us  [shifted(): lax.ppermute(value, axis, [(i, (i + by) % count) for i in range(count)])]
    pallas_call x3, Pallas kernels: 14.3 us -> 13.3 us  [merge(): pl.pallas_call(functools.partial(merge_kernel, nodes, last), out_shape=tu...]
where the time goes in v6:
time: 90.3 us; the launch traced here: 89.6 us
  starting transfers between devices  44.3 us (49%)
  Pallas kernels  19.8 us (22%)
  waiting for transfers between devices  15.1 us (17%)
  local copies, waits for them, and re-layouts  5.89 us (7%)
  other arithmetic  3.58 us (4%)
  between operations  0.97 us (1%)
    ppermute x6, starting transfers between devices, shifted(): lax.ppermute(value, axis, [(i, (i + by) % count) for i in range(count)])  20.5 us
    ppermute x4, starting transfers between devices, swapped(): return lax.ppermute(value, 'leaf', [(i, i ^ apart) for i in range(count)])  13.8 us
    pallas_call x3, Pallas kernels, merge(): pl.pallas_call(functools.partial(merge_kernel, nodes, last), out_shape=tu...  13.3 us
    ppermute x6, waiting for transfers between devices, shifted(): lax.ppermute(value, axis, [(i, (i + by) % count) for i in range(count)])  9.64 us
    ppermute x1, starting transfers between devices, local(): before = lax.ppermute(own, 'leaf', rising)  7.05 us
    ppermute x4, waiting for transfers between devices, swapped(): return lax.ppermute(value, 'leaf', [(i, i ^ apart) for i in range(count)])  5.47 us
    pallas_call x1, Pallas kernels, near(): pl.pallas_call(near_kernel, out_shape=(block, block), in_specs=[SMEM] * 3...  3.42 us
    pallas_call x2, Pallas kernels, transfer(): pl.pallas_call(functools.partial(transfer_kernel, nodes), out_shape=jax.S...  3.09 us
  transfers between devices with their start and end apart: 12, of which 5 were waited for; matrix products, arithmetic and copies ran while one was open for 7% of the time, Pallas kernels for 3%

profile of v6, /device:TPU:1, one launch (start us, length us, event | category | flops | bytes accessed | tf_op | source)
XLA Modules:
  0.0 89.6 jit_solution(14913402808603297194)
XLA Ops:
  1.3 1.0 %fusion.1 = bf16[528,256]{1,0:T(8,128)(2,1)S(1)} fusion(bf16[4,16]{1,0:T(4,128)(2,1)S(1)} %fusion.6, bf16[512,256]{1,0:T(8,128)(2,1)} %param.7), kind=kLoop, calls=%fused_computation.3 | loop fusion | flops 811008 | bytes 532608 | tf_op jit(solution)/shard_map/concatenate | solution.py:268
  2.3 5.2 %collective-permute-start.2 = (bf16[528,256]{1,0:T(8,128)(2,1)S(1)}, bf16[528,256]{1,0:T(8,128)(2,1)S(1)}, u32[]{:S(2)}, u32[]{:S(2)}) collective-permute-start(bf16[528,256]{1,0:T(8,128)(2,1)S(1)} %fusion.1), channel_id=1, source_target_pairs={{0,3},{1,0},{2,1},{3,2},{4,7},{5,4},{6,5},{7,6},{8,11},{9,8},{10,9... | collective-permute-start | bytes 811016 | tf_op jit(solution)/shard_map/ppermute | solution.py:242
  7.5 2.4 %collective-permute-start.1 = (bf16[528,256]{1,0:T(8,128)(2,1)S(1)}, bf16[528,256]{1,0:T(8,128)(2,1)S(1)}, u32[]{:S(2)}, u32[]{:S(2)}) collective-permute-start(bf16[528,256]{1,0:T(8,128)(2,1)S(1)} %fusion.1), channel_id=1, source_target_pairs={{0,2},{1,3},{2,0},{3,1},{4,6},{5,7},{6,4},{7,5},{8,10},{9,11},{10,... | collective-permute-start | bytes 811016 | tf_op jit(solution)/shard_map/ppermute | solution.py:242
  10.0 2.5 %collective-permute-start = (bf16[528,256]{1,0:T(8,128)(2,1)S(1)}, bf16[528,256]{1,0:T(8,128)(2,1)S(1)}, u32[]{:S(2)}, u32[]{:S(2)}) collective-permute-start(bf16[528,256]{1,0:T(8,128)(2,1)S(1)} %fusion.1), channel_id=1, source_target_pairs={{0,1},{1,2},{2,3},{3,0},{4,5},{5,6},{6,7},{7,4},{8,9},{9,10},{10,1... | collective-permute-start | bytes 811016 | tf_op jit(solution)/shard_map/ppermute | solution.py:242
  12.5 2.6 %constant_dynamic-slice_fusion.4 = (bf16[4,4,128,128]{3,2,1,0:T(8,128)(2,1)}, bf16[4,4,128,128]{3,2,1,0:T(8,128)(2,1)}, bf16[4,4,128,128]{3,2,1,0:T(8,128)(2,1)}) fusion(bf16[16,4,128,128]{3,2,1,0:T(8,128)(2,1)} %own_tiles.1, s32[]{:T(128)S(6)} %select_n.60, s32[]{:T(128)S(6)} %select_n.58, s32[]{:T(128)S(6)} %select_n.56), kind=kLoop, calls=%fused_computation.19 | loop fusion | bytes 3145740 | tf_op jit(solution)/shard_map/dynamic_slice | solution.py:271
  15.2 3.6 %collective-permute-start.3 = (bf16[4,4,128,128]{3,2,1,0:T(8,128)(2,1)}, bf16[4,4,128,128]{3,2,1,0:T(8,128)(2,1)}, u32[]{:S(2)}, u32[]{:S(2)}) collective-permute-start(bf16[4,4,128,128]{3,2,1,0:T(8,128)(2,1)} %get-tuple-element.28), channel_id=1, source_target_pairs={{0,1},{1,2},{2,3},{3,0},{4,5},{5,6},{6,7},{7,4},{8,9},{9,10},{10,1... | collective-permute-start | bytes 1572872 | tf_op jit(solution)/shard_map/ppermute | solution.py:242
  18.7 3.1 %collective-permute-start.4 = (bf16[4,4,128,128]{3,2,1,0:T(8,128)(2,1)}, bf16[4,4,128,128]{3,2,1,0:T(8,128)(2,1)}, u32[]{:S(2)}, u32[]{:S(2)}) collective-permute-start(bf16[4,4,128,128]{3,2,1,0:T(8,128)(2,1)} %get-tuple-element.27), channel_id=1, source_target_pairs={{0,3},{1,0},{2,1},{3,2},{4,7},{5,4},{6,5},{7,6},{8,11},{9,8},{10,9... | collective-permute-start | bytes 1572872 | tf_op jit(solution)/shard_map/ppermute | solution.py:242
  22.5 0.7 copy-done.4
  23.4 7.1 %collective-permute-start.7 = (bf16[2048,256]{1,0:T(8,128)(2,1)S(1)}, bf16[2048,256]{1,0:T(8,128)(2,1)}, u32[]{:S(2)}, u32[]{:S(2)}) collective-permute-start(bf16[2048,256]{1,0:T(8,128)(2,1)S(1)} %pad_maximum_fusion.own), channel_id=1, source_target_pairs={{0,4},{4,8},{8,12},{12,16},{16,20},{20,24},{24,28},{28,32},{32,36}... | collective-permute-start | bytes 3145736 | tf_op jit(solution)/shard_map/ppermute | solution.py:283
  30.4 3.0 %collective-permute-start.8 = (bf16[2048,256]{1,0:T(8,128)(2,1)S(1)}, bf16[2048,256]{1,0:T(8,128)(2,1)}, u32[]{:S(2)}, u32[]{:S(2)}) collective-permute-start(bf16[2048,256]{1,0:T(8,128)(2,1)S(1)} %pad_maximum_fusion.own), channel_id=1, source_target_pairs={{4,0},{8,4},{12,8},{16,12},{20,16},{24,20},{28,24},{32,28},{36,32}... | collective-permute-start | bytes 3145736 | tf_op jit(solution)/shard_map/ppermute | solution.py:284
  33.5 3.7 %collective-permute-start.5 = (bf16[4,4,128,128]{3,2,1,0:T(8,128)(2,1)}, bf16[4,4,128,128]{3,2,1,0:T(8,128)(2,1)S(1)}, u32[]{:S(2)}, u32[]{:S(2)}) collective-permute-start(bf16[4,4,128,128]{3,2,1,0:T(8,128)(2,1)} %get-tuple-element.15), channel_id=1, source_target_pairs={{0,2},{1,3},{2,0},{3,1},{4,6},{5,7},{6,4},{7,5},{8,10},{9,11},{10,... | collective-permute-start | bytes 1572872 | tf_op jit(solution)/shard_map/ppermute | solution.py:242
  37.3 1.9 %collective-permute-start.6 = (bf16[4,4,128,128]{3,2,1,0:T(8,128)(2,1)}, bf16[4,4,128,128]{3,2,1,0:T(8,128)(2,1)S(1)}, u32[]{:S(2)}, u32[]{:S(2)}) collective-permute-start(bf16[4,4,128,128]{3,2,1,0:T(8,128)(2,1)} %collective-permute-done.3.tiles_a), channel_id=1, source_target_pairs={{0,4},{4,0},{8,12},{12,8},{16,20},{20,16},{24,28},{28,24},{32,36},... | collective-permute-start | bytes 1572872 | tf_op jit(solution)/shard_map/ppermute | solution.py:247
  41.4 9.4 %collective-permute-done.5.tiles_b = bf16[4,4,128,128]{3,2,1,0:T(8,128)(2,1)S(1)} collective-permute-done((bf16[4,4,128,128]{3,2,1,0:T(8,128)(2,1)}, bf16[4,4,128,128]{3,2,1,0:T(8,128)(2,1)S(1)}, u32[]{:S(2)}, u32[]{:S(2)}) %collective-permute-start.5) | collective-permute-done | bytes 524320 | tf_op jit(solution)/shard_map/ppermute | solution.py:242
  50.8 3.4 %shard_map.102 = (f32[2,128,256]{2,1,0:T(8,128)S(1)}, f32[2,128,256]{2,1,0:T(8,128)S(1)}) custom-call(s32[4]{0:T(128)S(1)} %get-tuple-element.32.info, s32[16,16]{1,0:T(8,128)S(1)} %maximum_convert_fusion.cols, s32[16]{0:T(128)S(1)} %copy-done.1, bf16[16,4,128,128]{3,2,1,0:T(8,128)(2,1)S(1)} %copy-done, ...), custom_call_target="tpu_custom_call" | custom-call | flops 540000000 | bytes 6000000 | tf_op jit(solution)/shard_map/pallas_call | solution.py:94
  54.2 2.3 %collective-permute-start.9 = (f32[2,128,256]{2,1,0:T(8,128)S(1)}, f32[2,128,256]{2,1,0:T(8,128)S(1)}, u32[]{:S(2)}, u32[]{:S(2)}) collective-permute-start(f32[2,128,256]{2,1,0:T(8,128)S(1)} %get-tuple-element.19), channel_id=1, source_target_pairs={{0,4},{4,0},{8,12},{12,8},{16,20},{20,16},{24,28},{28,24},{32,36},... | collective-permute-start | bytes 786440 | tf_op jit(solution)/shard_map/ppermute | solution.py:247
  57.7 4.8 %shard_map.103 = (f32[1,128,256]{2,1,0:T(8,128)S(1)}, f32[1,128,256]{2,1,0:T(8,128)S(1)}) custom-call(f32[2,128,256]{2,1,0:T(8,128)S(1)} %get-tuple-element.18.refs_0_.own, f32[2,128,256]{2,1,0:T(8,128)S(1)} %collective-permute-done.9.refs_1_.other, bf16[2,128,256]{2,1,0:T(8,128)(2,1)S(1)} %fusion.2.refs_2_), custom_call_target="tpu_custom_call" | custom-call | flops 80000000 | bytes 1200000 | tf_op jit(solution)/shard_map/pallas_call | solution.py:206
  62.5 3.3 %collective-permute-start.10 = (f32[1,128,256]{2,1,0:T(8,128)S(1)}, f32[1,128,256]{2,1,0:T(8,128)S(1)}, u32[]{:S(2)}, u32[]{:S(2)}) collective-permute-start(f32[1,128,256]{2,1,0:T(8,128)S(1)} %get-tuple-element.20.refs_0_), channel_id=1, source_target_pairs={{0,8},{4,12},{8,0},{12,4},{16,24},{20,28},{24,16},{28,20},{32,40},... | collective-permute-start | bytes 393224 | tf_op jit(solution)/shard_map/ppermute | solution.py:247
  66.5 2.5 %collective-permute-done.10.refs_1_.other = f32[1,128,256]{2,1,0:T(8,128)S(1)} collective-permute-done((f32[1,128,256]{2,1,0:T(8,128)S(1)}, f32[1,128,256]{2,1,0:T(8,128)S(1)}, u32[]{:S(2)}, u32[]{:S(2)}) %collective-permute-start.10) | collective-permute-done | bytes 131104 | tf_op jit(solution)/shard_map/ppermute | solution.py:247
  69.1 3.5 %shard_map.105.refs_0_.refs_1_ = f32[1,128,256]{2,1,0:T(8,128)S(1)} custom-call(f32[1,128,256]{2,1,0:T(8,128)S(1)} %get-tuple-element.21.refs_1_.refs_0_.own, f32[1,128,256]{2,1,0:T(8,128)S(1)} %collective-permute-done.10.refs_1_.other, bf16[1,128,256]{2,1,0:T(8,128)(2,1)S(1)} %fusion.3.refs_2_), custom_call_target="tpu_custom_call" | custom-call | flops 40000000 | bytes 600000 | tf_op jit(solution)/shard_map/pallas_call | solution.py:206
  72.6 6.3 %collective-permute-start.11 = (f32[1,128,256]{2,1,0:T(8,128)S(1)}, f32[1,128,256]{2,1,0:T(8,128)S(1)}, u32[]{:S(2)}, u32[]{:S(2)}) collective-permute-start(f32[1,128,256]{2,1,0:T(8,128)S(1)} %shard_map.105.refs_0_.refs_1_), channel_id=1, source_target_pairs={{0,16},{4,20},{8,24},{12,28},{16,0},{20,4},{24,8},{28,12},{32,48},... | collective-permute-start | bytes 393224 | tf_op jit(solution)/shard_map/ppermute | solution.py:247
  79.0 1.6 %shard_map.104 = f32[1,2,256,128]{3,2,1,0:T(8,128)} custom-call(s32[4]{0:T(128)S(1)} %get-tuple-element.32.info, f32[2,128,256]{2,1,0:T(8,128)S(1)} %get-tuple-element.18.refs_0_.own, f32[2,128,256]{2,1,0:T(8,128)S(1)} %collective-permute-done.9.refs_1_.other, f32[1,128,256]{2,1,0:T(8,128)S(1)} %get-tuple-element.20.refs_0_, ...), custom_call_target="tpu_custom_call" | custom-call | flops 100000000 | bytes 1200000 | tf_op jit(solution)/shard_map/pallas_call | solution.py:228
  80.6 1.5 %shard_map.106 = f32[1,1,256,128]{3,2,1,0:T(8,128)} custom-call(s32[4]{0:T(128)S(1)} %get-tuple-element.31.info, f32[1,128,256]{2,1,0:T(8,128)S(1)} %get-tuple-element.21.refs_1_.refs_0_.own, f32[1,128,256]{2,1,0:T(8,128)S(1)} %collective-permute-done.10.refs_1_.other, f32[1,128,256]{2,1,0:T(8,128)S(1)} %shard_map.105.refs_0_.refs_1_), custom_call_target="tpu_custom_call" | custom-call | flops 50000000 | bytes 600000 | tf_op jit(solution)/shard_map/pallas_call | solution.py:228
  82.0 2.6 %collective-permute-done.11.refs_2_ = f32[1,128,256]{2,1,0:T(8,128)S(1)} collective-permute-done((f32[1,128,256]{2,1,0:T(8,128)S(1)}, f32[1,128,256]{2,1,0:T(8,128)S(1)}, u32[]{:S(2)}, u32[]{:S(2)}) %collective-permute-start.11) | collective-permute-done | bytes 131104 | tf_op jit(solution)/shard_map/ppermute | solution.py:247
  84.7 5.0 %shard_map.107 = (f32[1,128,256]{2,1,0:T(8,128)}, f32[1,1,256,128]{3,2,1,0:T(8,128)}) custom-call(s32[4]{0:T(128)S(1)} %get-tuple-element.24.refs_0_, f32[1,128,256]{2,1,0:T(8,128)S(1)} %shard_map.105.refs_0_.refs_1_, f32[1,128,256]{2,1,0:T(8,128)S(1)} %collective-permute-done.11.refs_2_, bf16[1,128,256]{2,1,0:T(8,128)(2,1)S(1)} %fusion.4.refs_3_), custom_call_target="tpu_custom_call" | custom-call | flops 40000000 | bytes 600000 | tf_op jit(solution)/shard_map/pallas_call | solution.py:206
  (36 shorter events, 5.8 us)
Async XLA Ops:
  2.3 19.5 %collective-permute-start.2 = (bf16[528,256]{1,0:T(8,128)(2,1)S(1)}, bf16[528,256]{1,0:T(8,128)(2,1)S(1)}, u32[]{:S(2)}, u32[]{:S(2)}) collective-permute-start(bf16[528,256]{1,0:T(8,128)(2,1)S(1)} %fusion.1), channel_id=1, source_target_pairs={{0,3},{1,0},{2,1},{3,2},{4,7},{5,4},{6,5},{7,6},{8,11},{9,8},{10,9... | collective-permute-start | bytes 811016 | tf_op jit(solution)/shard_map/ppermute | solution.py:242
  7.5 14.3 %collective-permute-start.1 = (bf16[528,256]{1,0:T(8,128)(2,1)S(1)}, bf16[528,256]{1,0:T(8,128)(2,1)S(1)}, u32[]{:S(2)}, u32[]{:S(2)}) collective-permute-start(bf16[528,256]{1,0:T(8,128)(2,1)S(1)} %fusion.1), channel_id=1, source_target_pairs={{0,2},{1,3},{2,0},{3,1},{4,6},{5,7},{6,4},{7,5},{8,10},{9,11},{10,... | collective-permute-start | bytes 811016 | tf_op jit(solution)/shard_map/ppermute | solution.py:242
  10.0 12.2 %collective-permute-start = (bf16[528,256]{1,0:T(8,128)(2,1)S(1)}, bf16[528,256]{1,0:T(8,128)(2,1)S(1)}, u32[]{:S(2)}, u32[]{:S(2)}) collective-permute-start(bf16[528,256]{1,0:T(8,128)(2,1)S(1)} %fusion.1), channel_id=1, source_target_pairs={{0,1},{1,2},{2,3},{3,0},{4,5},{5,6},{6,7},{7,4},{8,9},{9,10},{10,1... | collective-permute-start | bytes 811016 | tf_op jit(solution)/shard_map/ppermute | solution.py:242
  12.5 10.8 %copy-start.2 = (bf16[512,256]{1,0:T(8,128)(2,1)S(1)}, bf16[512,256]{1,0:T(8,128)(2,1)}, u32[]{:S(2)}) copy-start(bf16[512,256]{1,0:T(8,128)(2,1)} %param.7) | copy-start | bytes 786436
  15.2 35.6 %copy-start = (bf16[16,4,128,128]{3,2,1,0:T(8,128)(2,1)S(1)}, bf16[16,4,128,128]{3,2,1,0:T(8,128)(2,1)}, u32[]{:S(2)}) copy-start(bf16[16,4,128,128]{3,2,1,0:T(8,128)(2,1)} %own_tiles.1) | copy-start | bytes 6291460
  15.2 35.6 %copy-start.1 = (s32[16]{0:T(128)S(1)}, s32[16]{0:T(128)}, u32[]{:S(2)}) copy-start(s32[16]{0:T(128)} %counts.1) | copy-start | bytes 196
  15.2 22.1 %collective-permute-start.3 = (bf16[4,4,128,128]{3,2,1,0:T(8,128)(2,1)}, bf16[4,4,128,128]{3,2,1,0:T(8,128)(2,1)}, u32[]{:S(2)}, u32[]{:S(2)}) collective-permute-start(bf16[4,4,128,128]{3,2,1,0:T(8,128)(2,1)} %get-tuple-element.28), channel_id=1, source_target_pairs={{0,1},{1,2},{2,3},{3,0},{4,5},{5,6},{6,7},{7,4},{8,9},{9,10},{10,1... | collective-permute-start | bytes 1572872 | tf_op jit(solution)/shard_map/ppermute | solution.py:242
  18.7 18.6 %collective-permute-start.4 = (bf16[4,4,128,128]{3,2,1,0:T(8,128)(2,1)}, bf16[4,4,128,128]{3,2,1,0:T(8,128)(2,1)}, u32[]{:S(2)}, u32[]{:S(2)}) collective-permute-start(bf16[4,4,128,128]{3,2,1,0:T(8,128)(2,1)} %get-tuple-element.27), channel_id=1, source_target_pairs={{0,3},{1,0},{2,1},{3,2},{4,7},{5,4},{6,5},{7,6},{8,11},{9,8},{10,9... | collective-permute-start | bytes 1572872 | tf_op jit(solution)/shard_map/ppermute | solution.py:242
  21.8 0.7 copy-start.3
  22.5 0.7 copy-start.4
  23.4 27.4 %collective-permute-start.7 = (bf16[2048,256]{1,0:T(8,128)(2,1)S(1)}, bf16[2048,256]{1,0:T(8,128)(2,1)}, u32[]{:S(2)}, u32[]{:S(2)}) collective-permute-start(bf16[2048,256]{1,0:T(8,128)(2,1)S(1)} %pad_maximum_fusion.own), channel_id=1, source_target_pairs={{0,4},{4,8},{8,12},{12,16},{16,20},{20,24},{24,28},{28,32},{32,36}... | collective-permute-start | bytes 3145736 | tf_op jit(solution)/shard_map/ppermute | solution.py:283
  30.4 20.3 %collective-permute-start.8 = (bf16[2048,256]{1,0:T(8,128)(2,1)S(1)}, bf16[2048,256]{1,0:T(8,128)(2,1)}, u32[]{:S(2)}, u32[]{:S(2)}) collective-permute-start(bf16[2048,256]{1,0:T(8,128)(2,1)S(1)} %pad_maximum_fusion.own), channel_id=1, source_target_pairs={{4,0},{8,4},{12,8},{16,12},{20,16},{24,20},{28,24},{32,28},{36,32}... | collective-permute-start | bytes 3145736 | tf_op jit(solution)/shard_map/ppermute | solution.py:284
  33.5 17.2 %collective-permute-start.5 = (bf16[4,4,128,128]{3,2,1,0:T(8,128)(2,1)}, bf16[4,4,128,128]{3,2,1,0:T(8,128)(2,1)S(1)}, u32[]{:S(2)}, u32[]{:S(2)}) collective-permute-start(bf16[4,4,128,128]{3,2,1,0:T(8,128)(2,1)} %get-tuple-element.15), channel_id=1, source_target_pairs={{0,2},{1,3},{2,0},{3,1},{4,6},{5,7},{6,4},{7,5},{8,10},{9,11},{10,... | collective-permute-start | bytes 1572872 | tf_op jit(solution)/shard_map/ppermute | solution.py:242
  37.3 13.5 %collective-permute-start.6 = (bf16[4,4,128,128]{3,2,1,0:T(8,128)(2,1)}, bf16[4,4,128,128]{3,2,1,0:T(8,128)(2,1)S(1)}, u32[]{:S(2)}, u32[]{:S(2)}) collective-permute-start(bf16[4,4,128,128]{3,2,1,0:T(8,128)(2,1)} %collective-permute-done.3.tiles_a), channel_id=1, source_target_pairs={{0,4},{4,0},{8,12},{12,8},{16,20},{20,16},{24,28},{28,24},{32,36},... | collective-permute-start | bytes 1572872 | tf_op jit(solution)/shard_map/ppermute | solution.py:247
  54.2 3.5 %collective-permute-start.9 = (f32[2,128,256]{2,1,0:T(8,128)S(1)}, f32[2,128,256]{2,1,0:T(8,128)S(1)}, u32[]{:S(2)}, u32[]{:S(2)}) collective-permute-start(f32[2,128,256]{2,1,0:T(8,128)S(1)} %get-tuple-element.19), channel_id=1, source_target_pairs={{0,4},{4,0},{8,12},{12,8},{16,20},{20,16},{24,28},{28,24},{32,36},... | collective-permute-start | bytes 786440 | tf_op jit(solution)/shard_map/ppermute | solution.py:247
  62.5 6.6 %collective-permute-start.10 = (f32[1,128,256]{2,1,0:T(8,128)S(1)}, f32[1,128,256]{2,1,0:T(8,128)S(1)}, u32[]{:S(2)}, u32[]{:S(2)}) collective-permute-start(f32[1,128,256]{2,1,0:T(8,128)S(1)} %get-tuple-element.20.refs_0_), channel_id=1, source_target_pairs={{0,8},{4,12},{8,0},{12,4},{16,24},{20,28},{24,16},{28,20},{32,40},... | collective-permute-start | bytes 393224 | tf_op jit(solution)/shard_map/ppermute | solution.py:247
  72.6 12.1 %collective-permute-start.11 = (f32[1,128,256]{2,1,0:T(8,128)S(1)}, f32[1,128,256]{2,1,0:T(8,128)S(1)}, u32[]{:S(2)}, u32[]{:S(2)}) collective-permute-start(f32[1,128,256]{2,1,0:T(8,128)S(1)} %shard_map.105.refs_0_.refs_1_), channel_id=1, source_target_pairs={{0,16},{4,20},{8,24},{12,28},{16,0},{20,4},{24,8},{28,12},{32,48},... | collective-permute-start | bytes 393224 | tf_op jit(solution)/shard_map/ppermute | solution.py:247

commit v7 on v6

--- a/solution.py
+++ b/solution.py
@@ -270,9 +270,9 @@
     one, two, three = (
         lax.dynamic_slice_in_dim(near_tiles, (x + by) % 4 * 4, 4, axis=0) for by in (1, 2, 3)
     )
+    tiles_three = shifted(three, "cols", 3)
     tiles_one = shifted(one, "cols", 1)
-    tiles_three = shifted(three, "cols", 3)
-    tiles_one, tiles_three = lax.optimization_barrier((tiles_one, tiles_three))
+    tiles_three, tiles_one = lax.optimization_barrier((tiles_three, tiles_one))
     tie = swapped(tiles_one, 1)
     own = jnp.concatenate([samples] + [part[:512] for part in (by_one, by_two, by_three)], axis=0)
     cols = jnp.concatenate([part[512:516, :16] for part in (block, by_one, by_two, by_three)]).astype(jnp.int32)

time: 90.3 us -> 90.2 us (level)
    ppermute x4, starting transfers between devices: 13.8 us -> 14.9 us  [swapped(): return lax.ppermute(value, 'leaf', [(i, i ^ apart) for i in range(count)])]
    ppermute x1, starting transfers between devices: 2.99 us -> 1.92 us  [local(): after = lax.ppermute(own, 'leaf', [(j, i) for i, j in rising])]
where the time goes in v7:
time: 90.2 us; the launch traced here: 89.5 us
  starting transfers between devices  45 us (50%)
  Pallas kernels  19.8 us (22%)
  waiting for transfers between devices  14.7 us (16%)
  local copies, waits for them, and re-layouts  5.5 us (6%)
  other arithmetic  3.58 us (4%)
  between operations  0.97 us (1%)
    ppermute x6, starting transfers between devices, shifted(): lax.ppermute(value, axis, [(i, (i + by) % count) for i in range(count)])  21.1 us
    ppermute x4, starting transfers between devices, swapped(): return lax.ppermute(value, 'leaf', [(i, i ^ apart) for i in range(count)])  14.9 us
    pallas_call x3, Pallas kernels, merge(): pl.pallas_call(functools.partial(merge_kernel, nodes, last), out_shape=tu...  13.3 us
    ppermute x6, waiting for transfers between devices, shifted(): lax.ppermute(value, axis, [(i, (i + by) % count) for i in range(count)])  9.02 us
    ppermute x1, starting transfers between devices, local(): before = lax.ppermute(own, 'leaf', rising)  7.07 us
    ppermute x4, waiting for transfers between devices, swapped(): return lax.ppermute(value, 'leaf', [(i, i ^ apart) for i in range(count)])  5.7 us
    pallas_call x1, Pallas kernels, near(): pl.pallas_call(near_kernel, out_shape=(block, block), in_specs=[SMEM] * 3...  3.43 us
    pallas_call x2, Pallas kernels, transfer(): pl.pallas_call(functools.partial(transfer_kernel, nodes), out_shape=jax.S...  3.09 us
  transfers between devices with their start and end apart: 12, of which 5 were waited for; matrix products, arithmetic and copies ran while one was open for 7% of the time, Pallas kernels for 3%

profile of v7, /device:TPU:1, one launch (start us, length us, event | category | flops | bytes accessed | tf_op | source)
XLA Modules:
  0.0 89.5 jit_solution(5058160130337743146)
XLA Ops:
  1.3 1.0 %fusion.1 = bf16[528,256]{1,0:T(8,128)(2,1)S(1)} fusion(bf16[4,16]{1,0:T(4,128)(2,1)S(1)} %fusion.6, bf16[512,256]{1,0:T(8,128)(2,1)} %param.7), kind=kLoop, calls=%fused_computation.3 | loop fusion | flops 811008 | bytes 532608 | tf_op jit(solution)/shard_map/concatenate | solution.py:268
  2.3 5.2 %collective-permute-start.2 = (bf16[528,256]{1,0:T(8,128)(2,1)S(1)}, bf16[528,256]{1,0:T(8,128)(2,1)S(1)}, u32[]{:S(2)}, u32[]{:S(2)}) collective-permute-start(bf16[528,256]{1,0:T(8,128)(2,1)S(1)} %fusion.1), channel_id=1, source_target_pairs={{0,3},{1,0},{2,1},{3,2},{4,7},{5,4},{6,5},{7,6},{8,11},{9,8},{10,9... | collective-permute-start | bytes 811016 | tf_op jit(solution)/shard_map/ppermute | solution.py:242
  7.5 2.4 %collective-permute-start.1 = (bf16[528,256]{1,0:T(8,128)(2,1)S(1)}, bf16[528,256]{1,0:T(8,128)(2,1)S(1)}, u32[]{:S(2)}, u32[]{:S(2)}) collective-permute-start(bf16[528,256]{1,0:T(8,128)(2,1)S(1)} %fusion.1), channel_id=1, source_target_pairs={{0,2},{1,3},{2,0},{3,1},{4,6},{5,7},{6,4},{7,5},{8,10},{9,11},{10,... | collective-permute-start | bytes 811016 | tf_op jit(solution)/shard_map/ppermute | solution.py:242
  10.0 2.5 %collective-permute-start = (bf16[528,256]{1,0:T(8,128)(2,1)S(1)}, bf16[528,256]{1,0:T(8,128)(2,1)S(1)}, u32[]{:S(2)}, u32[]{:S(2)}) collective-permute-start(bf16[528,256]{1,0:T(8,128)(2,1)S(1)} %fusion.1), channel_id=1, source_target_pairs={{0,1},{1,2},{2,3},{3,0},{4,5},{5,6},{6,7},{7,4},{8,9},{9,10},{10,1... | collective-permute-start | bytes 811016 | tf_op jit(solution)/shard_map/ppermute | solution.py:242
  12.5 2.6 %constant_dynamic-slice_fusion.4 = (bf16[4,4,128,128]{3,2,1,0:T(8,128)(2,1)}, bf16[4,4,128,128]{3,2,1,0:T(8,128)(2,1)}, bf16[4,4,128,128]{3,2,1,0:T(8,128)(2,1)}) fusion(bf16[16,4,128,128]{3,2,1,0:T(8,128)(2,1)} %own_tiles.1, s32[]{:T(128)S(6)} %select_n.60, s32[]{:T(128)S(6)} %select_n.58, s32[]{:T(128)S(6)} %select_n.56), kind=kLoop, calls=%fused_computation.19 | loop fusion | bytes 3145740 | tf_op jit(solution)/shard_map/dynamic_slice | solution.py:271
  15.2 4.1 %collective-permute-start.3 = (bf16[4,4,128,128]{3,2,1,0:T(8,128)(2,1)}, bf16[4,4,128,128]{3,2,1,0:T(8,128)(2,1)}, u32[]{:S(2)}, u32[]{:S(2)}) collective-permute-start(bf16[4,4,128,128]{3,2,1,0:T(8,128)(2,1)} %get-tuple-element.28), channel_id=1, source_target_pairs={{0,3},{1,0},{2,1},{3,2},{4,7},{5,4},{6,5},{7,6},{8,11},{9,8},{10,9... | collective-permute-start | bytes 1572872 | tf_op jit(solution)/shard_map/ppermute | solution.py:242
  19.3 1.9 %collective-permute-start.4 = (bf16[4,4,128,128]{3,2,1,0:T(8,128)(2,1)}, bf16[4,4,128,128]{3,2,1,0:T(8,128)(2,1)}, u32[]{:S(2)}, u32[]{:S(2)}) collective-permute-start(bf16[4,4,128,128]{3,2,1,0:T(8,128)(2,1)} %get-tuple-element.27), channel_id=1, source_target_pairs={{0,1},{1,2},{2,3},{3,0},{4,5},{5,6},{6,7},{7,4},{8,9},{9,10},{10,1... | collective-permute-start | bytes 1572872 | tf_op jit(solution)/shard_map/ppermute | solution.py:242
  21.3 1.1 %collective-permute-done = bf16[528,256]{1,0:T(8,128)(2,1)S(1)} collective-permute-done((bf16[528,256]{1,0:T(8,128)(2,1)S(1)}, bf16[528,256]{1,0:T(8,128)(2,1)S(1)}, u32[]{:S(2)}, u32[]{:S(2)}) %collective-permute-start) | collective-permute-done | bytes 270368 | tf_op jit(solution)/shard_map/ppermute | solution.py:242
  23.3 7.1 %collective-permute-start.7 = (bf16[2048,256]{1,0:T(8,128)(2,1)S(1)}, bf16[2048,256]{1,0:T(8,128)(2,1)}, u32[]{:S(2)}, u32[]{:S(2)}) collective-permute-start(bf16[2048,256]{1,0:T(8,128)(2,1)S(1)} %pad_maximum_fusion.own), channel_id=1, source_target_pairs={{0,4},{4,8},{8,12},{12,16},{16,20},{20,24},{24,28},{28,32},{32,36}... | collective-permute-start | bytes 3145736 | tf_op jit(solution)/shard_map/ppermute | solution.py:283
  30.3 1.9 %collective-permute-start.8 = (bf16[2048,256]{1,0:T(8,128)(2,1)S(1)}, bf16[2048,256]{1,0:T(8,128)(2,1)}, u32[]{:S(2)}, u32[]{:S(2)}) collective-permute-start(bf16[2048,256]{1,0:T(8,128)(2,1)S(1)} %pad_maximum_fusion.own), channel_id=1, source_target_pairs={{4,0},{8,4},{12,8},{16,12},{20,16},{24,20},{28,24},{32,28},{36,32}... | collective-permute-start | bytes 3145736 | tf_op jit(solution)/shard_map/ppermute | solution.py:284
  32.4 4.9 %collective-permute-start.5 = (bf16[4,4,128,128]{3,2,1,0:T(8,128)(2,1)}, bf16[4,4,128,128]{3,2,1,0:T(8,128)(2,1)S(1)}, u32[]{:S(2)}, u32[]{:S(2)}) collective-permute-start(bf16[4,4,128,128]{3,2,1,0:T(8,128)(2,1)} %get-tuple-element.15), channel_id=1, source_target_pairs={{0,2},{1,3},{2,0},{3,1},{4,6},{5,7},{6,4},{7,5},{8,10},{9,11},{10,... | collective-permute-start | bytes 1572872 | tf_op jit(solution)/shard_map/ppermute | solution.py:242
  37.3 1.9 %collective-permute-start.6 = (bf16[4,4,128,128]{3,2,1,0:T(8,128)(2,1)}, bf16[4,4,128,128]{3,2,1,0:T(8,128)(2,1)S(1)}, u32[]{:S(2)}, u32[]{:S(2)}) collective-permute-start(bf16[4,4,128,128]{3,2,1,0:T(8,128)(2,1)} %collective-permute-done.4.tiles_a), channel_id=1, source_target_pairs={{0,4},{4,0},{8,12},{12,8},{16,20},{20,16},{24,28},{28,24},{32,36},... | collective-permute-start | bytes 1572872 | tf_op jit(solution)/shard_map/ppermute | solution.py:247
  41.4 7.9 %collective-permute-done.5.tiles_b = bf16[4,4,128,128]{3,2,1,0:T(8,128)(2,1)S(1)} collective-permute-done((bf16[4,4,128,128]{3,2,1,0:T(8,128)(2,1)}, bf16[4,4,128,128]{3,2,1,0:T(8,128)(2,1)S(1)}, u32[]{:S(2)}, u32[]{:S(2)}) %collective-permute-start.5) | collective-permute-done | bytes 524320 | tf_op jit(solution)/shard_map/ppermute | solution.py:242
  49.3 3.4 %shard_map.102 = (f32[2,128,256]{2,1,0:T(8,128)S(1)}, f32[2,128,256]{2,1,0:T(8,128)S(1)}) custom-call(s32[4]{0:T(128)S(1)} %get-tuple-element.32.info, s32[16,16]{1,0:T(8,128)S(1)} %maximum_convert_fusion.cols, s32[16]{0:T(128)S(1)} %copy-done.1, bf16[16,4,128,128]{3,2,1,0:T(8,128)(2,1)S(1)} %copy-done, ...), custom_call_target="tpu_custom_call" | custom-call | flops 540000000 | bytes 6000000 | tf_op jit(solution)/shard_map/pallas_call | solution.py:94
  52.7 2.3 %collective-permute-start.9 = (f32[2,128,256]{2,1,0:T(8,128)S(1)}, f32[2,128,256]{2,1,0:T(8,128)S(1)}, u32[]{:S(2)}, u32[]{:S(2)}) collective-permute-start(f32[2,128,256]{2,1,0:T(8,128)S(1)} %get-tuple-element.19), channel_id=1, source_target_pairs={{0,4},{4,0},{8,12},{12,8},{16,20},{20,16},{24,28},{28,24},{32,36},... | collective-permute-start | bytes 786440 | tf_op jit(solution)/shard_map/ppermute | solution.py:247
  56.2 4.8 %shard_map.103 = (f32[1,128,256]{2,1,0:T(8,128)S(1)}, f32[1,128,256]{2,1,0:T(8,128)S(1)}) custom-call(f32[2,128,256]{2,1,0:T(8,128)S(1)} %get-tuple-element.18.refs_0_.own, f32[2,128,256]{2,1,0:T(8,128)S(1)} %collective-permute-done.9.refs_1_.other, bf16[2,128,256]{2,1,0:T(8,128)(2,1)S(1)} %fusion.2.refs_2_), custom_call_target="tpu_custom_call" | custom-call | flops 80000000 | bytes 1200000 | tf_op jit(solution)/shard_map/pallas_call | solution.py:206
  61.0 4.7 %collective-permute-start.10 = (f32[1,128,256]{2,1,0:T(8,128)S(1)}, f32[1,128,256]{2,1,0:T(8,128)S(1)}, u32[]{:S(2)}, u32[]{:S(2)}) collective-permute-start(f32[1,128,256]{2,1,0:T(8,128)S(1)} %get-tuple-element.20.refs_0_), channel_id=1, source_target_pairs={{0,8},{4,12},{8,0},{12,4},{16,24},{20,28},{24,16},{28,20},{32,40},... | collective-permute-start | bytes 393224 | tf_op jit(solution)/shard_map/ppermute | solution.py:247
  66.5 2.7 %collective-permute-done.10.refs_1_.other = f32[1,128,256]{2,1,0:T(8,128)S(1)} collective-permute-done((f32[1,128,256]{2,1,0:T(8,128)S(1)}, f32[1,128,256]{2,1,0:T(8,128)S(1)}, u32[]{:S(2)}, u32[]{:S(2)}) %collective-permute-start.10) | collective-permute-done | bytes 131104 | tf_op jit(solution)/shard_map/ppermute | solution.py:247
  69.2 3.5 %shard_map.105.refs_0_.refs_1_ = f32[1,128,256]{2,1,0:T(8,128)S(1)} custom-call(f32[1,128,256]{2,1,0:T(8,128)S(1)} %get-tuple-element.21.refs_1_.refs_0_.own, f32[1,128,256]{2,1,0:T(8,128)S(1)} %collective-permute-done.10.refs_1_.other, bf16[1,128,256]{2,1,0:T(8,128)(2,1)S(1)} %fusion.3.refs_2_), custom_call_target="tpu_custom_call" | custom-call | flops 40000000 | bytes 600000 | tf_op jit(solution)/shard_map/pallas_call | solution.py:206
  72.7 6.1 %collective-permute-start.11 = (f32[1,128,256]{2,1,0:T(8,128)S(1)}, f32[1,128,256]{2,1,0:T(8,128)S(1)}, u32[]{:S(2)}, u32[]{:S(2)}) collective-permute-start(f32[1,128,256]{2,1,0:T(8,128)S(1)} %shard_map.105.refs_0_.refs_1_), channel_id=1, source_target_pairs={{0,16},{4,20},{8,24},{12,28},{16,0},{20,4},{24,8},{28,12},{32,48},... | collective-permute-start | bytes 393224 | tf_op jit(solution)/shard_map/ppermute | solution.py:247
  78.9 1.6 %shard_map.104 = f32[1,2,256,128]{3,2,1,0:T(8,128)} custom-call(s32[4]{0:T(128)S(1)} %get-tuple-element.32.info, f32[2,128,256]{2,1,0:T(8,128)S(1)} %get-tuple-element.18.refs_0_.own, f32[2,128,256]{2,1,0:T(8,128)S(1)} %collective-permute-done.9.refs_1_.other, f32[1,128,256]{2,1,0:T(8,128)S(1)} %get-tuple-element.20.refs_0_, ...), custom_call_target="tpu_custom_call" | custom-call | flops 100000000 | bytes 1200000 | tf_op jit(solution)/shard_map/pallas_call | solution.py:228
  80.5 1.5 %shard_map.106 = f32[1,1,256,128]{3,2,1,0:T(8,128)} custom-call(s32[4]{0:T(128)S(1)} %get-tuple-element.31.info, f32[1,128,256]{2,1,0:T(8,128)S(1)} %get-tuple-element.21.refs_1_.refs_0_.own, f32[1,128,256]{2,1,0:T(8,128)S(1)} %collective-permute-done.10.refs_1_.other, f32[1,128,256]{2,1,0:T(8,128)S(1)} %shard_map.105.refs_0_.refs_1_), custom_call_target="tpu_custom_call" | custom-call | flops 50000000 | bytes 600000 | tf_op jit(solution)/shard_map/pallas_call | solution.py:228
  82.0 2.6 %collective-permute-done.11.refs_2_ = f32[1,128,256]{2,1,0:T(8,128)S(1)} collective-permute-done((f32[1,128,256]{2,1,0:T(8,128)S(1)}, f32[1,128,256]{2,1,0:T(8,128)S(1)}, u32[]{:S(2)}, u32[]{:S(2)}) %collective-permute-start.11) | collective-permute-done | bytes 131104 | tf_op jit(solution)/shard_map/ppermute | solution.py:247
  84.6 5.0 %shard_map.107 = (f32[1,128,256]{2,1,0:T(8,128)}, f32[1,1,256,128]{3,2,1,0:T(8,128)}) custom-call(s32[4]{0:T(128)S(1)} %get-tuple-element.24.refs_0_, f32[1,128,256]{2,1,0:T(8,128)S(1)} %shard_map.105.refs_0_.refs_1_, f32[1,128,256]{2,1,0:T(8,128)S(1)} %collective-permute-done.11.refs_2_, bf16[1,128,256]{2,1,0:T(8,128)(2,1)S(1)} %fusion.4.refs_3_), custom_call_target="tpu_custom_call" | custom-call | flops 40000000 | bytes 600000 | tf_op jit(solution)/shard_map/pallas_call | solution.py:206
  (36 shorter events, 5.8 us)
Async XLA Ops:
  2.3 18.9 %collective-permute-start.2 = (bf16[528,256]{1,0:T(8,128)(2,1)S(1)}, bf16[528,256]{1,0:T(8,128)(2,1)S(1)}, u32[]{:S(2)}, u32[]{:S(2)}) collective-permute-start(bf16[528,256]{1,0:T(8,128)(2,1)S(1)} %fusion.1), channel_id=1, source_target_pairs={{0,3},{1,0},{2,1},{3,2},{4,7},{5,4},{6,5},{7,6},{8,11},{9,8},{10,9... | collective-permute-start | bytes 811016 | tf_op jit(solution)/shard_map/ppermute | solution.py:242
  7.5 13.7 %collective-permute-start.1 = (bf16[528,256]{1,0:T(8,128)(2,1)S(1)}, bf16[528,256]{1,0:T(8,128)(2,1)S(1)}, u32[]{:S(2)}, u32[]{:S(2)}) collective-permute-start(bf16[528,256]{1,0:T(8,128)(2,1)S(1)} %fusion.1), channel_id=1, source_target_pairs={{0,2},{1,3},{2,0},{3,1},{4,6},{5,7},{6,4},{7,5},{8,10},{9,11},{10,... | collective-permute-start | bytes 811016 | tf_op jit(solution)/shard_map/ppermute | solution.py:242
  10.0 12.5 %collective-permute-start = (bf16[528,256]{1,0:T(8,128)(2,1)S(1)}, bf16[528,256]{1,0:T(8,128)(2,1)S(1)}, u32[]{:S(2)}, u32[]{:S(2)}) collective-permute-start(bf16[528,256]{1,0:T(8,128)(2,1)S(1)} %fusion.1), channel_id=1, source_target_pairs={{0,1},{1,2},{2,3},{3,0},{4,5},{5,6},{6,7},{7,4},{8,9},{9,10},{10,1... | collective-permute-start | bytes 811016 | tf_op jit(solution)/shard_map/ppermute | solution.py:242
  12.5 10.7 %copy-start.2 = (bf16[512,256]{1,0:T(8,128)(2,1)S(1)}, bf16[512,256]{1,0:T(8,128)(2,1)}, u32[]{:S(2)}) copy-start(bf16[512,256]{1,0:T(8,128)(2,1)} %param.7) | copy-start | bytes 786436
  15.2 34.1 %copy-start = (bf16[16,4,128,128]{3,2,1,0:T(8,128)(2,1)S(1)}, bf16[16,4,128,128]{3,2,1,0:T(8,128)(2,1)}, u32[]{:S(2)}) copy-start(bf16[16,4,128,128]{3,2,1,0:T(8,128)(2,1)} %own_tiles.1) | copy-start | bytes 6291460
  15.2 34.1 %copy-start.1 = (s32[16]{0:T(128)S(1)}, s32[16]{0:T(128)}, u32[]{:S(2)}) copy-start(s32[16]{0:T(128)} %counts.1) | copy-start | bytes 196
  15.2 22.1 %collective-permute-start.3 = (bf16[4,4,128,128]{3,2,1,0:T(8,128)(2,1)}, bf16[4,4,128,128]{3,2,1,0:T(8,128)(2,1)}, u32[]{:S(2)}, u32[]{:S(2)}) collective-permute-start(bf16[4,4,128,128]{3,2,1,0:T(8,128)(2,1)} %get-tuple-element.28), channel_id=1, source_target_pairs={{0,3},{1,0},{2,1},{3,2},{4,7},{5,4},{6,5},{7,6},{8,11},{9,8},{10,9... | collective-permute-start | bytes 1572872 | tf_op jit(solution)/shard_map/ppermute | solution.py:242
  19.3 18.0 %collective-permute-start.4 = (bf16[4,4,128,128]{3,2,1,0:T(8,128)(2,1)}, bf16[4,4,128,128]{3,2,1,0:T(8,128)(2,1)}, u32[]{:S(2)}, u32[]{:S(2)}) collective-permute-start(bf16[4,4,128,128]{3,2,1,0:T(8,128)(2,1)} %get-tuple-element.27), channel_id=1, source_target_pairs={{0,1},{1,2},{2,3},{3,0},{4,5},{5,6},{6,7},{7,4},{8,9},{9,10},{10,1... | collective-permute-start | bytes 1572872 | tf_op jit(solution)/shard_map/ppermute | solution.py:242
  21.2 1.2 %copy-start.3 = (bf16[528,256]{1,0:T(8,128)(2,1)}, bf16[528,256]{1,0:T(8,128)(2,1)S(1)}, u32[]{:S(2)}) copy-start(bf16[528,256]{1,0:T(8,128)(2,1)S(1)} %collective-permute-done.1) | copy-start | bytes 811012
  22.4 0.7 copy-start.4
  23.3 26.0 %collective-permute-start.7 = (bf16[2048,256]{1,0:T(8,128)(2,1)S(1)}, bf16[2048,256]{1,0:T(8,128)(2,1)}, u32[]{:S(2)}, u32[]{:S(2)}) collective-permute-start(bf16[2048,256]{1,0:T(8,128)(2,1)S(1)} %pad_maximum_fusion.own), channel_id=1, source_target_pairs={{0,4},{4,8},{8,12},{12,16},{16,20},{20,24},{24,28},{28,32},{32,36}... | collective-permute-start | bytes 3145736 | tf_op jit(solution)/shard_map/ppermute | solution.py:283
  30.3 18.9 %collective-permute-start.8 = (bf16[2048,256]{1,0:T(8,128)(2,1)S(1)}, bf16[2048,256]{1,0:T(8,128)(2,1)}, u32[]{:S(2)}, u32[]{:S(2)}) collective-permute-start(bf16[2048,256]{1,0:T(8,128)(2,1)S(1)} %pad_maximum_fusion.own), channel_id=1, source_target_pairs={{4,0},{8,4},{12,8},{16,12},{20,16},{24,20},{28,24},{32,28},{36,32}... | collective-permute-start | bytes 3145736 | tf_op jit(solution)/shard_map/ppermute | solution.py:284
  32.4 16.9 %collective-permute-start.5 = (bf16[4,4,128,128]{3,2,1,0:T(8,128)(2,1)}, bf16[4,4,128,128]{3,2,1,0:T(8,128)(2,1)S(1)}, u32[]{:S(2)}, u32[]{:S(2)}) collective-permute-start(bf16[4,4,128,128]{3,2,1,0:T(8,128)(2,1)} %get-tuple-element.15), channel_id=1, source_target_pairs={{0,2},{1,3},{2,0},{3,1},{4,6},{5,7},{6,4},{7,5},{8,10},{9,11},{10,... | collective-permute-start | bytes 1572872 | tf_op jit(solution)/shard_map/ppermute | solution.py:242
  37.3 12.0 %collective-permute-start.6 = (bf16[4,4,128,128]{3,2,1,0:T(8,128)(2,1)}, bf16[4,4,128,128]{3,2,1,0:T(8,128)(2,1)S(1)}, u32[]{:S(2)}, u32[]{:S(2)}) collective-permute-start(bf16[4,4,128,128]{3,2,1,0:T(8,128)(2,1)} %collective-permute-done.4.tiles_a), channel_id=1, source_target_pairs={{0,4},{4,0},{8,12},{12,8},{16,20},{20,16},{24,28},{28,24},{32,36},... | collective-permute-start | bytes 1572872 | tf_op jit(solution)/shard_map/ppermute | solution.py:247
  52.7 3.4 %collective-permute-start.9 = (f32[2,128,256]{2,1,0:T(8,128)S(1)}, f32[2,128,256]{2,1,0:T(8,128)S(1)}, u32[]{:S(2)}, u32[]{:S(2)}) collective-permute-start(f32[2,128,256]{2,1,0:T(8,128)S(1)} %get-tuple-element.19), channel_id=1, source_target_pairs={{0,4},{4,0},{8,12},{12,8},{16,20},{20,16},{24,28},{28,24},{32,36},... | collective-permute-start | bytes 786440 | tf_op jit(solution)/shard_map/ppermute | solution.py:247
  61.0 8.2 %collective-permute-start.10 = (f32[1,128,256]{2,1,0:T(8,128)S(1)}, f32[1,128,256]{2,1,0:T(8,128)S(1)}, u32[]{:S(2)}, u32[]{:S(2)}) collective-permute-start(f32[1,128,256]{2,1,0:T(8,128)S(1)} %get-tuple-element.20.refs_0_), channel_id=1, source_target_pairs={{0,8},{4,12},{8,0},{12,4},{16,24},{20,28},{24,16},{28,20},{32,40},... | collective-permute-start | bytes 393224 | tf_op jit(solution)/shard_map/ppermute | solution.py:247
  72.7 11.8 %collective-permute-start.11 = (f32[1,128,256]{2,1,0:T(8,128)S(1)}, f32[1,128,256]{2,1,0:T(8,128)S(1)}, u32[]{:S(2)}, u32[]{:S(2)}) collective-permute-start(f32[1,128,256]{2,1,0:T(8,128)S(1)} %shard_map.105.refs_0_.refs_1_), channel_id=1, source_target_pairs={{0,16},{4,20},{8,24},{12,28},{16,0},{20,4},{24,8},{28,12},{32,48},... | collective-permute-start | bytes 393224 | tf_op jit(solution)/shard_map/ppermute | solution.py:247
